TPU v7x, 512 devices: a whole 4x8x8 slice. The times are simulated.
512 devices in a mesh: inner: 32 (over x_hi, y, core), outer: 16 (over z, x_lo).
Axes of the slice: x: 4 (x_hi: 2, x_lo: 2; x = x_hi * 2 + x_lo), y: 8, z: 8, core: 2. Of those that a mesh axis runs over, the one named last changes fastest.
Arguments:
- tokens: bfloat16 [65536, 8192], P(('inner', 'outer')), may hold values from -3600 to 3600
- cotangent: bfloat16 [65536, 256], P(('inner', 'outer')), may hold values from -10 to 10
- kv_weight: bfloat16 [8192, 256], P('inner'), may hold values from -0.0625 to 0.0625
- norm_gain: bfloat16 [8192], P('inner'), may hold values from 0.5 to 1.5
Outputs:
- kv_out: bfloat16 [65536, 256], P(('inner', 'outer'))
- token_grad: bfloat16 [65536, 8192], P(('inner', 'outer'))
- kv_grad: bfloat16 [8192, 256], P(('inner', 'outer'))
- gain_grad: bfloat16 [8192], P(('inner', 'outer'))
All inputs are finite; a program needn't handle non-finite values.
Results may differ from a plain program's by a relative error of at most 0.02.
Values may be sent and summed in bfloat16 or wider, within the bound.
No kernel may reach another device: no remote copies, remote signals or barrier semaphores. Data moves between devices by JAX's collectives and lax.ppermute only.
A program may use at most 64 MiB of HBM per device.

v0:
```python
import math

import jax
import jax.numpy as jnp
from jax import lax
from jax.sharding import PartitionSpec as P


def body(tokens, cotangent, kv_weight, norm_gain):
    inner_count = lax.axis_size("inner")
    outer_count = lax.axis_size("outer")
    tok_rows = tokens.shape[0]
    model_width = tokens.shape[1]
    kv_width = cotangent.shape[1]
    scale_factor = 1.0 / math.sqrt(tok_rows * inner_count * outer_count)
    wide_tokens = tokens.astype(jnp.float32)
    inv_rms = lax.rsqrt(jnp.mean(wide_tokens * wide_tokens, -1, keepdims=True) + 1e-05)
    unit_rows = wide_tokens * inv_rms
    weight_rows = lax.all_gather(kv_weight, "inner", axis=0, tiled=True)
    gain_piece = lax.all_gather(norm_gain, "inner", axis=0, tiled=True)
    gain_part = gain_piece.astype(jnp.float32)
    normed_part = (unit_rows * gain_part).astype(jnp.bfloat16)
    summed = jnp.dot(normed_part, weight_rows, preferred_element_type=jnp.float32)
    normed = (unit_rows * gain_part).astype(jnp.bfloat16)
    back_rows = lax.dot_general(
        cotangent,
        lax.all_gather(kv_weight, "inner", axis=0, tiled=True),
        (((1,), (1,)), ((), ())),
        preferred_element_type=jnp.float32,
    )
    kv_out = summed.astype(jnp.bfloat16)
    unit_grad = back_rows * gain_part
    slopes = jnp.mean(unit_grad * unit_rows, -1, keepdims=True)
    token_grad = (inv_rms * (unit_grad - unit_rows * slopes)).astype(jnp.bfloat16)
    gain_term = (jnp.sum(back_rows * unit_rows, 0) * scale_factor).astype(jnp.bfloat16)
    weight_term = (
        lax.dot_general(
            normed, cotangent, (((0,), (0,)), ((), ())), preferred_element_type=jnp.float32
        )
        * scale_factor
    ).astype(jnp.bfloat16)
    owner_rows = model_width // (inner_count * outer_count)
    moved_weight, moved_gain = (
        lax.all_to_all(
            lax.all_to_all(
                weight_term.reshape(inner_count, outer_count, owner_rows, kv_width),
                "inner",
                split_axis=0,
                concat_axis=0,
                tiled=True,
            ),
            "outer",
            split_axis=1,
            concat_axis=1,
            tiled=True,
        ),
        lax.all_to_all(
            lax.all_to_all(
                gain_term.reshape(inner_count, outer_count, owner_rows),
                "inner",
                split_axis=0,
                concat_axis=0,
                tiled=True,
            ),
            "outer",
            split_axis=1,
            concat_axis=1,
            tiled=True,
        ),
    )
    group_weight = jnp.sum(moved_weight, 0, dtype=jnp.float32).astype(jnp.bfloat16)
    group_gain = jnp.sum(moved_gain, 0, dtype=jnp.float32).astype(jnp.bfloat16)
    final_weight = jnp.sum(group_weight, 0, dtype=jnp.float32).astype(jnp.bfloat16)
    final_gain = jnp.sum(group_gain, 0, dtype=jnp.float32).astype(jnp.bfloat16)
    return (kv_out, token_grad, final_weight, final_gain)


def solution(mesh):
    return jax.shard_map(
        body,
        mesh=mesh,
        in_specs=(
            P(("inner", "outer"), None),
            P(("inner", "outer"), None),
            P("inner", None),
            P("inner"),
        ),
        out_specs=(
            P(("inner", "outer"), None),
            P(("inner", "outer"), None),
            P(("inner", "outer"), None),
            P(("inner", "outer")),
        ),
        check_vma=False,
    )
```

profile of v0, /device:TPU:1, one launch (start us, length us, event | category | flops | bytes accessed | tf_op | source)
XLA Modules:
  0.0 359.1 jit_solution(6792167371874632421)
XLA Ops:
  7.2 0.0 copy-start
  7.2 0.0 all-gather.3.cloned.1.call-start
  7.2 0.7 all-gather.3.cloned.1.call-update
  7.9 0.7 reshape.30
  8.6 43.6 %all-gather = bf16[32,1,256]{2,1,0:T(2,128)(2,1)S(1)} all-gather(bf16[1,1,256]{2,1,0:T(2,128)(2,1)S(1)} %reshape.30), channel_id=1, replica_groups=mesh['inner'=32,'outer'=16] {'inner'}, dimensions={0}, use_global_device_ids=true | all-gather | bytes 16896 | tf_op jit(solution)/shard_map/all_gather | solution.py:20
  52.2 2.1 fusion.11
  54.3 54.8 %all-gather.3.cloned.1.call-done = bf16[8192,256]{1,0:T(8,128)(2,1)} async-done(((bf16[256,256]{1,0:T(8,128)(2,1)}), bf16[8192,256]{1,0:T(8,128)(2,1)}) %all-gather.3.cloned.1.call-update) | async-done | bytes 4194320 | tf_op jit(solution)/shard_map/all_gather | solution.py:19
  109.1 0.0 copy-done
  109.1 6.5 %fusion.10 = (f32[8192]{0:T(1024)S(1)}, f32[128]{0:T(128)S(1)}, f32[128,8192]{1,0:T(8,128)}) fusion(bf16[128,8192]{1,0:T(8,128)(2,1)} %param.4, f32[128]{0:T(128)S(1)} %add_rsqrt_fusion, f32[8192]{0:T(1024)S(1)} %bitcast.10, bf16[128,256]{1,0:T(8,128)(2,1)S(1)} %copy-done, bf16[8192,256]{1,0:T(8,128)(2,1)} %all-gather.3.cloned.1.call-done), kind=kOutput, calls=%fused_computation.13 | convolution fusion | flops 544202624 | bytes 10617856 | tf_op jit(solution)/shard_map/dot_general | solution.py:25
  115.6 0.1 convert_element_type.41
  115.8 0.7 reshape.33
  116.5 5.0 %all-to-all-start.2 = ((bf16[32,2,128]{2,1,0:T(2,128)(2,1)}), bf16[32,2,128]{2,1,0:T(2,128)(2,1)S(1)}, u32[]{:S(2)}, u32[]{:S(2)}) async-start(bf16[32,2,128]{2,1,0:T(2,128)(2,1)} %reshape.33), calls=%async_computation.2 | async-start | bytes 32768 | tf_op jit(solution)/shard_map/all_to_all | solution.py:58
  121.6 0.0 copy-done.1
  121.6 3.4 fusion
  125.0 5.9 %all-to-all-done.2 = bf16[32,2,128]{2,1,0:T(2,128)(2,1)S(1)} async-done(((bf16[32,2,128]{2,1,0:T(2,128)(2,1)}), bf16[32,2,128]{2,1,0:T(2,128)(2,1)S(1)}, u32[]{:S(2)}, u32[]{:S(2)}) %all-to-all-start.2) | async-done | bytes 16416 | tf_op jit(solution)/shard_map/all_to_all | solution.py:58
  130.8 5.3 %all-to-all-start = ((bf16[32,16,16,256]{3,2,1,0:T(8,128)(2,1)}), bf16[32,16,16,256]{3,2,1,0:T(8,128)(2,1)}, u32[]{:S(2)}, u32[]{:S(2)}) async-start(bf16[32,16,16,256]{3,2,1,0:T(8,128)(2,1)} %bitcast.9), calls=%async_computation | async-start | bytes 8388608 | tf_op jit(solution)/shard_map/all_to_all | solution.py:45
  136.1 0.1 reshape.34
  136.2 0.2 copy.11
  136.4 0.7 reshape.35
  137.1 95.2 %all-to-all-done = bf16[32,16,16,256]{3,2,1,0:T(8,128)(2,1)} async-done(((bf16[32,16,16,256]{3,2,1,0:T(8,128)(2,1)}), bf16[32,16,16,256]{3,2,1,0:T(8,128)(2,1)}, u32[]{:S(2)}, u32[]{:S(2)}) %all-to-all-start) | async-done | bytes 4194336 | tf_op jit(solution)/shard_map/all_to_all | solution.py:45
  232.4 8.1 %all-to-all-start.3 = ((bf16[16,2,256]{2,1,0:T(2,128)(2,1)}), bf16[16,2,256]{2,1,0:T(2,128)(2,1)S(1)}, u32[]{:S(2)}, u32[]{:S(2)}) async-start(bf16[16,2,256]{2,1,0:T(2,128)(2,1)} %reshape.35), calls=%async_computation.3 | async-start | bytes 32768 | tf_op jit(solution)/shard_map/all_to_all | solution.py:57
  240.5 4.6 %copy.10 = bf16[32,16,16,256]{3,2,0,1:T(8,128)(2,1)} copy(bf16[32,16,16,256]{3,2,1,0:T(8,128)(2,1)} %all-to-all-done) | data formatting | bytes 8388608 | tf_op jit(solution)/shard_map/all_to_all | solution.py:45
  245.1 2.8 all-to-all-done.3
  247.9 4.8 %all-to-all-start.1 = ((bf16[32,16,16,256]{3,2,0,1:T(8,128)(2,1)}), bf16[32,16,16,256]{3,2,0,1:T(8,128)(2,1)}, u32[]{:S(2)}, u32[]{:S(2)}) async-start(bf16[32,16,16,256]{3,2,0,1:T(8,128)(2,1)} %copy.10), calls=%async_computation.1 | async-start | bytes 8388608 | tf_op jit(solution)/shard_map/all_to_all | solution.py:44
  252.7 0.0 copy-start.2
  252.7 3.7 %convolution_convert_fusion = bf16[128,256]{1,0:T(8,128)(2,1)} fusion(bf16[8192,256]{1,0:T(8,128)(2,1)} %all-gather.3.cloned.1.call-done, bf16[128,8192]{1,0:T(8,128)(2,1)S(1)} %copy-done.1, f32[8192]{0:T(1024)S(1)} %bitcast.12, f32[128]{0:T(128)S(1)} %add_rsqrt_fusion), kind=kOutput, calls=%fused_computation.15 | convolution fusion | flops 541097984 | bytes 6390272 | tf_op jit(solution)/shard_map/dot_general | solution.py:23
  256.5 0.0 copy-done.2
  256.5 2.3 fusion.9
  258.8 0.1 reshape.36
  258.9 0.6 bitcast_reduce_fusion
  259.6 89.3 %all-to-all-done.1 = bf16[32,16,16,256]{3,2,0,1:T(8,128)(2,1)} async-done(((bf16[32,16,16,256]{3,2,0,1:T(8,128)(2,1)}), bf16[32,16,16,256]{3,2,0,1:T(8,128)(2,1)}, u32[]{:S(2)}, u32[]{:S(2)}) %all-to-all-start.1) | async-done | bytes 4194336 | tf_op jit(solution)/shard_map/all_to_all | solution.py:44
  348.9 3.4 reduce_sum.67
  (5 shorter events, 0.1 us)
Async XLA Ops:
  7.2 101.9 %copy-start = (bf16[128,256]{1,0:T(8,128)(2,1)S(1)}, bf16[128,256]{1,0:T(8,128)(2,1)}, u32[]{:S(2)}) copy-start(bf16[128,256]{1,0:T(8,128)(2,1)} %param.5) | copy-start | bytes 196612
  7.2 101.9 %all-gather.3.cloned.1.call-start = ((), (), s32[]{:S(2)}) async-start(), calls=%async_computation.4 | async-start | bytes 4325376 | tf_op jit(solution)/shard_map/all_gather | solution.py:19
  109.1 12.5 %copy-start.1 = (bf16[128,8192]{1,0:T(8,128)(2,1)S(1)}, bf16[128,8192]{1,0:T(8,128)(2,1)}, u32[]{:S(2)}) copy-start(bf16[128,8192]{1,0:T(8,128)(2,1)} %param.4) | copy-start | bytes 6291460
  116.5 14.3 %all-to-all-start.2 = ((bf16[32,2,128]{2,1,0:T(2,128)(2,1)}), bf16[32,2,128]{2,1,0:T(2,128)(2,1)S(1)}, u32[]{:S(2)}, u32[]{:S(2)}) async-start(bf16[32,2,128]{2,1,0:T(2,128)(2,1)} %reshape.33), calls=%async_computation.2 | async-start | bytes 32768 | tf_op jit(solution)/shard_map/all_to_all | solution.py:58
  130.8 101.5 %all-to-all-start = ((bf16[32,16,16,256]{3,2,1,0:T(8,128)(2,1)}), bf16[32,16,16,256]{3,2,1,0:T(8,128)(2,1)}, u32[]{:S(2)}, u32[]{:S(2)}) async-start(bf16[32,16,16,256]{3,2,1,0:T(8,128)(2,1)} %bitcast.9), calls=%async_computation | async-start | bytes 8388608 | tf_op jit(solution)/shard_map/all_to_all | solution.py:45
  232.4 15.5 %all-to-all-start.3 = ((bf16[16,2,256]{2,1,0:T(2,128)(2,1)}), bf16[16,2,256]{2,1,0:T(2,128)(2,1)S(1)}, u32[]{:S(2)}, u32[]{:S(2)}) async-start(bf16[16,2,256]{2,1,0:T(2,128)(2,1)} %reshape.35), calls=%async_computation.3 | async-start | bytes 32768 | tf_op jit(solution)/shard_map/all_to_all | solution.py:57
  247.9 101.0 %all-to-all-start.1 = ((bf16[32,16,16,256]{3,2,0,1:T(8,128)(2,1)}), bf16[32,16,16,256]{3,2,0,1:T(8,128)(2,1)}, u32[]{:S(2)}, u32[]{:S(2)}) async-start(bf16[32,16,16,256]{3,2,0,1:T(8,128)(2,1)} %copy.10), calls=%async_computation.1 | async-start | bytes 8388608 | tf_op jit(solution)/shard_map/all_to_all | solution.py:44
  252.7 3.8 %copy-start.2 = (f32[128,8192]{1,0:T(8,128)S(1)}, f32[128,8192]{1,0:T(8,128)}, u32[]{:S(2)}) copy-start(f32[128,8192]{1,0:T(8,128)} %get-tuple-element.6) | copy-start | bytes 12582916
Sparse Core Ops, SparseCore 0:
  11.4 97.6 all-gather.2
where the time goes:
time: 360 us; the launch traced here: 359 us
  waiting for transfers between devices  249 us (69%)
  blocking collectives  43.6 us (12%)
  starting transfers between devices  23.2 us (6%)
  between operations  14.1 us (4%)
  matrix products  13.7 us (4%)
  other arithmetic  8.52 us (2%)
  local copies, waits for them, and re-layouts  7.28 us (2%)
    all_to_all x1, waiting for transfers between devices, body(): lax.all_to_all(weight_term.reshape(inner_count, outer_count, owner_rows,...  95.2 us
    all_to_all x1, waiting for transfers between devices, body(): lax.all_to_all(lax.all_to_all(weight_term.reshape(inner_count, outer_coun...  89.3 us
    all_gather x1, waiting for transfers between devices, body(): weight_rows = lax.all_gather(kv_weight, 'inner', axis=0, tiled=True)  54.8 us
    all_gather x1, blocking collectives, body(): gain_piece = lax.all_gather(norm_gain, 'inner', axis=0, tiled=True)  43.6 us
    all_to_all x1, starting transfers between devices, body(): lax.all_to_all(lax.all_to_all(gain_term.reshape(inner_count, outer_count,...  8.09 us
  transfers between devices with their start and end apart: 5, of which 5 were waited for; matrix products, arithmetic and copies ran while one was open for 5% of the time, Pallas kernels for 0%

commit v1 on v0

v1 whole, which is shorter than its diff:
```python
import functools

import jax
import jax.numpy as jnp
from jax import lax
from jax.experimental import pallas as pl
from jax.experimental.pallas import tpu as pltpu
from jax.sharding import Mesh, PartitionSpec as P

AXES = ("xh", "y", "c", "z", "xl")
F32, BF16 = jnp.float32, jnp.bfloat16


def prep_kernel(core, tokens, cot, sent, scaled, inv, total):
    step = pl.program_id(0)
    other = 1 - core[0]
    wide = tokens[...].astype(F32)
    part = jnp.sum(wide * wide, -1, keepdims=True)

    @pl.when(step == 0)
    def _():
        total[...] = part

    @pl.when(step > 0)
    def _():
        total[...] += part

    for j in range(sent.shape[1] // 256):
        start = pl.multiple_of(512 * j + 256 * other, 256)
        sent[:, 256 * j : 256 * (j + 1)] = tokens[:, pl.ds(start, 256)]

    @pl.when(step == pl.num_programs(0) - 1)
    def _():
        width = tokens.shape[1] * pl.num_programs(0)
        root = lax.rsqrt(total[...] / width + 1e-05)
        inv[...] = jnp.broadcast_to(root, inv.shape)
        scaled[...] = (cot[...].astype(F32) * root).astype(BF16)


def prep(core, tokens, cot):
    rows, width = tokens.shape
    steps = 4
    return pl.pallas_call(
        prep_kernel,
        grid_spec=pltpu.PrefetchScalarGridSpec(
            num_scalar_prefetch=1,
            grid=(steps,),
            in_specs=[
                pl.BlockSpec((rows, width // steps), lambda i, c: (0, i)),
                pl.BlockSpec(cot.shape, lambda i, c: (0, 0)),
            ],
            out_specs=[
                pl.BlockSpec((rows, width // steps // 2), lambda i, c: (0, i)),
                pl.BlockSpec(cot.shape, lambda i, c: (0, 0)),
                pl.BlockSpec((rows, 128), lambda i, c: (0, 0)),
            ],
            scratch_shapes=[pltpu.VMEM((rows, 1), F32)],
        ),
        out_shape=[
            jax.ShapeDtypeStruct((rows, width // 2), BF16),
            jax.ShapeDtypeStruct(cot.shape, BF16),
            jax.ShapeDtypeStruct((rows, 128), F32),
        ],
        compiler_params=pltpu.CompilerParams(vmem_limit_bytes=16 << 20),
        cost_estimate=pl.CostEstimate(flops=2 * rows * width, bytes_accessed=3 * rows * width, transcendentals=0),
    )(core, tokens, cot)


def outer_kernel(core, tokens, got, mine, theirs, out):
    own = core[0]
    blocks = got.shape[1] // 256
    for j in range(blocks):
        start = pl.multiple_of(512 * j + 256 * own, 256)
        left = jnp.concatenate([tokens[:, pl.ds(start, 256)], got[:, 256 * j : 256 * (j + 1)]], 0)
        right = jnp.concatenate([mine[...], theirs[...]], 0)
        u = lax.dot_general(left, right, (((0,), (0,)), ((), ())), preferred_element_type=F32)
        u = u.reshape(8, 2, 16, 256).astype(BF16)
        for xl in range(2):
            out[0, xl, j] = u[:, xl]


def outer_terms(core, tokens, got, mine, theirs):
    rows, width = tokens.shape
    steps = 4
    per = 16 // steps
    return pl.pallas_call(
        outer_kernel,
        grid_spec=pltpu.PrefetchScalarGridSpec(
            num_scalar_prefetch=1,
            grid=(steps,),
            in_specs=[
                pl.BlockSpec((rows, width // steps), lambda i, c: (0, i)),
                pl.BlockSpec((rows, width // 2 // steps), lambda i, c: (0, i)),
                pl.BlockSpec(mine.shape, lambda i, c: (0, 0)),
                pl.BlockSpec(mine.shape, lambda i, c: (0, 0)),
            ],
            out_specs=pl.BlockSpec(
                (1, 2, per, 8, 16, 256), lambda i, c: (i // 2, 0, i % 2, 0, 0, 0)
            ),
        ),
        out_shape=jax.ShapeDtypeStruct((2, 2, 8, 8, 16, 256), BF16),
        compiler_params=pltpu.CompilerParams(vmem_limit_bytes=16 << 20),
        cost_estimate=pl.CostEstimate(flops=2 * rows * width * 256, bytes_accessed=6 * rows * width, transcendentals=0),
    )(core, tokens, got, mine, theirs)


def final_kernel(core, tokens, cot, inv, w_mine, w_theirs, kv_out, token_grad):
    own = core[0]
    rows, width = tokens.shape
    total = jnp.zeros((rows, 256), F32)
    pieces = []
    for xh in range(2):
        for y in range(8):
            for ref, side in ((w_mine, own), (w_theirs, 1 - own)):
                start = pl.multiple_of(512 * (8 * xh + y) + 256 * side, 256)
                pieces.append((ref, xh, y, start))
    for ref, xh, y, start in pieces:
        w = jnp.concatenate([ref[xh, 0, y], ref[xh, 1, y]], 0)
        total += jnp.dot(tokens[:, pl.ds(start, 256)], w, preferred_element_type=F32)
    root = inv[:, :1]
    kv = total * root
    kv_out[...] = kv.astype(BF16)
    slopes = jnp.sum(cot[...].astype(F32) * kv, -1, keepdims=True) * (1.0 / width)
    slopes = root * slopes
    for ref, xh, y, start in pieces:
        w = jnp.concatenate([ref[xh, 0, y], ref[xh, 1, y]], 0)
        back = lax.dot_general(cot[...], w, (((1,), (1,)), ((), ())), preferred_element_type=F32)
        x = tokens[:, pl.ds(start, 256)].astype(F32)
        token_grad[:, pl.ds(start, 256)] = (root * (back - x * slopes)).astype(BF16)


def final(core, tokens, cot, inv, w_mine, w_theirs):
    vmem = pl.BlockSpec(memory_space=pltpu.VMEM)
    return pl.pallas_call(
        final_kernel,
        in_specs=[pl.BlockSpec(memory_space=pltpu.SMEM)] + [vmem] * 5,
        out_specs=[vmem, vmem],
        out_shape=[
            jax.ShapeDtypeStruct(cot.shape, BF16),
            jax.ShapeDtypeStruct(tokens.shape, BF16),
        ],
        compiler_params=pltpu.CompilerParams(vmem_limit_bytes=24 << 20),
        cost_estimate=pl.CostEstimate(flops=4 * tokens.size * 256, bytes_accessed=8 << 20, transcendentals=0),
    )(core, tokens, cot, inv, w_mine, w_theirs)


SWAP = [(0, 1), (1, 0)]


def body(tokens, cotangent, kv_weight, norm_gain):
    factor = 1.0 / 256.0
    core = lax.axis_index("c").astype(jnp.int32).reshape(1)
    half = lax.axis_index("xl")
    piece = 2 * lax.axis_index("z") + half
    gain = norm_gain.astype(F32)[:, None]
    wide = kv_weight.astype(F32)
    scaled_weight = (wide * gain).astype(BF16)

    share = lax.dynamic_slice_in_dim(scaled_weight, 128 * half, 128, 0)
    along_y = lax.all_to_all(jnp.broadcast_to(share, (8, 128, 256)), "y", 0, 0, tiled=True)
    w_mine = lax.all_to_all(
        jnp.broadcast_to(along_y, (4, 8, 128, 256)), ("xh", "xl"), 0, 0, tiled=True
    ).reshape(2, 2, 8, 128, 256)
    w_theirs = lax.ppermute(w_mine, "c", SWAP)

    sent, scaled, inv = prep(core, tokens, cotangent)
    got = lax.ppermute(sent, "c", SWAP)
    got_scaled = lax.ppermute(scaled, "c", SWAP)
    u = outer_terms(core, tokens, got, scaled, got_scaled)
    u = lax.all_to_all(u.reshape(4, 64, 16, 256), ("xh", "xl"), 0, 0, tiled=True)
    u = jnp.sum(u, 0, dtype=F32).astype(BF16)
    u = lax.all_to_all(u, ("y", "z"), 0, 0, tiled=True)
    u = jnp.sum(u, 0, dtype=F32) * factor
    kv_grad = (u * lax.dynamic_slice_in_dim(gain, 16 * piece, 16, 0)).astype(BF16)
    gain_grad = jnp.sum(u * lax.dynamic_slice_in_dim(wide, 16 * piece, 16, 0), -1).astype(BF16)

    kv_out, token_grad = final(core, tokens, cotangent, inv, w_mine, w_theirs)
    return (kv_out, token_grad, kv_grad, gain_grad)


def solution(mesh):
    split = Mesh(mesh.devices.reshape(2, 8, 2, 8, 2), AXES)
    every, inner = P(AXES, None), ("xh", "y", "c")
    return jax.shard_map(
        body,
        mesh=split,
        in_specs=(every, every, P(inner, None), P(inner)),
        out_specs=(every, every, every, P(AXES)),
        check_vma=False,
    )
```

time: 360 us -> 128 us (0.36)
  the two profiles are of different devices: /device:TPU:1 before, /device:TPU:16 now
where the time goes in v1:
time: 128 us; the launch traced here: 127 us
  waiting for transfers between devices  53.3 us (42%)
  starting transfers between devices  32.9 us (26%)
  blocking collectives  22 us (17%)
  Pallas kernels  9.26 us (7%)
  other arithmetic  5.34 us (4%)
  local copies, waits for them, and re-layouts  3.71 us (3%)
    all_to_all x1, blocking collectives, body(): lax.all_to_all(jnp.broadcast_to(share, (8, 128, 256)), 'y', 0, 0, tiled=T...  22 us
    all_to_all x1, waiting for transfers between devices, body(): lax.all_to_all(u.reshape(4, 64, 16, 256), ('xh', 'xl'), 0, 0, tiled=True)  21.2 us
    all_to_all x1, starting transfers between devices, body(): u = lax.all_to_all(u, ('y', 'z'), 0, 0, tiled=True)  17.7 us
    all_to_all x1, waiting for transfers between devices, body(): u = lax.all_to_all(u, ('y', 'z'), 0, 0, tiled=True)  17 us
    all_to_all x1, waiting for transfers between devices, body(): lax.all_to_all(jnp.broadcast_to(along_y, (4, 8, 128, 256)), ('xh', 'xl'),...  14.2 us
    pallas_call x1, Pallas kernels, final(): pl.pallas_call(final_kernel, in_specs=[pl.BlockSpec(memory_space=pltpu.SM...  6.02 us
    all_to_all x1, starting transfers between devices, body(): lax.all_to_all(jnp.broadcast_to(along_y, (4, 8, 128, 256)), ('xh', 'xl'),...  4.57 us
    all_to_all x1, starting transfers between devices, body(): lax.all_to_all(u.reshape(4, 64, 16, 256), ('xh', 'xl'), 0, 0, tiled=True)  4.45 us
  transfers between devices with their start and end apart: 6, of which 4 were waited for; matrix products, arithmetic and copies ran while one was open for 3% of the time, Pallas kernels for 3%

profile of v1, /device:TPU:16, one launch (start us, length us, event | category | flops | bytes accessed | tf_op | source)
XLA Modules:
  0.0 127.3 jit_solution(11889507363474697335)
XLA Ops:
  0.6 0.9 convert_element_type.20
  1.6 0.7 dynamic-slice.1
  2.3 0.1 fusion
  2.4 22.0 %all_to_all.20 = bf16[8,128,256]{2,1,0:T(8,128)(2,1)S(1)} all-to-all(bf16[8,128,256]{2,1,0:T(8,128)(2,1)S(1)} %broadcast_in_dim.7), channel_id=1, replica_groups=mesh['xh'=2,'y'=8,'c'=2,'z'=8,'xl'=2] {'y'}, dimensions={0} | all-to-all | bytes 1048576 | tf_op jit(solution)/shard_map/all_to_all | solution.py:160
  24.5 1.6 %broadcast_in_dim.8 = bf16[4,8,128,256]{3,2,1,0:T(8,128)(2,1)} broadcast(bf16[8,128,256]{2,1,0:T(8,128)(2,1)S(1)} %all_to_all.20), dimensions={1,2,3} | broadcast | bytes 2621440 | tf_op jit(solution)/shard_map/broadcast_in_dim | solution.py:162
  26.0 0.0 copy-start
  26.0 0.0 copy-start.2
  26.0 4.6 %all-to-all-start.1 = ((bf16[4,8,128,256]{3,2,1,0:T(8,128)(2,1)}), bf16[4,8,128,256]{3,2,1,0:T(8,128)(2,1)}, u32[]{:S(2)}, u32[]{:S(2)}) async-start(bf16[4,8,128,256]{3,2,1,0:T(8,128)(2,1)} %broadcast_in_dim.8), calls=%async_computation.1 | async-start | bytes 4194304 | tf_op jit(solution)/shard_map/all_to_all | solution.py:161
  30.6 0.0 copy-done
  30.6 0.0 copy-done.2
  30.6 1.3 %shard_map.75 = (bf16[128,4096]{1,0:T(8,128)(2,1)S(1)}, bf16[128,256]{1,0:T(8,128)(2,1)S(1)}, f32[128,128]{1,0:T(8,128)S(1)}) custom-call(s32[1]{0:T(128)} %bitcast.core, bf16[128,8192]{1,0:T(8,128)(2,1)S(1)} %copy-done, bf16[128,256]{1,0:T(8,128)(2,1)S(1)} %copy-done.2), custom_call_target="tpu_custom_call" | custom-call | flops 2097152 | bytes 3145728 | tf_op jit(solution)/shard_map/pallas_call | solution.py:43
  31.9 1.9 %collective-permute-start.1 = (bf16[128,4096]{1,0:T(8,128)(2,1)S(1)}, bf16[128,4096]{1,0:T(8,128)(2,1)S(1)}, u32[]{:S(2)}, u32[]{:S(2)}) collective-permute-start(bf16[128,4096]{1,0:T(8,128)(2,1)S(1)} %get-tuple-element.12), channel_id=1, source_target_pairs={{0,16},{16,0},{1,17},{17,1},{2,18},{18,2},{3,19},{19,3},{4,20},{20... | collective-permute-start | bytes 3145736 | tf_op jit(solution)/shard_map/ppermute | solution.py:167
  33.9 2.4 %collective-permute-start.2 = (bf16[128,256]{1,0:T(8,128)(2,1)S(1)}, bf16[128,256]{1,0:T(8,128)(2,1)S(1)}, u32[]{:S(2)}, u32[]{:S(2)}) collective-permute-start(bf16[128,256]{1,0:T(8,128)(2,1)S(1)} %get-tuple-element.13.mine), channel_id=1, source_target_pairs={{0,16},{16,0},{1,17},{17,1},{2,18},{18,2},{3,19},{19,3},{4,20},{20... | collective-permute-start | bytes 196616 | tf_op jit(solution)/shard_map/ppermute | solution.py:168
  36.3 0.9 collective-permute-done.2.theirs
  37.1 0.0 collective-permute-done.1.got
  37.2 2.0 %shard_map.77 = bf16[2,2,8,8,16,256]{5,4,3,2,1,0:T(8,128)(2,1)S(1)} custom-call(s32[1]{0:T(128)} %bitcast.core, bf16[128,8192]{1,0:T(8,128)(2,1)S(1)} %copy-done, bf16[128,4096]{1,0:T(8,128)(2,1)S(1)} %collective-permute-done.1.got, bf16[128,256]{1,0:T(8,128)(2,1)S(1)} %get-tuple-element.13.mine, bf16[128,256]{1,0:T(8,128)(2,1)S(1)} %collective-permute-done.2.theirs), custom_call_target="tpu_custom_call" | custom-call | flops 536870912 | bytes 6291456 | tf_op jit(solution)/shard_map/pallas_call | solution.py:86
  39.1 0.0 copy-start.1
  39.1 1.4 %copy-done.1 = bf16[2,2,8,8,16,256]{5,4,3,2,1,0:T(8,128)(2,1)} copy-done((bf16[2,2,8,8,16,256]{5,4,3,2,1,0:T(8,128)(2,1)}, bf16[2,2,8,8,16,256]{5,4,3,2,1,0:T(8,128)(2,1)S(1)}, u32[]{:S(2)}) %copy-start.1) | copy-done | bytes 2097176
  40.5 14.2 %all-to-all-done.1 = bf16[4,8,128,256]{3,2,1,0:T(8,128)(2,1)} async-done(((bf16[4,8,128,256]{3,2,1,0:T(8,128)(2,1)}), bf16[4,8,128,256]{3,2,1,0:T(8,128)(2,1)}, u32[]{:S(2)}, u32[]{:S(2)}) %all-to-all-start.1) | async-done | bytes 2097184 | tf_op jit(solution)/shard_map/all_to_all | solution.py:161
  54.7 4.5 %all-to-all-start.2 = ((bf16[4,64,16,256]{3,2,1,0:T(8,128)(2,1)}), bf16[4,64,16,256]{3,2,1,0:T(8,128)(2,1)}, u32[]{:S(2)}, u32[]{:S(2)}) async-start(bf16[4,64,16,256]{3,2,1,0:T(8,128)(2,1)} %bitcast.3), calls=%async_computation.2 | async-start | bytes 4194304 | tf_op jit(solution)/shard_map/all_to_all | solution.py:170
  59.1 0.0 copy-start.3
  59.1 1.9 %collective-permute-start = (bf16[2,2,8,128,256]{4,3,2,1,0:T(8,128)(2,1)}, bf16[2,2,8,128,256]{4,3,2,1,0:T(8,128)(2,1)}, u32[]{:S(2)}, u32[]{:S(2)}) collective-permute-start(bf16[2,2,8,128,256]{4,3,2,1,0:T(8,128)(2,1)} %bitcast.1.w_mine), channel_id=1, source_target_pairs={{0,16},{16,0},{1,17},{17,1},{2,18},{18,2},{3,19},{19,3},{4,20},{20... | collective-permute-start | bytes 6291464 | tf_op jit(solution)/shard_map/ppermute | solution.py:164
  61.1 21.2 %all-to-all-done.2 = bf16[4,64,16,256]{3,2,1,0:T(8,128)(2,1)} async-done(((bf16[4,64,16,256]{3,2,1,0:T(8,128)(2,1)}), bf16[4,64,16,256]{3,2,1,0:T(8,128)(2,1)}, u32[]{:S(2)}, u32[]{:S(2)}) %all-to-all-start.2) | async-done | bytes 2097184 | tf_op jit(solution)/shard_map/all_to_all | solution.py:170
  82.3 2.9 %reduce_sum.30 = bf16[64,16,256]{2,1,0:T(8,128)(2,1)} reduce(bf16[4,64,16,256]{3,2,1,0:T(8,128)(2,1)} %all-to-all-done.2, bf16[]{:T(256)} %constant.22.clone.1), dimensions={0}, to_apply=%region_0.0 | reduce | flops 786432 | bytes 2621442 | tf_op jit(solution)/shard_map/reduce_sum | solution.py:171
  85.1 17.7 %all-to-all-start.3 = ((bf16[64,16,256]{2,1,0:T(8,128)(2,1)}), bf16[64,16,256]{2,1,0:T(8,128)(2,1)S(1)}, u32[]{:S(2)}, u32[]{:S(2)}) async-start(bf16[64,16,256]{2,1,0:T(8,128)(2,1)} %reduce_sum.30), calls=%async_computation.3 | async-start | bytes 1048576 | tf_op jit(solution)/shard_map/all_to_all | solution.py:172
  102.8 0.0 copy-done.3
  102.8 0.1 dynamic-slice_multiply_fusion.1
  102.9 17.0 %all-to-all-done.3 = bf16[64,16,256]{2,1,0:T(8,128)(2,1)S(1)} async-done(((bf16[64,16,256]{2,1,0:T(8,128)(2,1)}), bf16[64,16,256]{2,1,0:T(8,128)(2,1)S(1)}, u32[]{:S(2)}, u32[]{:S(2)}) %all-to-all-start.3) | async-done | bytes 524320 | tf_op jit(solution)/shard_map/all_to_all | solution.py:172
  119.9 0.1 convert_reduce_fusion
  120.0 1.3 %multiply_reduce_fusion = (bf16[16]{0:T(256)(128)(2,1)}, bf16[16,256]{1,0:T(8,128)(2,1)}) fusion(f32[256,256]{1,0:T(8,128)S(1)} %convert_element_type.20, s32[]{:T(128)S(6)} %select_n.8, f32[16,256]{1,0:T(8,128)S(1)} %convert_reduce_fusion, f32[16]{0:T(128)S(1)} %dynamic-slice_multiply_fusion.1), kind=kLoop, calls=%fused_computation.3 | loop fusion | flops 20464 | bytes 41060 | tf_op jit(solution)/shard_map/reduce_sum | solution.py:175
  121.3 0.0 collective-permute-done.w_theirs
  121.3 6.0 %shard_map.76 = (bf16[128,256]{1,0:T(8,128)(2,1)}, bf16[128,8192]{1,0:T(8,128)(2,1)}) custom-call(s32[1]{0:T(128)} %bitcast.core, bf16[128,8192]{1,0:T(8,128)(2,1)S(1)} %copy-done, bf16[128,256]{1,0:T(8,128)(2,1)S(1)} %copy-done.2, f32[128,128]{1,0:T(8,128)S(1)} %get-tuple-element.9.inv, bf16[2,2,8,128,256]{4,3,2,1,0:T(8,128)(2,1)} %bitcast.1.w_mine, ...), custom_call_target="tpu_custom_call" | custom-call | flops 1073741824 | bytes 8388608 | tf_op jit(solution)/shard_map/pallas_call | solution.py:134
  (2 shorter events, 0.0 us)
Async XLA Ops:
  26.0 4.6 %copy-start = (bf16[128,8192]{1,0:T(8,128)(2,1)S(1)}, bf16[128,8192]{1,0:T(8,128)(2,1)}, u32[]{:S(2)}) copy-start(bf16[128,8192]{1,0:T(8,128)(2,1)} %tokens.5) | copy-start | bytes 6291460
  26.0 4.6 %copy-start.2 = (bf16[128,256]{1,0:T(8,128)(2,1)S(1)}, bf16[128,256]{1,0:T(8,128)(2,1)}, u32[]{:S(2)}) copy-start(bf16[128,256]{1,0:T(8,128)(2,1)} %cot.3) | copy-start | bytes 196612
  26.0 28.6 %all-to-all-start.1 = ((bf16[4,8,128,256]{3,2,1,0:T(8,128)(2,1)}), bf16[4,8,128,256]{3,2,1,0:T(8,128)(2,1)}, u32[]{:S(2)}, u32[]{:S(2)}) async-start(bf16[4,8,128,256]{3,2,1,0:T(8,128)(2,1)} %broadcast_in_dim.8), calls=%async_computation.1 | async-start | bytes 4194304 | tf_op jit(solution)/shard_map/all_to_all | solution.py:161
  31.9 5.2 %collective-permute-start.1 = (bf16[128,4096]{1,0:T(8,128)(2,1)S(1)}, bf16[128,4096]{1,0:T(8,128)(2,1)S(1)}, u32[]{:S(2)}, u32[]{:S(2)}) collective-permute-start(bf16[128,4096]{1,0:T(8,128)(2,1)S(1)} %get-tuple-element.12), channel_id=1, source_target_pairs={{0,16},{16,0},{1,17},{17,1},{2,18},{18,2},{3,19},{19,3},{4,20},{20... | collective-permute-start | bytes 3145736 | tf_op jit(solution)/shard_map/ppermute | solution.py:167
  33.9 3.3 %collective-permute-start.2 = (bf16[128,256]{1,0:T(8,128)(2,1)S(1)}, bf16[128,256]{1,0:T(8,128)(2,1)S(1)}, u32[]{:S(2)}, u32[]{:S(2)}) collective-permute-start(bf16[128,256]{1,0:T(8,128)(2,1)S(1)} %get-tuple-element.13.mine), channel_id=1, source_target_pairs={{0,16},{16,0},{1,17},{17,1},{2,18},{18,2},{3,19},{19,3},{4,20},{20... | collective-permute-start | bytes 196616 | tf_op jit(solution)/shard_map/ppermute | solution.py:168
  39.1 1.4 %copy-start.1 = (bf16[2,2,8,8,16,256]{5,4,3,2,1,0:T(8,128)(2,1)}, bf16[2,2,8,8,16,256]{5,4,3,2,1,0:T(8,128)(2,1)S(1)}, u32[]{:S(2)}) copy-start(bf16[2,2,8,8,16,256]{5,4,3,2,1,0:T(8,128)(2,1)S(1)} %shard_map.77) | copy-start | bytes 6291460
  54.7 27.6 %all-to-all-start.2 = ((bf16[4,64,16,256]{3,2,1,0:T(8,128)(2,1)}), bf16[4,64,16,256]{3,2,1,0:T(8,128)(2,1)}, u32[]{:S(2)}, u32[]{:S(2)}) async-start(bf16[4,64,16,256]{3,2,1,0:T(8,128)(2,1)} %bitcast.3), calls=%async_computation.2 | async-start | bytes 4194304 | tf_op jit(solution)/shard_map/all_to_all | solution.py:170
  59.1 43.7 %copy-start.3 = (bf16[256]{0:T(256)(128)(2,1)S(1)}, bf16[256]{0:T(256)(128)(2,1)}, u32[]{:S(2)}) copy-start(bf16[256]{0:T(256)(128)(2,1)} %param.7) | copy-start | bytes 1540
  59.1 62.1 %collective-permute-start = (bf16[2,2,8,128,256]{4,3,2,1,0:T(8,128)(2,1)}, bf16[2,2,8,128,256]{4,3,2,1,0:T(8,128)(2,1)}, u32[]{:S(2)}, u32[]{:S(2)}) collective-permute-start(bf16[2,2,8,128,256]{4,3,2,1,0:T(8,128)(2,1)} %bitcast.1.w_mine), channel_id=1, source_target_pairs={{0,16},{16,0},{1,17},{17,1},{2,18},{18,2},{3,19},{19,3},{4,20},{20... | collective-permute-start | bytes 6291464 | tf_op jit(solution)/shard_map/ppermute | solution.py:164
  85.1 34.8 %all-to-all-start.3 = ((bf16[64,16,256]{2,1,0:T(8,128)(2,1)}), bf16[64,16,256]{2,1,0:T(8,128)(2,1)S(1)}, u32[]{:S(2)}, u32[]{:S(2)}) async-start(bf16[64,16,256]{2,1,0:T(8,128)(2,1)} %reduce_sum.30), calls=%async_computation.3 | async-start | bytes 1048576 | tf_op jit(solution)/shard_map/all_to_all | solution.py:172

commit v2 on v1

v2 whole, which is shorter than its diff:
```python
import jax
import jax.numpy as jnp
from jax import lax
from jax.experimental import pallas as pl
from jax.experimental.pallas import tpu as pltpu
from jax.sharding import Mesh, PartitionSpec as P

AXES = ("xh", "y", "c", "z", "xl")
F32, BF16 = jnp.float32, jnp.bfloat16


def prep_kernel(core, tokens, cot, sent, scaled, inv, total):
    step = pl.program_id(0)
    other = 1 - core[0]
    wide = tokens[...].astype(F32)
    part = jnp.sum(wide * wide, -1, keepdims=True)

    @pl.when(step == 0)
    def _():
        total[...] = part

    @pl.when(step > 0)
    def _():
        total[...] += part

    for j in range(sent.shape[1] // 256):
        start = pl.multiple_of(512 * j + 256 * other, 256)
        sent[:, 256 * j : 256 * (j + 1)] = tokens[:, pl.ds(start, 256)]

    @pl.when(step == pl.num_programs(0) - 1)
    def _():
        width = tokens.shape[1] * pl.num_programs(0)
        root = lax.rsqrt(total[...] / width + 1e-05)
        inv[...] = jnp.broadcast_to(root, inv.shape)
        scaled[...] = (cot[...].astype(F32) * root).astype(BF16)


def prep(core, tokens, cot):
    rows, width = tokens.shape
    steps = 4
    return pl.pallas_call(
        prep_kernel,
        grid_spec=pltpu.PrefetchScalarGridSpec(
            num_scalar_prefetch=1,
            grid=(steps,),
            in_specs=[
                pl.BlockSpec((rows, width // steps), lambda i, c: (0, i)),
                pl.BlockSpec(cot.shape, lambda i, c: (0, 0)),
            ],
            out_specs=[
                pl.BlockSpec((rows, width // steps // 2), lambda i, c: (0, i)),
                pl.BlockSpec(cot.shape, lambda i, c: (0, 0)),
                pl.BlockSpec((rows, 128), lambda i, c: (0, 0)),
            ],
            scratch_shapes=[pltpu.VMEM((rows, 1), F32)],
        ),
        out_shape=[
            jax.ShapeDtypeStruct((rows, width // 2), BF16),
            jax.ShapeDtypeStruct(cot.shape, BF16),
            jax.ShapeDtypeStruct((rows, 128), F32),
        ],
        compiler_params=pltpu.CompilerParams(vmem_limit_bytes=16 << 20),
        cost_estimate=pl.CostEstimate(flops=2 * rows * width, bytes_accessed=3 * rows * width, transcendentals=0),
    )(core, tokens, cot)


def outer_kernel(place, tokens, got, mine, theirs, out0, out1, out2, out3):
    core, xh, xl = place[0], place[1], place[2]
    right = jnp.concatenate([mine[...], theirs[...]], 0)
    for hi in range(2):
        outs = ((out0, out1), (out2, out3))[hi]
        for y in range(8):
            block = 8 * (hi + xh - 2 * hi * xh) + y
            start = pl.multiple_of(512 * block + 256 * core, 256)
            start_got = pl.multiple_of(256 * block, 256)
            left = jnp.concatenate([tokens[:, pl.ds(start, 256)], got[:, pl.ds(start_got, 256)]], 0)
            u = lax.dot_general(left, right, (((0,), (0,)), ((), ())), preferred_element_type=F32)
            u = u.reshape(8, 2, 16, 256)
            outs[0][y] = jnp.where(xl == 0, u[:, 0], u[:, 1]).astype(BF16)
            outs[1][y] = jnp.where(xl == 0, u[:, 1], u[:, 0]).astype(BF16)


def outer_terms(place, tokens, got, mine, theirs):
    vmem = pl.BlockSpec(memory_space=pltpu.VMEM)
    return pl.pallas_call(
        outer_kernel,
        in_specs=[pl.BlockSpec(memory_space=pltpu.SMEM)] + [vmem] * 4,
        out_specs=[vmem] * 4,
        out_shape=[jax.ShapeDtypeStruct((8, 8, 16, 256), BF16)] * 4,
        compiler_params=pltpu.CompilerParams(vmem_limit_bytes=16 << 20),
        cost_estimate=pl.CostEstimate(flops=2 * tokens.size * 256, bytes_accessed=6 * tokens.size, transcendentals=0),
    )(place, tokens, got, mine, theirs)


def final_kernel(place, tokens, cot, inv, *refs):
    core, xh, xl = place[0], place[1], place[2]
    own, other, (kv_out, token_grad) = refs[:4], refs[4:8], refs[8:]
    rows, width = tokens.shape
    g = cot[...]
    g = jnp.where(xl == 0, g, jnp.concatenate([g[:, 128:], g[:, :128]], 1))
    pieces = []
    for hi in range(2):
        for y in range(8):
            for refs_of, side in ((own, core), (other, 1 - core)):
                start = pl.multiple_of(512 * (8 * (hi + xh - 2 * hi * xh) + y) + 256 * side, 256)
                pieces.append((refs_of[2 * hi], refs_of[2 * hi + 1], y, start))
    total = jnp.zeros((rows, 256), F32)
    for a, b, y, start in pieces:
        w = jnp.concatenate([a[y], b[y]], 1)
        total += jnp.dot(tokens[:, pl.ds(start, 256)], w, preferred_element_type=F32)
    root = inv[:, :1]
    kv = total * root
    kv_out[...] = jnp.where(xl == 0, kv, jnp.concatenate([kv[:, 128:], kv[:, :128]], 1)).astype(BF16)
    slopes = jnp.sum(g.astype(F32) * kv, -1, keepdims=True) * (1.0 / width)
    slopes = root * slopes
    for a, b, y, start in pieces:
        w = jnp.concatenate([a[y], b[y]], 1)
        back = lax.dot_general(g, w, (((1,), (1,)), ((), ())), preferred_element_type=F32)
        x = tokens[:, pl.ds(start, 256)].astype(F32)
        token_grad[:, pl.ds(start, 256)] = (root * (back - x * slopes)).astype(BF16)


def final(place, tokens, cot, inv, own, other):
    vmem = pl.BlockSpec(memory_space=pltpu.VMEM)
    return pl.pallas_call(
        final_kernel,
        in_specs=[pl.BlockSpec(memory_space=pltpu.SMEM)] + [vmem] * 11,
        out_specs=[vmem, vmem],
        out_shape=[
            jax.ShapeDtypeStruct(cot.shape, BF16),
            jax.ShapeDtypeStruct(tokens.shape, BF16),
        ],
        compiler_params=pltpu.CompilerParams(vmem_limit_bytes=24 << 20),
        cost_estimate=pl.CostEstimate(flops=4 * tokens.size * 256, bytes_accessed=8 << 20, transcendentals=0),
    )(place, tokens, cot, inv, *own, *other)


SWAP = [(0, 1), (1, 0)]


def along_x(values):
    moved = {}
    for k in (2, 1, 3):
        moved[k] = lax.ppermute(values[k - 1], ("xh", "xl"), [(i, i ^ k) for i in range(4)])
    return [moved[1], moved[2], moved[3]]


def body(tokens, cotangent, kv_weight, norm_gain):
    factor = 1.0 / 256.0
    half = lax.axis_index("xl")
    place = jnp.stack([lax.axis_index("c"), lax.axis_index("xh"), half]).astype(jnp.int32)
    piece = 2 * lax.axis_index("z") + half
    gain = norm_gain.astype(F32)[:, None]
    wide = kv_weight.astype(F32)
    share = (jnp.where(half == 0, wide[:, :128], wide[:, 128:]) * gain).astype(BF16)

    sent, scaled, inv = prep(place, tokens, cotangent)
    share, inv = lax.optimization_barrier((share, inv))
    got = lax.ppermute(sent, "c", SWAP)
    got_scaled = lax.ppermute(scaled, "c", SWAP)
    terms = outer_terms(place, tokens, got, scaled, got_scaled)
    moved = along_x(terms[1:])

    along_y = lax.all_to_all(jnp.broadcast_to(share, (8, 256, 128)), "y", 0, 0, tiled=True)
    own = [along_y] + along_x([along_y] * 3)
    other = [lax.ppermute(w, "c", SWAP) for w in own]

    u = sum(m.astype(F32) for m in (terms[0], *moved)).astype(BF16)
    u = lax.all_to_all(u, "y", 0, 0, tiled=True)
    u = jnp.sum(u, 0, dtype=F32).astype(BF16)
    u = lax.all_to_all(u, "z", 0, 0, tiled=True)
    u = jnp.sum(u, 0, dtype=F32) * factor
    kv_grad = (u * lax.dynamic_slice_in_dim(gain, 16 * piece, 16, 0)).astype(BF16)
    gain_grad = jnp.sum(u * lax.dynamic_slice_in_dim(wide, 16 * piece, 16, 0), -1).astype(BF16)

    kv_out, token_grad = final(place, tokens, cotangent, inv, own, other)
    return (kv_out, token_grad, kv_grad, gain_grad)


def solution(mesh):
    split = Mesh(mesh.devices.reshape(2, 8, 2, 8, 2), AXES)
    every, inner = P(AXES, None), ("xh", "y", "c")
    return jax.shard_map(
        body,
        mesh=split,
        in_specs=(every, every, P(inner, None), P(inner)),
        out_specs=(every, every, every, P(AXES)),
        check_vma=False,
    )
```

time: 128 us -> 104 us (0.81)
  the two profiles are of different devices: /device:TPU:16 before, /device:TPU:1 now
where the time goes in v2:
time: 104 us; the launch traced here: 102 us
  starting transfers between devices  55.1 us (53%)
  waiting for transfers between devices  22.8 us (22%)
  Pallas kernels  11.6 us (11%)
  other arithmetic  7.71 us (7%)
  local copies, waits for them, and re-layouts  4.1 us (4%)
    ppermute x6, starting transfers between devices, along_x(): lax.ppermute(values[k - 1], ('xh', 'xl'), [(i, i ^ k) for i in range(4)])  17.3 us
    ppermute x6, waiting for transfers between devices, along_x(): lax.ppermute(values[k - 1], ('xh', 'xl'), [(i, i ^ k) for i in range(4)])  17.1 us
    ppermute x4, starting transfers between devices, body(): other = [lax.ppermute(w, 'c', SWAP) for w in own]  9.48 us
    ppermute x1, starting transfers between devices, body(): got = lax.ppermute(sent, 'c', SWAP)  8.77 us
    all_to_all x1, starting transfers between devices, body(): u = lax.all_to_all(u, 'z', 0, 0, tiled=True)  7.6 us
    all_to_all x1, starting transfers between devices, body(): u = lax.all_to_all(u, 'y', 0, 0, tiled=True)  6.55 us
    pallas_call x1, Pallas kernels, final(): pl.pallas_call(final_kernel, in_specs=[pl.BlockSpec(memory_space=pltpu.SM...  5.62 us
    all_to_all x1, starting transfers between devices, body(): lax.all_to_all(jnp.broadcast_to(share, (8, 256, 128)), 'y', 0, 0, tiled=T...  3.49 us
  transfers between devices with their start and end apart: 15, of which 7 were waited for; matrix products, arithmetic and copies ran while one was open for 6% of the time, Pallas kernels for 9%

profile of v2, /device:TPU:1, one launch (start us, length us, event | category | flops | bytes accessed | tf_op | source)
XLA Modules:
  0.0 102.1 jit_solution(10904979560720042382)
XLA Ops:
  0.7 1.6 %copy-done = bf16[128,8192]{1,0:T(8,128)(2,1)S(1)} copy-done((bf16[128,8192]{1,0:T(8,128)(2,1)S(1)}, bf16[128,8192]{1,0:T(8,128)(2,1)}, u32[]{:S(2)}) %copy-start) | copy-done | bytes 2097176
  2.3 0.8 copy-done.3
  3.2 2.9 %shard_map.75 = (bf16[128,4096]{1,0:T(8,128)(2,1)}, bf16[128,256]{1,0:T(8,128)(2,1)S(1)}, f32[128,128]{1,0:T(8,128)S(1)}) custom-call(s32[3]{0:T(128)S(1)} %pad_add_fusion.core.place, bf16[128,8192]{1,0:T(8,128)(2,1)S(1)} %copy-done, bf16[128,256]{1,0:T(8,128)(2,1)S(1)} %copy-done.3), custom_call_target="tpu_custom_call" | custom-call | flops 2097152 | bytes 3145728 | tf_op jit(solution)/shard_map/pallas_call | solution.py:41
  6.0 8.8 %collective-permute-start.7 = (bf16[128,4096]{1,0:T(8,128)(2,1)}, bf16[128,4096]{1,0:T(8,128)(2,1)}, u32[]{:S(2)}, u32[]{:S(2)}) collective-permute-start(bf16[128,4096]{1,0:T(8,128)(2,1)} %get-tuple-element.20), channel_id=1, source_target_pairs={{0,16},{16,0},{1,17},{17,1},{2,18},{18,2},{3,19},{19,3},{4,20},{20... | collective-permute-start | bytes 3145736 | tf_op jit(solution)/shard_map/ppermute | solution.py:159
  14.8 0.9 convert_element_type.35
  15.9 0.9 broadcast_in_dim.4
  16.7 3.5 %all-to-all-start = ((bf16[8,256,128]{2,1,0:T(8,128)(2,1)}), bf16[8,256,128]{2,1,0:T(8,128)(2,1)S(1)}, u32[]{:S(2)}, u32[]{:S(2)}) async-start(bf16[8,256,128]{2,1,0:T(8,128)(2,1)} %broadcast_in_dim.4), calls=%async_computation | async-start | bytes 1048576 | tf_op jit(solution)/shard_map/all_to_all | solution.py:164
  20.2 1.9 %collective-permute-start.8 = (bf16[128,256]{1,0:T(8,128)(2,1)S(1)}, bf16[128,256]{1,0:T(8,128)(2,1)S(1)}, u32[]{:S(2)}, u32[]{:S(2)}) collective-permute-start(bf16[128,256]{1,0:T(8,128)(2,1)S(1)} %get-tuple-element.21.mine), channel_id=1, source_target_pairs={{0,16},{16,0},{1,17},{17,1},{2,18},{18,2},{3,19},{19,3},{4,20},{20... | collective-permute-start | bytes 196616 | tf_op jit(solution)/shard_map/ppermute | solution.py:160
  22.2 1.2 %collective-permute-done.8.theirs = bf16[128,256]{1,0:T(8,128)(2,1)S(1)} collective-permute-done((bf16[128,256]{1,0:T(8,128)(2,1)S(1)}, bf16[128,256]{1,0:T(8,128)(2,1)S(1)}, u32[]{:S(2)}, u32[]{:S(2)}) %collective-permute-start.8) | collective-permute-done | bytes 65568 | tf_op jit(solution)/shard_map/ppermute | solution.py:160
  23.4 3.1 %shard_map.77 = (bf16[8,8,16,256]{3,2,1,0:T(8,128)(2,1)S(1)}, bf16[8,8,16,256]{3,2,1,0:T(8,128)(2,1)}, bf16[8,8,16,256]{3,2,1,0:T(8,128)(2,1)}, bf16[8,8,16,256]{3,2,1,0:T(8,128)(2,1)}) custom-call(s32[3]{0:T(128)S(1)} %pad_add_fusion.core.place, bf16[128,8192]{1,0:T(8,128)(2,1)S(1)} %copy-done.1, bf16[128,4096]{1,0:T(8,128)(2,1)} %collective-permute-done.7.got, ...), custom_call_target="tpu_custom_call" | custom-call | flops 536870912 | bytes 6291456 | tf_op jit(solution)/shard_map/pallas_call | solution.py:85
  26.5 0.8 copy-done.2
  27.2 2.6 %collective-permute-start.10 = (bf16[8,8,16,256]{3,2,1,0:T(8,128)(2,1)}, bf16[8,8,16,256]{3,2,1,0:T(8,128)(2,1)}, u32[]{:S(2)}, u32[]{:S(2)}) collective-permute-start(bf16[8,8,16,256]{3,2,1,0:T(8,128)(2,1)} %get-tuple-element.24), channel_id=1, source_target_pairs={{0,256},{1,257},{256,0},{257,1},{2,258},{3,259},{258,2},{259,3},{4... | collective-permute-start | bytes 1572872 | tf_op jit(solution)/shard_map/ppermute | solution.py:144
  29.8 2.8 %collective-permute-start.11 = (bf16[8,8,16,256]{3,2,1,0:T(8,128)(2,1)}, bf16[8,8,16,256]{3,2,1,0:T(8,128)(2,1)}, u32[]{:S(2)}, u32[]{:S(2)}) collective-permute-start(bf16[8,8,16,256]{3,2,1,0:T(8,128)(2,1)} %get-tuple-element.25), channel_id=1, source_target_pairs={{0,257},{1,256},{256,1},{257,0},{2,259},{3,258},{258,3},{259,2},{4... | collective-permute-start | bytes 1572872 | tf_op jit(solution)/shard_map/ppermute | solution.py:144
  32.6 3.0 %collective-permute-start.9 = (bf16[8,8,16,256]{3,2,1,0:T(8,128)(2,1)}, bf16[8,8,16,256]{3,2,1,0:T(8,128)(2,1)}, u32[]{:S(2)}, u32[]{:S(2)}) collective-permute-start(bf16[8,8,16,256]{3,2,1,0:T(8,128)(2,1)} %get-tuple-element.23), channel_id=1, source_target_pairs={{0,1},{1,0},{256,257},{257,256},{2,3},{3,2},{258,259},{259,258},{4... | collective-permute-start | bytes 1572872 | tf_op jit(solution)/shard_map/ppermute | solution.py:144
  35.6 2.6 %all-to-all-done.refs_0_ = bf16[8,256,128]{2,1,0:T(8,128)(2,1)S(1)} async-done(((bf16[8,256,128]{2,1,0:T(8,128)(2,1)}), bf16[8,256,128]{2,1,0:T(8,128)(2,1)S(1)}, u32[]{:S(2)}, u32[]{:S(2)}) %all-to-all-start) | async-done | bytes 524320 | tf_op jit(solution)/shard_map/all_to_all | solution.py:164
  38.2 1.9 %collective-permute-start = (bf16[8,256,128]{2,1,0:T(8,128)(2,1)S(1)}, bf16[8,256,128]{2,1,0:T(8,128)(2,1)S(1)}, u32[]{:S(2)}, u32[]{:S(2)}) collective-permute-start(bf16[8,256,128]{2,1,0:T(8,128)(2,1)S(1)} %all-to-all-done.refs_0_), channel_id=1, source_target_pairs={{0,1},{1,0},{256,257},{257,256},{2,3},{3,2},{258,259},{259,258},{4... | collective-permute-start | bytes 1572872 | tf_op jit(solution)/shard_map/ppermute | solution.py:144
  40.1 3.6 %collective-permute-start.1 = (bf16[8,256,128]{2,1,0:T(8,128)(2,1)S(1)}, bf16[8,256,128]{2,1,0:T(8,128)(2,1)}, u32[]{:S(2)}, u32[]{:S(2)}) collective-permute-start(bf16[8,256,128]{2,1,0:T(8,128)(2,1)S(1)} %all-to-all-done.refs_0_), channel_id=1, source_target_pairs={{0,256},{1,257},{256,0},{257,1},{2,258},{3,259},{258,2},{259,3},{4... | collective-permute-start | bytes 1572872 | tf_op jit(solution)/shard_map/ppermute | solution.py:144
  44.4 3.4 %collective-permute-start.2 = (bf16[8,256,128]{2,1,0:T(8,128)(2,1)S(1)}, bf16[8,256,128]{2,1,0:T(8,128)(2,1)}, u32[]{:S(2)}, u32[]{:S(2)}) collective-permute-start(bf16[8,256,128]{2,1,0:T(8,128)(2,1)S(1)} %all-to-all-done.refs_0_), channel_id=1, source_target_pairs={{0,257},{1,256},{256,1},{257,0},{2,259},{3,258},{258,3},{259,2},{4... | collective-permute-start | bytes 1572872 | tf_op jit(solution)/shard_map/ppermute | solution.py:144
  47.8 8.2 %collective-permute-done.11 = bf16[8,8,16,256]{3,2,1,0:T(8,128)(2,1)} collective-permute-done((bf16[8,8,16,256]{3,2,1,0:T(8,128)(2,1)}, bf16[8,8,16,256]{3,2,1,0:T(8,128)(2,1)}, u32[]{:S(2)}, u32[]{:S(2)}) %collective-permute-start.11) | collective-permute-done | bytes 524320 | tf_op jit(solution)/shard_map/ppermute | solution.py:144
  56.0 2.6 %add_convert_fusion = bf16[8,8,16,256]{3,2,1,0:T(8,128)(2,1)} fusion(bf16[8,8,16,256]{3,2,1,0:T(8,128)(2,1)} %collective-permute-done.11, bf16[8,8,16,256]{3,2,1,0:T(8,128)(2,1)} %collective-permute-done.10, bf16[8,8,16,256]{3,2,1,0:T(8,128)(2,1)} %collective-permute-done.9, bf16[8,8,16,256]{3,2,1,0:T(8,128)(2,1)} %copy-done.2), kind=kLoop, calls=%fused_computation | loop fusion | flops 2097152 | bytes 2621440 | tf_op jit(solution)/shard_map/convert_element_type | solution.py:168
  58.7 6.6 %all-to-all-start.1 = ((bf16[8,8,16,256]{3,2,1,0:T(8,128)(2,1)}), bf16[8,8,16,256]{3,2,1,0:T(8,128)(2,1)}, u32[]{:S(2)}, u32[]{:S(2)}) async-start(bf16[8,8,16,256]{3,2,1,0:T(8,128)(2,1)} %add_convert_fusion), calls=%async_computation.1 | async-start | bytes 1048576 | tf_op jit(solution)/shard_map/all_to_all | solution.py:169
  65.2 2.8 %collective-permute-start.3 = (bf16[8,256,128]{2,1,0:T(8,128)(2,1)S(1)}, bf16[8,256,128]{2,1,0:T(8,128)(2,1)}, u32[]{:S(2)}, u32[]{:S(2)}) collective-permute-start(bf16[8,256,128]{2,1,0:T(8,128)(2,1)S(1)} %all-to-all-done.refs_0_), channel_id=1, source_target_pairs={{0,16},{16,0},{1,17},{17,1},{2,18},{18,2},{3,19},{19,3},{4,20},{20... | collective-permute-start | bytes 1572872 | tf_op jit(solution)/shard_map/ppermute | solution.py:166
  68.0 1.9 %collective-permute-start.4 = (bf16[8,256,128]{2,1,0:T(8,128)(2,1)S(1)}, bf16[8,256,128]{2,1,0:T(8,128)(2,1)}, u32[]{:S(2)}, u32[]{:S(2)}) collective-permute-start(bf16[8,256,128]{2,1,0:T(8,128)(2,1)S(1)} %collective-permute-done.refs_1_), channel_id=1, source_target_pairs={{0,16},{16,0},{1,17},{17,1},{2,18},{18,2},{3,19},{19,3},{4,20},{20... | collective-permute-start | bytes 1572872 | tf_op jit(solution)/shard_map/ppermute | solution.py:166
  69.9 8.1 %collective-permute-done.1.refs_2_ = bf16[8,256,128]{2,1,0:T(8,128)(2,1)} collective-permute-done((bf16[8,256,128]{2,1,0:T(8,128)(2,1)S(1)}, bf16[8,256,128]{2,1,0:T(8,128)(2,1)}, u32[]{:S(2)}, u32[]{:S(2)}) %collective-permute-start.1) | collective-permute-done | bytes 524320 | tf_op jit(solution)/shard_map/ppermute | solution.py:144
  78.1 2.9 %collective-permute-start.5 = (bf16[8,256,128]{2,1,0:T(8,128)(2,1)}, bf16[8,256,128]{2,1,0:T(8,128)(2,1)}, u32[]{:S(2)}, u32[]{:S(2)}) collective-permute-start(bf16[8,256,128]{2,1,0:T(8,128)(2,1)} %collective-permute-done.1.refs_2_), channel_id=1, source_target_pairs={{0,16},{16,0},{1,17},{17,1},{2,18},{18,2},{3,19},{19,3},{4,20},{20... | collective-permute-start | bytes 1572872 | tf_op jit(solution)/shard_map/ppermute | solution.py:166
  81.0 1.9 %collective-permute-start.6 = (bf16[8,256,128]{2,1,0:T(8,128)(2,1)}, bf16[8,256,128]{2,1,0:T(8,128)(2,1)}, u32[]{:S(2)}, u32[]{:S(2)}) collective-permute-start(bf16[8,256,128]{2,1,0:T(8,128)(2,1)} %collective-permute-done.2.refs_3_), channel_id=1, source_target_pairs={{0,16},{16,0},{1,17},{17,1},{2,18},{18,2},{3,19},{19,3},{4,20},{20... | collective-permute-start | bytes 1572872 | tf_op jit(solution)/shard_map/ppermute | solution.py:166
  83.3 1.7 %reduce_sum.30 = bf16[8,16,256]{2,1,0:T(8,128)(2,1)} reduce(bf16[8,8,16,256]{3,2,1,0:T(8,128)(2,1)} %all-to-all-done.1, bf16[]{:T(256)} %constant.23.clone.1), dimensions={0}, to_apply=%region_0.1 | reduce | flops 229376 | bytes 589826 | tf_op jit(solution)/shard_map/reduce_sum | solution.py:170
  85.0 7.6 %all-to-all-start.2 = ((bf16[8,16,256]{2,1,0:T(8,128)(2,1)}), bf16[8,16,256]{2,1,0:T(8,128)(2,1)}, u32[]{:S(2)}, u32[]{:S(2)}) async-start(bf16[8,16,256]{2,1,0:T(8,128)(2,1)} %reduce_sum.30), calls=%async_computation.2 | async-start | bytes 131072 | tf_op jit(solution)/shard_map/all_to_all | solution.py:171
  92.7 5.6 %shard_map.76 = (bf16[128,256]{1,0:T(8,128)(2,1)}, bf16[128,8192]{1,0:T(8,128)(2,1)}) custom-call(s32[3]{0:T(128)S(1)} %pad_add_fusion.core.place, bf16[128,8192]{1,0:T(8,128)(2,1)S(1)} %copy-done.1, bf16[128,256]{1,0:T(8,128)(2,1)S(1)} %copy-done.4, f32[128,128]{1,0:T(8,128)S(1)} %get-tuple-element.16.inv, bf16[8,256,128]{2,1,0:T(8,128)(2,1)S(1)} %all-to-all-done.refs_0_, ...), custom_call_target="tpu_custom_call" | custom-call | flops 1073741824 | bytes 8388608 | tf_op jit(solution)/shard_map/pallas_call | solution.py:125
  98.4 1.6 %all-to-all-done.2 = bf16[8,16,256]{2,1,0:T(8,128)(2,1)} async-done(((bf16[8,16,256]{2,1,0:T(8,128)(2,1)}), bf16[8,16,256]{2,1,0:T(8,128)(2,1)}, u32[]{:S(2)}, u32[]{:S(2)}) %all-to-all-start.2) | async-done | bytes 65568 | tf_op jit(solution)/shard_map/all_to_all | solution.py:171
  100.0 0.9 convert_reduce_fusion
  100.8 1.3 %multiply_reduce_fusion = (bf16[16]{0:T(256)(128)(2,1)}, bf16[16,256]{1,0:T(8,128)(2,1)}) fusion(f32[256,256]{1,0:T(8,128)S(1)} %convert_element_type.35, s32[]{:T(128)S(6)} %select_n.14, f32[16,256]{1,0:T(8,128)S(1)} %convert_reduce_fusion, f32[16]{0:T(128)S(1)} %dynamic-slice_multiply_fusion), kind=kLoop, calls=%fused_computation.5 | loop fusion | flops 20464 | bytes 41060 | tf_op jit(solution)/shard_map/reduce_sum | solution.py:174
  (23 shorter events, 1.4 us)
Async XLA Ops:
  0.6 14.2 %copy-start.5 = (bf16[256]{0:T(256)(128)(2,1)S(1)}, bf16[256]{0:T(256)(128)(2,1)}, u32[]{:S(2)}) copy-start(bf16[256]{0:T(256)(128)(2,1)} %param.7) | copy-start | bytes 1540
  0.7 1.6 %copy-start = (bf16[128,8192]{1,0:T(8,128)(2,1)S(1)}, bf16[128,8192]{1,0:T(8,128)(2,1)}, u32[]{:S(2)}) copy-start(bf16[128,8192]{1,0:T(8,128)(2,1)} %tokens.5) | copy-start | bytes 6291460
  2.3 0.8 copy-start.3
  3.2 20.2 %copy-start.1 = (bf16[128,8192]{1,0:T(8,128)(2,1)S(1)}, bf16[128,8192]{1,0:T(8,128)(2,1)}, u32[]{:S(2)}) copy-start(bf16[128,8192]{1,0:T(8,128)(2,1)} %tokens.5) | copy-start | bytes 6291460
  6.0 17.4 %collective-permute-start.7 = (bf16[128,4096]{1,0:T(8,128)(2,1)}, bf16[128,4096]{1,0:T(8,128)(2,1)}, u32[]{:S(2)}, u32[]{:S(2)}) collective-permute-start(bf16[128,4096]{1,0:T(8,128)(2,1)} %get-tuple-element.20), channel_id=1, source_target_pairs={{0,16},{16,0},{1,17},{17,1},{2,18},{18,2},{3,19},{19,3},{4,20},{20... | collective-permute-start | bytes 3145736 | tf_op jit(solution)/shard_map/ppermute | solution.py:159
  16.7 21.5 %all-to-all-start = ((bf16[8,256,128]{2,1,0:T(8,128)(2,1)}), bf16[8,256,128]{2,1,0:T(8,128)(2,1)S(1)}, u32[]{:S(2)}, u32[]{:S(2)}) async-start(bf16[8,256,128]{2,1,0:T(8,128)(2,1)} %broadcast_in_dim.4), calls=%async_computation | async-start | bytes 1048576 | tf_op jit(solution)/shard_map/all_to_all | solution.py:164
  20.2 3.1 %collective-permute-start.8 = (bf16[128,256]{1,0:T(8,128)(2,1)S(1)}, bf16[128,256]{1,0:T(8,128)(2,1)S(1)}, u32[]{:S(2)}, u32[]{:S(2)}) collective-permute-start(bf16[128,256]{1,0:T(8,128)(2,1)S(1)} %get-tuple-element.21.mine), channel_id=1, source_target_pairs={{0,16},{16,0},{1,17},{17,1},{2,18},{18,2},{3,19},{19,3},{4,20},{20... | collective-permute-start | bytes 196616 | tf_op jit(solution)/shard_map/ppermute | solution.py:160
  26.5 0.8 copy-start.2
  27.2 17.1 %collective-permute-start.10 = (bf16[8,8,16,256]{3,2,1,0:T(8,128)(2,1)}, bf16[8,8,16,256]{3,2,1,0:T(8,128)(2,1)}, u32[]{:S(2)}, u32[]{:S(2)}) collective-permute-start(bf16[8,8,16,256]{3,2,1,0:T(8,128)(2,1)} %get-tuple-element.24), channel_id=1, source_target_pairs={{0,256},{1,257},{256,0},{257,1},{2,258},{3,259},{258,2},{259,3},{4... | collective-permute-start | bytes 1572872 | tf_op jit(solution)/shard_map/ppermute | solution.py:144
  29.8 26.2 %collective-permute-start.11 = (bf16[8,8,16,256]{3,2,1,0:T(8,128)(2,1)}, bf16[8,8,16,256]{3,2,1,0:T(8,128)(2,1)}, u32[]{:S(2)}, u32[]{:S(2)}) collective-permute-start(bf16[8,8,16,256]{3,2,1,0:T(8,128)(2,1)} %get-tuple-element.25), channel_id=1, source_target_pairs={{0,257},{1,256},{256,1},{257,0},{2,259},{3,258},{258,3},{259,2},{4... | collective-permute-start | bytes 1572872 | tf_op jit(solution)/shard_map/ppermute | solution.py:144
  32.6 23.4 %collective-permute-start.9 = (bf16[8,8,16,256]{3,2,1,0:T(8,128)(2,1)}, bf16[8,8,16,256]{3,2,1,0:T(8,128)(2,1)}, u32[]{:S(2)}, u32[]{:S(2)}) collective-permute-start(bf16[8,8,16,256]{3,2,1,0:T(8,128)(2,1)} %get-tuple-element.23), channel_id=1, source_target_pairs={{0,1},{1,0},{256,257},{257,256},{2,3},{3,2},{258,259},{259,258},{4... | collective-permute-start | bytes 1572872 | tf_op jit(solution)/shard_map/ppermute | solution.py:144
  38.2 29.8 %collective-permute-start = (bf16[8,256,128]{2,1,0:T(8,128)(2,1)S(1)}, bf16[8,256,128]{2,1,0:T(8,128)(2,1)S(1)}, u32[]{:S(2)}, u32[]{:S(2)}) collective-permute-start(bf16[8,256,128]{2,1,0:T(8,128)(2,1)S(1)} %all-to-all-done.refs_0_), channel_id=1, source_target_pairs={{0,1},{1,0},{256,257},{257,256},{2,3},{3,2},{258,259},{259,258},{4... | collective-permute-start | bytes 1572872 | tf_op jit(solution)/shard_map/ppermute | solution.py:144
  40.1 38.0 %collective-permute-start.1 = (bf16[8,256,128]{2,1,0:T(8,128)(2,1)S(1)}, bf16[8,256,128]{2,1,0:T(8,128)(2,1)}, u32[]{:S(2)}, u32[]{:S(2)}) collective-permute-start(bf16[8,256,128]{2,1,0:T(8,128)(2,1)S(1)} %all-to-all-done.refs_0_), channel_id=1, source_target_pairs={{0,256},{1,257},{256,0},{257,1},{2,258},{3,259},{258,2},{259,3},{4... | collective-permute-start | bytes 1572872 | tf_op jit(solution)/shard_map/ppermute | solution.py:144
  44.4 36.6 %collective-permute-start.2 = (bf16[8,256,128]{2,1,0:T(8,128)(2,1)S(1)}, bf16[8,256,128]{2,1,0:T(8,128)(2,1)}, u32[]{:S(2)}, u32[]{:S(2)}) collective-permute-start(bf16[8,256,128]{2,1,0:T(8,128)(2,1)S(1)} %all-to-all-done.refs_0_), channel_id=1, source_target_pairs={{0,257},{1,256},{256,1},{257,0},{2,259},{3,258},{258,3},{259,2},{4... | collective-permute-start | bytes 1572872 | tf_op jit(solution)/shard_map/ppermute | solution.py:144
  56.0 36.7 %copy-start.4 = (bf16[128,256]{1,0:T(8,128)(2,1)S(1)}, bf16[128,256]{1,0:T(8,128)(2,1)}, u32[]{:S(2)}) copy-start(bf16[128,256]{1,0:T(8,128)(2,1)} %cot.3) | copy-start | bytes 196612
  58.7 24.6 %all-to-all-start.1 = ((bf16[8,8,16,256]{3,2,1,0:T(8,128)(2,1)}), bf16[8,8,16,256]{3,2,1,0:T(8,128)(2,1)}, u32[]{:S(2)}, u32[]{:S(2)}) async-start(bf16[8,8,16,256]{3,2,1,0:T(8,128)(2,1)} %add_convert_fusion), calls=%async_computation.1 | async-start | bytes 1048576 | tf_op jit(solution)/shard_map/all_to_all | solution.py:169
  65.2 27.5 %collective-permute-start.3 = (bf16[8,256,128]{2,1,0:T(8,128)(2,1)S(1)}, bf16[8,256,128]{2,1,0:T(8,128)(2,1)}, u32[]{:S(2)}, u32[]{:S(2)}) collective-permute-start(bf16[8,256,128]{2,1,0:T(8,128)(2,1)S(1)} %all-to-all-done.refs_0_), channel_id=1, source_target_pairs={{0,16},{16,0},{1,17},{17,1},{2,18},{18,2},{3,19},{19,3},{4,20},{20... | collective-permute-start | bytes 1572872 | tf_op jit(solution)/shard_map/ppermute | solution.py:166
  68.0 24.7 %collective-permute-start.4 = (bf16[8,256,128]{2,1,0:T(8,128)(2,1)S(1)}, bf16[8,256,128]{2,1,0:T(8,128)(2,1)}, u32[]{:S(2)}, u32[]{:S(2)}) collective-permute-start(bf16[8,256,128]{2,1,0:T(8,128)(2,1)S(1)} %collective-permute-done.refs_1_), channel_id=1, source_target_pairs={{0,16},{16,0},{1,17},{17,1},{2,18},{18,2},{3,19},{19,3},{4,20},{20... | collective-permute-start | bytes 1572872 | tf_op jit(solution)/shard_map/ppermute | solution.py:166
  78.1 14.6 %collective-permute-start.5 = (bf16[8,256,128]{2,1,0:T(8,128)(2,1)}, bf16[8,256,128]{2,1,0:T(8,128)(2,1)}, u32[]{:S(2)}, u32[]{:S(2)}) collective-permute-start(bf16[8,256,128]{2,1,0:T(8,128)(2,1)} %collective-permute-done.1.refs_2_), channel_id=1, source_target_pairs={{0,16},{16,0},{1,17},{17,1},{2,18},{18,2},{3,19},{19,3},{4,20},{20... | collective-permute-start | bytes 1572872 | tf_op jit(solution)/shard_map/ppermute | solution.py:166
  81.0 11.8 %collective-permute-start.6 = (bf16[8,256,128]{2,1,0:T(8,128)(2,1)}, bf16[8,256,128]{2,1,0:T(8,128)(2,1)}, u32[]{:S(2)}, u32[]{:S(2)}) collective-permute-start(bf16[8,256,128]{2,1,0:T(8,128)(2,1)} %collective-permute-done.2.refs_3_), channel_id=1, source_target_pairs={{0,16},{16,0},{1,17},{17,1},{2,18},{18,2},{3,19},{19,3},{4,20},{20... | collective-permute-start | bytes 1572872 | tf_op jit(solution)/shard_map/ppermute | solution.py:166
  85.0 14.9 %all-to-all-start.2 = ((bf16[8,16,256]{2,1,0:T(8,128)(2,1)}), bf16[8,16,256]{2,1,0:T(8,128)(2,1)}, u32[]{:S(2)}, u32[]{:S(2)}) async-start(bf16[8,16,256]{2,1,0:T(8,128)(2,1)} %reduce_sum.30), calls=%async_computation.2 | async-start | bytes 131072 | tf_op jit(solution)/shard_map/all_to_all | solution.py:171

commit v3 on v2

v3 whole, which is shorter than its diff:
```python
import jax
import jax.numpy as jnp
from jax import lax
from jax.experimental import pallas as pl
from jax.experimental.pallas import tpu as pltpu
from jax.sharding import Mesh, PartitionSpec as P

AXES = ("xh", "y", "c", "z", "xl")
F32, BF16 = jnp.float32, jnp.bfloat16


def prep_kernel(tokens, cot, scaled, inv):
    wide = tokens[...].astype(F32)
    root = lax.rsqrt(jnp.mean(wide * wide, -1, keepdims=True) + 1e-05)
    inv[...] = jnp.broadcast_to(root, inv.shape)
    scaled[...] = (cot[...].astype(F32) * root).astype(BF16)


def prep(tokens, cot):
    rows, width = tokens.shape
    steps = 4
    return pl.pallas_call(
        prep_kernel,
        grid=(steps,),
        in_specs=[
            pl.BlockSpec((rows // steps, width), lambda i: (i, 0)),
            pl.BlockSpec((rows // steps, 256), lambda i: (i, 0)),
        ],
        out_specs=[
            pl.BlockSpec((rows // steps, 256), lambda i: (i, 0)),
            pl.BlockSpec((rows // steps, 128), lambda i: (i, 0)),
        ],
        out_shape=[
            jax.ShapeDtypeStruct(cot.shape, BF16),
            jax.ShapeDtypeStruct((rows, 128), F32),
        ],
        compiler_params=pltpu.CompilerParams(vmem_limit_bytes=8 << 20),
        cost_estimate=pl.CostEstimate(flops=2 * rows * width, bytes_accessed=2 * rows * width, transcendentals=0),
    )(tokens, cot)


def outer_kernel(place, tokens, got, mine, theirs, out0, out1, out2, out3):
    core, xh, xl = place[0], place[1], place[2]
    right = jnp.concatenate([mine[...], theirs[...]], 0)
    for hi in range(2):
        outs = ((out0, out1), (out2, out3))[hi]
        for y in range(8):
            block = 8 * (hi + xh - 2 * hi * xh) + y
            start = pl.multiple_of(512 * block + 256 * core, 256)
            left = jnp.concatenate([tokens[:, pl.ds(start, 256)], got[:, pl.ds(start, 256)]], 0)
            u = lax.dot_general(left, right, (((0,), (0,)), ((), ())), preferred_element_type=F32)
            u = u.reshape(8, 2, 16, 256)
            outs[0][y] = jnp.where(xl == 0, u[:, 0], u[:, 1]).astype(BF16)
            outs[1][y] = jnp.where(xl == 0, u[:, 1], u[:, 0]).astype(BF16)


def outer_terms(place, tokens, got, mine, theirs):
    vmem = pl.BlockSpec(memory_space=pltpu.VMEM)
    return pl.pallas_call(
        outer_kernel,
        in_specs=[pl.BlockSpec(memory_space=pltpu.SMEM)] + [vmem] * 4,
        out_specs=[vmem] * 4,
        out_shape=[jax.ShapeDtypeStruct((8, 8, 16, 256), BF16)] * 4,
        compiler_params=pltpu.CompilerParams(vmem_limit_bytes=10 << 20),
        cost_estimate=pl.CostEstimate(flops=2 * tokens.size * 256, bytes_accessed=6 * tokens.size, transcendentals=0),
    )(place, tokens, got, mine, theirs)


def final_kernel(place, tokens, cot, inv, own_a, own_b, other_a, other_b, kv_out, token_grad):
    core, xh, parity = place[0], place[1], place[3]
    rows, width = tokens.shape
    g = cot[...]
    g = jnp.where(parity == 0, g, jnp.concatenate([g[:, 128:], g[:, :128]], 1))
    pieces = []
    for hi in range(2):
        for y in range(8):
            for a, b, side in ((own_a, own_b, core), (other_a, other_b, 1 - core)):
                start = pl.multiple_of(512 * (8 * (hi + xh - 2 * hi * xh) + y) + 256 * side, 256)
                pieces.append((a, b, y, hi, start))
    total = jnp.zeros((rows, 256), F32)
    for a, b, y, hi, start in pieces:
        w = jnp.concatenate([a[y, hi], b[y, hi]], 1)
        total += jnp.dot(tokens[:, pl.ds(start, 256)], w, preferred_element_type=F32)
    root = inv[:, :1]
    kv = total * root
    kv_out[...] = jnp.where(parity == 0, kv, jnp.concatenate([kv[:, 128:], kv[:, :128]], 1)).astype(BF16)
    slopes = jnp.sum(g.astype(F32) * kv, -1, keepdims=True) * (1.0 / width)
    slopes = root * slopes
    for a, b, y, hi, start in pieces:
        w = jnp.concatenate([a[y, hi], b[y, hi]], 1)
        back = lax.dot_general(g, w, (((1,), (1,)), ((), ())), preferred_element_type=F32)
        x = tokens[:, pl.ds(start, 256)].astype(F32)
        token_grad[:, pl.ds(start, 256)] = (root * (back - x * slopes)).astype(BF16)


def final(place, tokens, cot, inv, weights):
    vmem = pl.BlockSpec(memory_space=pltpu.VMEM)
    return pl.pallas_call(
        final_kernel,
        in_specs=[pl.BlockSpec(memory_space=pltpu.SMEM)] + [vmem] * 7,
        out_specs=[vmem, vmem],
        out_shape=[
            jax.ShapeDtypeStruct(cot.shape, BF16),
            jax.ShapeDtypeStruct(tokens.shape, BF16),
        ],
        compiler_params=pltpu.CompilerParams(vmem_limit_bytes=14 << 20),
        cost_estimate=pl.CostEstimate(flops=4 * tokens.size * 256, bytes_accessed=8 << 20, transcendentals=0),
    )(place, tokens, cot, inv, *weights)


SWAP = [(0, 1), (1, 0)]


def along_x(values):
    moved = {}
    for k in (2, 1, 3):
        moved[k] = lax.ppermute(values[k - 1], ("xh", "xl"), [(i, i ^ k) for i in range(4)])
    return [moved[1], moved[2], moved[3]]


ALONG_Z = [(z, z ^ 1) for z in range(8)] + [(8 + z, 8 + (z + 1 if z % 2 else z - 1) % 8) for z in range(8)]


def body(tokens, cotangent, kv_weight, norm_gain):
    factor = 1.0 / 256.0
    half = lax.axis_index("xl")
    along_z = lax.axis_index("z")
    parity = along_z % 2
    place = jnp.stack([lax.axis_index("c"), lax.axis_index("xh"), half, parity]).astype(jnp.int32)
    piece = 2 * along_z + half
    gain = norm_gain.astype(F32)[:, None]

    scaled_weight = (kv_weight.astype(F32) * gain).astype(BF16)
    across = lax.ppermute(scaled_weight, ("xh", "xl"), [(i, i ^ 3) for i in range(4)])

    got = lax.ppermute(tokens, "c", SWAP)
    scaled, inv = prep(tokens, cotangent)
    got_scaled = lax.ppermute(scaled, "c", SWAP)
    share = jnp.stack([scaled_weight, across])
    share = jnp.where(parity == 0, share[:, :, :128], share[:, :, 128:])
    share, got_scaled = lax.optimization_barrier((share, got_scaled))
    own_a = lax.all_to_all(jnp.broadcast_to(share, (8, 2, 256, 128)), "y", 0, 0, tiled=True)
    own_b = lax.ppermute(own_a, ("c", "z"), ALONG_Z)
    other_a = lax.ppermute(own_a, "c", SWAP)
    other_b = lax.ppermute(own_b, "c", SWAP)

    terms = outer_terms(place, tokens, got, scaled, got_scaled)
    moved = along_x(terms[1:])
    u = sum(m.astype(F32) for m in (terms[0], *moved)).astype(BF16)
    u = lax.all_to_all(u, "y", 0, 0, tiled=True)
    u = jnp.sum(u, 0, dtype=F32).astype(BF16)
    u = lax.all_to_all(u, "z", 0, 0, tiled=True)
    u = jnp.sum(u, 0, dtype=F32) * factor
    kv_grad = (u * lax.dynamic_slice_in_dim(gain, 16 * piece, 16, 0)).astype(BF16)
    rows = lax.dynamic_slice_in_dim(kv_weight, 16 * piece, 16, 0).astype(F32)
    gain_grad = jnp.sum(u * rows, -1).astype(BF16)

    kv_out, token_grad = final(place, tokens, cotangent, inv, (own_a, own_b, other_a, other_b))
    return (kv_out, token_grad, kv_grad, gain_grad)


def solution(mesh):
    split = Mesh(mesh.devices.reshape(2, 8, 2, 8, 2), AXES)
    every, inner = P(AXES, None), ("xh", "y", "c")
    return jax.shard_map(
        body,
        mesh=split,
        in_specs=(every, every, P(inner, None), P(inner)),
        out_specs=(every, every, every, P(AXES)),
        check_vma=False,
    )
```

time: 104 us -> 116 us (1.12)
  the two profiles are of different devices: /device:TPU:1 before, /device:TPU:6 now
where the time goes in v3:
time: 116 us; the launch traced here: 115 us
  starting transfers between devices  49.8 us (43%)
  waiting for transfers between devices  42.1 us (36%)
  Pallas kernels  9.9 us (9%)
  other arithmetic  7.66 us (7%)
  local copies, waits for them, and re-layouts  4.42 us (4%)
    all_to_all x1, waiting for transfers between devices, body(): lax.all_to_all(jnp.broadcast_to(share, (8, 2, 256, 128)), 'y', 0, 0, tile...  14.6 us
    all_to_all x1, waiting for transfers between devices, body(): u = lax.all_to_all(u, 'y', 0, 0, tiled=True)  11.6 us
    ppermute x3, starting transfers between devices, along_x(): lax.ppermute(values[k - 1], ('xh', 'xl'), [(i, i ^ k) for i in range(4)])  10.4 us
    all_to_all x1, starting transfers between devices, body(): u = lax.all_to_all(u, 'z', 0, 0, tiled=True)  10.3 us
    all_to_all x1, waiting for transfers between devices, body(): u = lax.all_to_all(u, 'z', 0, 0, tiled=True)  8.3 us
    ppermute x1, starting transfers between devices, body(): lax.ppermute(scaled_weight, ('xh', 'xl'), [(i, i ^ 3) for i in range(4)])  7.76 us
    all_to_all x1, starting transfers between devices, body(): u = lax.all_to_all(u, 'y', 0, 0, tiled=True)  6.92 us
    ppermute x3, waiting for transfers between devices, along_x(): lax.ppermute(values[k - 1], ('xh', 'xl'), [(i, i ^ k) for i in range(4)])  6.79 us
  transfers between devices with their start and end apart: 12, of which 6 were waited for; matrix products, arithmetic and copies ran while one was open for 8% of the time, Pallas kernels for 4%

profile of v3, /device:TPU:6, one launch (start us, length us, event | category | flops | bytes accessed | tf_op | source)
XLA Modules:
  0.0 114.8 jit_solution(2879558093138391289)
XLA Ops:
  0.6 2.1 %collective-permute-start.5 = (bf16[128,8192]{1,0:T(8,128)(2,1)}, bf16[128,8192]{1,0:T(8,128)(2,1)}, u32[]{:S(2)}, u32[]{:S(2)}) collective-permute-start(bf16[128,8192]{1,0:T(8,128)(2,1)} %tokens.5), channel_id=1, source_target_pairs={{0,16},{16,0},{1,17},{17,1},{2,18},{18,2},{3,19},{19,3},{4,20},{20... | collective-permute-start | bytes 6291464 | tf_op jit(solution)/shard_map/ppermute | solution.py:136
  2.7 0.7 convert_element_type.39
  3.4 1.0 multiply_convert_fusion
  4.4 7.8 %collective-permute-start = (bf16[256,256]{1,0:T(8,128)(2,1)S(1)}, bf16[256,256]{1,0:T(8,128)(2,1)S(1)}, u32[]{:S(2)}, u32[]{:S(2)}) collective-permute-start(bf16[256,256]{1,0:T(8,128)(2,1)S(1)} %multiply_convert_fusion), channel_id=1, source_target_pairs={{0,257},{1,256},{256,1},{257,0},{2,259},{3,258},{258,3},{259,2},{4... | collective-permute-start | bytes 393224 | tf_op jit(solution)/shard_map/ppermute | solution.py:134
  12.2 1.6 %copy-done = bf16[128,8192]{1,0:T(8,128)(2,1)S(1)} copy-done((bf16[128,8192]{1,0:T(8,128)(2,1)S(1)}, bf16[128,8192]{1,0:T(8,128)(2,1)}, u32[]{:S(2)}) %copy-start) | copy-done | bytes 2097176
  13.7 0.8 copy-done.3
  14.6 0.9 shard_map.75
  15.5 2.3 %collective-permute-start.1 = (bf16[128,256]{1,0:T(8,128)(2,1)S(1)}, bf16[128,256]{1,0:T(8,128)(2,1)S(1)}, u32[]{:S(2)}, u32[]{:S(2)}) collective-permute-start(bf16[128,256]{1,0:T(8,128)(2,1)S(1)} %get-tuple-element.15.mine), channel_id=1, source_target_pairs={{0,16},{16,0},{1,17},{17,1},{2,18},{18,2},{3,19},{19,3},{4,20},{20... | collective-permute-start | bytes 196616 | tf_op jit(solution)/shard_map/ppermute | solution.py:138
  17.7 0.1 fusion.2
  17.9 0.8 collective-permute-done.1.theirs
  18.7 1.2 %broadcast_in_dim.4 = bf16[8,2,256,128]{3,2,1,0:T(8,128)(2,1)} broadcast(bf16[2,256,128]{2,1,0:T(8,128)(2,1)S(1)} %fusion.1), dimensions={1,2,3} | broadcast | bytes 1179648 | tf_op jit(solution)/shard_map/broadcast_in_dim | solution.py:142
  19.9 3.6 %all-to-all-start = ((bf16[8,2,256,128]{3,2,1,0:T(8,128)(2,1)}), bf16[8,2,256,128]{3,2,1,0:T(8,128)(2,1)S(1)}, u32[]{:S(2)}, u32[]{:S(2)}) async-start(bf16[8,2,256,128]{3,2,1,0:T(8,128)(2,1)} %broadcast_in_dim.4), calls=%async_computation | async-start | bytes 2097152 | tf_op jit(solution)/shard_map/all_to_all | solution.py:142
  23.5 0.1 pad_add_fusion.place
  23.6 3.4 %shard_map.77 = (bf16[8,8,16,256]{3,2,1,0:T(8,128)(2,1)S(1)}, bf16[8,8,16,256]{3,2,1,0:T(8,128)(2,1)}, bf16[8,8,16,256]{3,2,1,0:T(8,128)(2,1)}, bf16[8,8,16,256]{3,2,1,0:T(8,128)(2,1)}) custom-call(s32[4]{0:T(128)S(1)} %pad_add_fusion.place, bf16[128,8192]{1,0:T(8,128)(2,1)S(1)} %copy-done.1, bf16[128,8192]{1,0:T(8,128)(2,1)} %collective-permute-done.5.got, ...), custom_call_target="tpu_custom_call" | custom-call | flops 536870912 | bytes 6291456 | tf_op jit(solution)/shard_map/pallas_call | solution.py:59
  27.0 0.8 copy-done.2
  27.8 1.9 %collective-permute-start.6 = (bf16[8,8,16,256]{3,2,1,0:T(8,128)(2,1)}, bf16[8,8,16,256]{3,2,1,0:T(8,128)(2,1)}, u32[]{:S(2)}, u32[]{:S(2)}) collective-permute-start(bf16[8,8,16,256]{3,2,1,0:T(8,128)(2,1)} %get-tuple-element.21), channel_id=1, source_target_pairs={{0,1},{1,0},{256,257},{257,256},{2,3},{3,2},{258,259},{259,258},{4... | collective-permute-start | bytes 1572872 | tf_op jit(solution)/shard_map/ppermute | solution.py:117
  29.7 4.3 %collective-permute-start.7 = (bf16[8,8,16,256]{3,2,1,0:T(8,128)(2,1)}, bf16[8,8,16,256]{3,2,1,0:T(8,128)(2,1)}, u32[]{:S(2)}, u32[]{:S(2)}) collective-permute-start(bf16[8,8,16,256]{3,2,1,0:T(8,128)(2,1)} %get-tuple-element.22), channel_id=1, source_target_pairs={{0,256},{1,257},{256,0},{257,1},{2,258},{3,259},{258,2},{259,3},{4... | collective-permute-start | bytes 1572872 | tf_op jit(solution)/shard_map/ppermute | solution.py:117
  34.0 4.2 %collective-permute-start.8 = (bf16[8,8,16,256]{3,2,1,0:T(8,128)(2,1)}, bf16[8,8,16,256]{3,2,1,0:T(8,128)(2,1)}, u32[]{:S(2)}, u32[]{:S(2)}) collective-permute-start(bf16[8,8,16,256]{3,2,1,0:T(8,128)(2,1)} %get-tuple-element.23), channel_id=1, source_target_pairs={{0,257},{1,256},{256,1},{257,0},{2,259},{3,258},{258,3},{259,2},{4... | collective-permute-start | bytes 1572872 | tf_op jit(solution)/shard_map/ppermute | solution.py:117
  38.2 14.6 %all-to-all-done.own_a = bf16[8,2,256,128]{3,2,1,0:T(8,128)(2,1)S(1)} async-done(((bf16[8,2,256,128]{3,2,1,0:T(8,128)(2,1)}), bf16[8,2,256,128]{3,2,1,0:T(8,128)(2,1)S(1)}, u32[]{:S(2)}, u32[]{:S(2)}) %all-to-all-start) | async-done | bytes 1048608 | tf_op jit(solution)/shard_map/all_to_all | solution.py:142
  52.8 2.2 %collective-permute-start.2 = (bf16[8,2,256,128]{3,2,1,0:T(8,128)(2,1)S(1)}, bf16[8,2,256,128]{3,2,1,0:T(8,128)(2,1)}, u32[]{:S(2)}, u32[]{:S(2)}) collective-permute-start(bf16[8,2,256,128]{3,2,1,0:T(8,128)(2,1)S(1)} %all-to-all-done.own_a), channel_id=1, source_target_pairs={{0,2},{2,0},{4,6},{6,4},{8,10},{10,8},{12,14},{14,12},{16,30},{18,... | collective-permute-start | bytes 3145736 | tf_op jit(solution)/shard_map/ppermute | solution.py:143
  55.1 0.4 collective-permute-done.7
  55.5 6.4 %collective-permute-done.8 = bf16[8,8,16,256]{3,2,1,0:T(8,128)(2,1)} collective-permute-done((bf16[8,8,16,256]{3,2,1,0:T(8,128)(2,1)}, bf16[8,8,16,256]{3,2,1,0:T(8,128)(2,1)}, u32[]{:S(2)}, u32[]{:S(2)}) %collective-permute-start.8) | collective-permute-done | bytes 524320 | tf_op jit(solution)/shard_map/ppermute | solution.py:117
  61.9 2.6 %add_convert_fusion = bf16[8,8,16,256]{3,2,1,0:T(8,128)(2,1)} fusion(bf16[8,8,16,256]{3,2,1,0:T(8,128)(2,1)} %collective-permute-done.8, bf16[8,8,16,256]{3,2,1,0:T(8,128)(2,1)} %collective-permute-done.7, bf16[8,8,16,256]{3,2,1,0:T(8,128)(2,1)} %collective-permute-done.6, bf16[8,8,16,256]{3,2,1,0:T(8,128)(2,1)} %copy-done.2), kind=kLoop, calls=%fused_computation | loop fusion | flops 2097152 | bytes 2621440 | tf_op jit(solution)/shard_map/convert_element_type | solution.py:149
  64.5 6.9 %all-to-all-start.1 = ((bf16[8,8,16,256]{3,2,1,0:T(8,128)(2,1)}), bf16[8,8,16,256]{3,2,1,0:T(8,128)(2,1)}, u32[]{:S(2)}, u32[]{:S(2)}) async-start(bf16[8,8,16,256]{3,2,1,0:T(8,128)(2,1)} %add_convert_fusion), calls=%async_computation.1 | async-start | bytes 1048576 | tf_op jit(solution)/shard_map/all_to_all | solution.py:150
  71.4 1.9 %collective-permute-start.3 = (bf16[8,2,256,128]{3,2,1,0:T(8,128)(2,1)S(1)}, bf16[8,2,256,128]{3,2,1,0:T(8,128)(2,1)}, u32[]{:S(2)}, u32[]{:S(2)}) collective-permute-start(bf16[8,2,256,128]{3,2,1,0:T(8,128)(2,1)S(1)} %all-to-all-done.own_a), channel_id=1, source_target_pairs={{0,16},{16,0},{1,17},{17,1},{2,18},{18,2},{3,19},{19,3},{4,20},{20... | collective-permute-start | bytes 3145736 | tf_op jit(solution)/shard_map/ppermute | solution.py:144
  73.4 2.4 %collective-permute-start.4 = (bf16[8,2,256,128]{3,2,1,0:T(8,128)(2,1)}, bf16[8,2,256,128]{3,2,1,0:T(8,128)(2,1)}, u32[]{:S(2)}, u32[]{:S(2)}) collective-permute-start(bf16[8,2,256,128]{3,2,1,0:T(8,128)(2,1)} %collective-permute-done.2.own_b), channel_id=1, source_target_pairs={{0,16},{16,0},{1,17},{17,1},{2,18},{18,2},{3,19},{19,3},{4,20},{20... | collective-permute-start | bytes 3145736 | tf_op jit(solution)/shard_map/ppermute | solution.py:145
  75.8 11.6 %all-to-all-done.1 = bf16[8,8,16,256]{3,2,1,0:T(8,128)(2,1)} async-done(((bf16[8,8,16,256]{3,2,1,0:T(8,128)(2,1)}), bf16[8,8,16,256]{3,2,1,0:T(8,128)(2,1)}, u32[]{:S(2)}, u32[]{:S(2)}) %all-to-all-start.1) | async-done | bytes 524320 | tf_op jit(solution)/shard_map/all_to_all | solution.py:150
  87.4 1.8 %reduce_sum.30 = bf16[8,16,256]{2,1,0:T(8,128)(2,1)} reduce(bf16[8,8,16,256]{3,2,1,0:T(8,128)(2,1)} %all-to-all-done.1, bf16[]{:T(256)} %constant.35.clone.1), dimensions={0}, to_apply=%region_0.1 | reduce | flops 229376 | bytes 589826 | tf_op jit(solution)/shard_map/reduce_sum | solution.py:151
  89.1 10.3 %all-to-all-start.2 = ((bf16[8,16,256]{2,1,0:T(8,128)(2,1)}), bf16[8,16,256]{2,1,0:T(8,128)(2,1)S(1)}, u32[]{:S(2)}, u32[]{:S(2)}) async-start(bf16[8,16,256]{2,1,0:T(8,128)(2,1)} %reduce_sum.30), calls=%async_computation.2 | async-start | bytes 131072 | tf_op jit(solution)/shard_map/all_to_all | solution.py:152
  99.5 8.3 %all-to-all-done.2 = bf16[8,16,256]{2,1,0:T(8,128)(2,1)S(1)} async-done(((bf16[8,16,256]{2,1,0:T(8,128)(2,1)}), bf16[8,16,256]{2,1,0:T(8,128)(2,1)S(1)}, u32[]{:S(2)}, u32[]{:S(2)}) %all-to-all-start.2) | async-done | bytes 65568 | tf_op jit(solution)/shard_map/all_to_all | solution.py:152
  107.9 1.3 %multiply_reduce_fusion = (bf16[16]{0:T(256)(128)(2,1)}, bf16[16,256]{1,0:T(8,128)(2,1)}) fusion(f32[16,256]{1,0:T(8,128)S(1)} %convert_reduce_fusion, bf16[256,256]{1,0:T(8,128)(2,1)S(1)} %copy-done.5, s32[]{:T(128)S(6)} %select_n.22, f32[16]{0:T(128)S(1)} %dynamic-slice_multiply_fusion), kind=kLoop, calls=%fused_computation.8 | loop fusion | flops 24560 | bytes 32868 | tf_op jit(solution)/shard_map/reduce_sum | solution.py:156
  109.2 5.6 %shard_map.76 = (bf16[128,256]{1,0:T(8,128)(2,1)}, bf16[128,8192]{1,0:T(8,128)(2,1)}) custom-call(s32[4]{0:T(128)S(1)} %pad_add_fusion.place, bf16[128,8192]{1,0:T(8,128)(2,1)S(1)} %copy-done.1, bf16[128,256]{1,0:T(8,128)(2,1)S(1)} %copy-done.4, f32[128,128]{1,0:T(8,128)S(1)} %get-tuple-element.14.inv, bf16[8,2,256,128]{3,2,1,0:T(8,128)(2,1)S(1)} %all-to-all-done.own_a, ...), custom_call_target="tpu_custom_call" | custom-call | flops 1073741824 | bytes 8388608 | tf_op jit(solution)/shard_map/pallas_call | solution.py:98
  (18 shorter events, 0.2 us)
Async XLA Ops:
  0.6 17.1 %copy-start.5 = (bf16[256,256]{1,0:T(8,128)(2,1)S(1)}, bf16[256,256]{1,0:T(8,128)(2,1)}, u32[]{:S(2)}) copy-start(bf16[256,256]{1,0:T(8,128)(2,1)} %param.6) | copy-start | bytes 393220
  0.6 22.9 %collective-permute-start.5 = (bf16[128,8192]{1,0:T(8,128)(2,1)}, bf16[128,8192]{1,0:T(8,128)(2,1)}, u32[]{:S(2)}, u32[]{:S(2)}) collective-permute-start(bf16[128,8192]{1,0:T(8,128)(2,1)} %tokens.5), channel_id=1, source_target_pairs={{0,16},{16,0},{1,17},{17,1},{2,18},{18,2},{3,19},{19,3},{4,20},{20... | collective-permute-start | bytes 6291464 | tf_op jit(solution)/shard_map/ppermute | solution.py:136
  4.4 13.5 %collective-permute-start = (bf16[256,256]{1,0:T(8,128)(2,1)S(1)}, bf16[256,256]{1,0:T(8,128)(2,1)S(1)}, u32[]{:S(2)}, u32[]{:S(2)}) collective-permute-start(bf16[256,256]{1,0:T(8,128)(2,1)S(1)} %multiply_convert_fusion), channel_id=1, source_target_pairs={{0,257},{1,256},{256,1},{257,0},{2,259},{3,258},{258,3},{259,2},{4... | collective-permute-start | bytes 393224 | tf_op jit(solution)/shard_map/ppermute | solution.py:134
  12.1 1.6 %copy-start = (bf16[128,8192]{1,0:T(8,128)(2,1)S(1)}, bf16[128,8192]{1,0:T(8,128)(2,1)}, u32[]{:S(2)}) copy-start(bf16[128,8192]{1,0:T(8,128)(2,1)} %tokens.5) | copy-start | bytes 6291460
  13.7 0.8 copy-start.3
  15.4 8.1 %copy-start.1 = (bf16[128,8192]{1,0:T(8,128)(2,1)S(1)}, bf16[128,8192]{1,0:T(8,128)(2,1)}, u32[]{:S(2)}) copy-start(bf16[128,8192]{1,0:T(8,128)(2,1)} %tokens.5) | copy-start | bytes 6291460
  15.5 3.3 %collective-permute-start.1 = (bf16[128,256]{1,0:T(8,128)(2,1)S(1)}, bf16[128,256]{1,0:T(8,128)(2,1)S(1)}, u32[]{:S(2)}, u32[]{:S(2)}) collective-permute-start(bf16[128,256]{1,0:T(8,128)(2,1)S(1)} %get-tuple-element.15.mine), channel_id=1, source_target_pairs={{0,16},{16,0},{1,17},{17,1},{2,18},{18,2},{3,19},{19,3},{4,20},{20... | collective-permute-start | bytes 196616 | tf_op jit(solution)/shard_map/ppermute | solution.py:138
  19.9 32.9 %all-to-all-start = ((bf16[8,2,256,128]{3,2,1,0:T(8,128)(2,1)}), bf16[8,2,256,128]{3,2,1,0:T(8,128)(2,1)S(1)}, u32[]{:S(2)}, u32[]{:S(2)}) async-start(bf16[8,2,256,128]{3,2,1,0:T(8,128)(2,1)} %broadcast_in_dim.4), calls=%async_computation | async-start | bytes 2097152 | tf_op jit(solution)/shard_map/all_to_all | solution.py:142
  27.0 0.8 copy-start.2
  27.8 27.3 %collective-permute-start.6 = (bf16[8,8,16,256]{3,2,1,0:T(8,128)(2,1)}, bf16[8,8,16,256]{3,2,1,0:T(8,128)(2,1)}, u32[]{:S(2)}, u32[]{:S(2)}) collective-permute-start(bf16[8,8,16,256]{3,2,1,0:T(8,128)(2,1)} %get-tuple-element.21), channel_id=1, source_target_pairs={{0,1},{1,0},{256,257},{257,256},{2,3},{3,2},{258,259},{259,258},{4... | collective-permute-start | bytes 1572872 | tf_op jit(solution)/shard_map/ppermute | solution.py:117
  29.7 25.8 %collective-permute-start.7 = (bf16[8,8,16,256]{3,2,1,0:T(8,128)(2,1)}, bf16[8,8,16,256]{3,2,1,0:T(8,128)(2,1)}, u32[]{:S(2)}, u32[]{:S(2)}) collective-permute-start(bf16[8,8,16,256]{3,2,1,0:T(8,128)(2,1)} %get-tuple-element.22), channel_id=1, source_target_pairs={{0,256},{1,257},{256,0},{257,1},{2,258},{3,259},{258,2},{259,3},{4... | collective-permute-start | bytes 1572872 | tf_op jit(solution)/shard_map/ppermute | solution.py:117
  34.0 27.9 %collective-permute-start.8 = (bf16[8,8,16,256]{3,2,1,0:T(8,128)(2,1)}, bf16[8,8,16,256]{3,2,1,0:T(8,128)(2,1)}, u32[]{:S(2)}, u32[]{:S(2)}) collective-permute-start(bf16[8,8,16,256]{3,2,1,0:T(8,128)(2,1)} %get-tuple-element.23), channel_id=1, source_target_pairs={{0,257},{1,256},{256,1},{257,0},{2,259},{3,258},{258,3},{259,2},{4... | collective-permute-start | bytes 1572872 | tf_op jit(solution)/shard_map/ppermute | solution.py:117
  52.8 20.5 %collective-permute-start.2 = (bf16[8,2,256,128]{3,2,1,0:T(8,128)(2,1)S(1)}, bf16[8,2,256,128]{3,2,1,0:T(8,128)(2,1)}, u32[]{:S(2)}, u32[]{:S(2)}) collective-permute-start(bf16[8,2,256,128]{3,2,1,0:T(8,128)(2,1)S(1)} %all-to-all-done.own_a), channel_id=1, source_target_pairs={{0,2},{2,0},{4,6},{6,4},{8,10},{10,8},{12,14},{14,12},{16,30},{18,... | collective-permute-start | bytes 3145736 | tf_op jit(solution)/shard_map/ppermute | solution.py:143
  61.9 47.3 %copy-start.4 = (bf16[128,256]{1,0:T(8,128)(2,1)S(1)}, bf16[128,256]{1,0:T(8,128)(2,1)}, u32[]{:S(2)}) copy-start(bf16[128,256]{1,0:T(8,128)(2,1)} %cot.3) | copy-start | bytes 196612
  64.5 22.9 %all-to-all-start.1 = ((bf16[8,8,16,256]{3,2,1,0:T(8,128)(2,1)}), bf16[8,8,16,256]{3,2,1,0:T(8,128)(2,1)}, u32[]{:S(2)}, u32[]{:S(2)}) async-start(bf16[8,8,16,256]{3,2,1,0:T(8,128)(2,1)} %add_convert_fusion), calls=%async_computation.1 | async-start | bytes 1048576 | tf_op jit(solution)/shard_map/all_to_all | solution.py:150
  71.4 37.7 %collective-permute-start.3 = (bf16[8,2,256,128]{3,2,1,0:T(8,128)(2,1)S(1)}, bf16[8,2,256,128]{3,2,1,0:T(8,128)(2,1)}, u32[]{:S(2)}, u32[]{:S(2)}) collective-permute-start(bf16[8,2,256,128]{3,2,1,0:T(8,128)(2,1)S(1)} %all-to-all-done.own_a), channel_id=1, source_target_pairs={{0,16},{16,0},{1,17},{17,1},{2,18},{18,2},{3,19},{19,3},{4,20},{20... | collective-permute-start | bytes 3145736 | tf_op jit(solution)/shard_map/ppermute | solution.py:144
  73.4 35.8 %collective-permute-start.4 = (bf16[8,2,256,128]{3,2,1,0:T(8,128)(2,1)}, bf16[8,2,256,128]{3,2,1,0:T(8,128)(2,1)}, u32[]{:S(2)}, u32[]{:S(2)}) collective-permute-start(bf16[8,2,256,128]{3,2,1,0:T(8,128)(2,1)} %collective-permute-done.2.own_b), channel_id=1, source_target_pairs={{0,16},{16,0},{1,17},{17,1},{2,18},{18,2},{3,19},{19,3},{4,20},{20... | collective-permute-start | bytes 3145736 | tf_op jit(solution)/shard_map/ppermute | solution.py:145
  89.1 18.7 %all-to-all-start.2 = ((bf16[8,16,256]{2,1,0:T(8,128)(2,1)}), bf16[8,16,256]{2,1,0:T(8,128)(2,1)S(1)}, u32[]{:S(2)}, u32[]{:S(2)}) async-start(bf16[8,16,256]{2,1,0:T(8,128)(2,1)} %reduce_sum.30), calls=%async_computation.2 | async-start | bytes 131072 | tf_op jit(solution)/shard_map/all_to_all | solution.py:152

commit v4 on v3

v4 whole, which is shorter than its diff:
```python
import itertools
import math

import jax
import jax.numpy as jnp
import numpy as np
from jax import lax
from jax.experimental import pallas as pl
from jax.experimental.pallas import tpu as pltpu
from jax.sharding import Mesh, PartitionSpec as P

AXES = ("xh", "yh", "yl", "c", "zh", "zl", "xl")
SIZES = (2, 4, 2, 2, 4, 2, 2)
F32, BF16 = jnp.float32, jnp.bfloat16


def prep_kernel(tokens, cot, scaled, inv):
    wide = tokens[...].astype(F32)
    root = lax.rsqrt(jnp.mean(wide * wide, -1, keepdims=True) + 1e-05)
    inv[...] = jnp.broadcast_to(root, inv.shape)
    scaled[...] = (cot[...].astype(F32) * root).astype(BF16)


def prep(tokens, cot):
    rows, width = tokens.shape
    steps = 4
    return pl.pallas_call(
        prep_kernel,
        grid=(steps,),
        in_specs=[
            pl.BlockSpec((rows // steps, width), lambda i: (i, 0)),
            pl.BlockSpec((rows // steps, 256), lambda i: (i, 0)),
        ],
        out_specs=[
            pl.BlockSpec((rows // steps, 256), lambda i: (i, 0)),
            pl.BlockSpec((rows // steps, 128), lambda i: (i, 0)),
        ],
        out_shape=[
            jax.ShapeDtypeStruct(cot.shape, BF16),
            jax.ShapeDtypeStruct((rows, 128), F32),
        ],
        compiler_params=pltpu.CompilerParams(vmem_limit_bytes=8 << 20),
        cost_estimate=pl.CostEstimate(flops=2 * rows * width, bytes_accessed=2 * rows * width, transcendentals=0),
    )(tokens, cot)


def merge_kernel(core, tokens, got, mine, theirs, weights, out):
    right = jnp.concatenate([mine[...], theirs[...]], 0)
    for xh in range(2):
        for yh in range(4):
            for yl in range(2):
                block = 8 * xh + 2 * yh + yl
                start = pl.multiple_of(512 * block + 256 * core[0], 256)
                left = jnp.concatenate([tokens[:, pl.ds(start, 256)], got[:, pl.ds(start, 256)]], 0)
                u = lax.dot_general(left, right, (((0,), (0,)), ((), ())), preferred_element_type=F32)
                u = u.reshape(4, 2, 2, 16, 256).astype(BF16)
                first = 64 * (4 * xh + yh)
                for xl in range(2):
                    for zl in range(2):
                        out[4 * xl + 2 * yl + zl, first : first + 64] = u[:, zl, xl].reshape(64, 256)
    for k in range(8):
        out[k, 512:] = weights[...]


def merge(core, tokens, got, mine, theirs, weights):
    vmem = pl.BlockSpec(memory_space=pltpu.VMEM)
    return pl.pallas_call(
        merge_kernel,
        in_specs=[pl.BlockSpec(memory_space=pltpu.SMEM)] + [vmem] * 5,
        out_specs=vmem,
        out_shape=jax.ShapeDtypeStruct((8, 1024, 256), BF16),
        compiler_params=pltpu.CompilerParams(vmem_limit_bytes=12 << 20),
        cost_estimate=pl.CostEstimate(flops=2 * tokens.size * 256, bytes_accessed=8 * tokens.size, transcendentals=0),
    )(core, tokens, got, mine, theirs, weights)


def final_kernel(core, tokens, cot, inv, w_mine, w_theirs, kv_out, token_grad):
    rows, width = tokens.shape
    pieces = []
    for block in range(16):
        for ref, side in ((w_mine, core[0]), (w_theirs, 1 - core[0])):
            pieces.append((ref, 32 * block, pl.multiple_of(512 * block + 256 * side, 256)))
    total = jnp.zeros((rows, 256), F32)
    for ref, row, start in pieces:
        w = ref[:, row : row + 32].reshape(256, 256)
        total += jnp.dot(tokens[:, pl.ds(start, 256)], w, preferred_element_type=F32)
    root = inv[:, :1]
    kv = total * root
    kv_out[...] = kv.astype(BF16)
    g = cot[...]
    slopes = jnp.sum(g.astype(F32) * kv, -1, keepdims=True) * (1.0 / width)
    slopes = root * slopes
    for ref, row, start in pieces:
        w = ref[:, row : row + 32].reshape(256, 256)
        back = lax.dot_general(g, w, (((1,), (1,)), ((), ())), preferred_element_type=F32)
        x = tokens[:, pl.ds(start, 256)].astype(F32)
        token_grad[:, pl.ds(start, 256)] = (root * (back - x * slopes)).astype(BF16)


def final(core, tokens, cot, inv, w_mine, w_theirs):
    vmem = pl.BlockSpec(memory_space=pltpu.VMEM)
    return pl.pallas_call(
        final_kernel,
        in_specs=[pl.BlockSpec(memory_space=pltpu.SMEM)] + [vmem] * 5,
        out_specs=[vmem, vmem],
        out_shape=[
            jax.ShapeDtypeStruct(cot.shape, BF16),
            jax.ShapeDtypeStruct(tokens.shape, BF16),
        ],
        compiler_params=pltpu.CompilerParams(vmem_limit_bytes=14 << 20),
        cost_estimate=pl.CostEstimate(flops=4 * tokens.size * 256, bytes_accessed=8 << 20, transcendentals=0),
    )(core, tokens, cot, inv, w_mine, w_theirs)


SWAP = [(0, 1), (1, 0)]


def cubes():
    index = np.arange(math.prod(SIZES)).reshape(SIZES)
    groups = []
    for core in range(2):
        for x0, y0, z0 in itertools.product(range(core, 4, 2), range(core, 8, 2), range(core, 8, 2)):
            members = {}
            for a, b, c in itertools.product(range(2), repeat=3):
                x, y, z = (x0 + a) % 4, (y0 + b) % 8, (z0 + c) % 8
                members[x % 2, y % 2, z % 2] = int(index[x // 2, y // 2, y % 2, core, z // 2, z % 2, x % 2])
            groups.append([members[k] for k in sorted(members)])
    return groups


def body(tokens, cotangent, kv_weight, norm_gain):
    factor = 1.0 / 256.0
    core = lax.axis_index("c").astype(jnp.int32).reshape(1)
    xl, zl = lax.axis_index("xl"), lax.axis_index("zl")
    piece = 4 * lax.axis_index("zh") + 2 * zl + xl

    got = lax.ppermute(tokens, "c", SWAP)
    scaled, inv = prep(tokens, cotangent)
    got_scaled = lax.ppermute(scaled, "c", SWAP)

    scaled_weight = (kv_weight.astype(F32) * norm_gain.astype(F32)[:, None]).astype(BF16).reshape(2, 2, 2, 32, 256)
    share = lax.dynamic_slice(scaled_weight, (xl, 0, zl, 0, 0), (1, 2, 1, 32, 256)).reshape(2, 32, 256)
    share = jnp.broadcast_to(share, (8, 2, 32, 256)).reshape(16, 32, 256)
    share = lax.all_to_all(share, ("xh", "yh", "yl"), 0, 0, tiled=True).reshape(512, 256)

    both = merge(core, tokens, got, scaled, got_scaled, share)
    both = lax.all_to_all(both, AXES, 0, 0, tiled=True, axis_index_groups=cubes())
    u = jnp.sum(both[:, :512], 0, dtype=F32).astype(BF16).reshape(32, 16, 256)
    w_mine = both[:, 512:]
    w_theirs = lax.ppermute(w_mine, "c", SWAP)

    u = lax.all_to_all(u, ("xh", "yh", "zh"), 0, 0, tiled=True)
    kv_out, token_grad = final(core, tokens, cotangent, inv, w_mine, w_theirs)
    u, kv_out = lax.optimization_barrier((u, kv_out))
    u = jnp.sum(u, 0, dtype=F32) * factor
    gain = lax.dynamic_slice_in_dim(norm_gain, 16 * piece, 16, 0).astype(F32)
    kv_grad = (u * gain[:, None]).astype(BF16)
    rows = lax.dynamic_slice_in_dim(kv_weight, 16 * piece, 16, 0).astype(F32)
    gain_grad = jnp.sum(u * rows, -1).astype(BF16)

    return (kv_out, token_grad, kv_grad, gain_grad)


def solution(mesh):
    split = Mesh(mesh.devices.reshape(SIZES), AXES)
    every, inner = P(AXES, None), ("xh", "yh", "yl", "c")
    return jax.shard_map(
        body,
        mesh=split,
        in_specs=(every, every, P(inner, None), P(inner)),
        out_specs=(every, every, every, P(AXES)),
        check_vma=False,
    )
```

time: 116 us -> 98.9 us (0.85)
  the two profiles are of different devices: /device:TPU:6 before, /device:TPU:1 now
where the time goes in v4:
time: 98.9 us; the launch traced here: 98.3 us
  blocking collectives  42.7 us (43%)
  starting transfers between devices  22 us (22%)
  waiting for transfers between devices  14.1 us (14%)
  Pallas kernels  9.41 us (10%)
  other arithmetic  6.15 us (6%)
  local copies, waits for them, and re-layouts  3.18 us (3%)
    all_to_all x1, blocking collectives, body(): lax.all_to_all(both, AXES, 0, 0, tiled=True, axis_index_groups=cubes())  42.7 us
    all_to_all x1, waiting for transfers between devices, body(): u = lax.all_to_all(u, ('xh', 'yh', 'zh'), 0, 0, tiled=True)  9.09 us
    ppermute x1, starting transfers between devices, body(): got = lax.ppermute(tokens, 'c', SWAP)  8.79 us
    pallas_call x1, Pallas kernels, final(): pl.pallas_call(final_kernel, in_specs=[pl.BlockSpec(memory_space=pltpu.SM...  6.02 us
    all_to_all x1, starting transfers between devices, body(): u = lax.all_to_all(u, ('xh', 'yh', 'zh'), 0, 0, tiled=True)  5.09 us
    all_to_all x1, waiting for transfers between devices, body(): lax.all_to_all(share, ('xh', 'yh', 'yl'), 0, 0, tiled=True)  4.08 us
    all_to_all x1, starting transfers between devices, body(): lax.all_to_all(share, ('xh', 'yh', 'yl'), 0, 0, tiled=True)  4.01 us
    pallas_call x1, Pallas kernels, merge(): pl.pallas_call(merge_kernel, in_specs=[pl.BlockSpec(memory_space=pltpu.SM...  2.54 us
  transfers between devices with their start and end apart: 5, of which 3 were waited for; matrix products, arithmetic and copies ran while one was open for 3% of the time, Pallas kernels for 7%

profile of v4, /device:TPU:1, one launch (start us, length us, event | category | flops | bytes accessed | tf_op | source)
XLA Modules:
  0.0 98.3 jit_solution(11287481664902957078)
XLA Ops:
  0.6 8.8 %collective-permute-start = (bf16[128,8192]{1,0:T(8,128)(2,1)}, bf16[128,8192]{1,0:T(8,128)(2,1)}, u32[]{:S(2)}, u32[]{:S(2)}) collective-permute-start(bf16[128,8192]{1,0:T(8,128)(2,1)} %tokens.5), channel_id=1, source_target_pairs={{0,16},{16,0},{1,17},{17,1},{2,18},{18,2},{3,19},{19,3},{4,20},{20... | collective-permute-start | bytes 6291464 | tf_op jit(solution)/shard_map/ppermute | solution.py:137
  9.4 0.7 convert_element_type.27
  10.1 1.0 %multiply_convert_fusion = bf16[256,256]{1,0:T(8,128)(2,1)S(1)} fusion(bf16[256,256]{1,0:T(8,128)(2,1)} %param.6, f32[256]{0:T(256)S(1)} %convert_element_type.27), kind=kLoop, calls=%fused_computation.2 | loop fusion | flops 196608 | bytes 263168 | tf_op jit(solution)/shard_map/convert_element_type | solution.py:141
  11.1 0.7 broadcast_in_dim.2
  11.9 4.0 %all-to-all-start = ((bf16[16,32,256]{2,1,0:T(8,128)(2,1)}), bf16[16,32,256]{2,1,0:T(8,128)(2,1)S(1)}, u32[]{:S(2)}, u32[]{:S(2)}) async-start(bf16[16,32,256]{2,1,0:T(8,128)(2,1)} %bitcast.3), calls=%async_computation | async-start | bytes 524288 | tf_op jit(solution)/shard_map/all_to_all | solution.py:144
  15.9 0.0 copy-start
  15.9 1.6 %copy-done = bf16[128,8192]{1,0:T(8,128)(2,1)S(1)} copy-done((bf16[128,8192]{1,0:T(8,128)(2,1)S(1)}, bf16[128,8192]{1,0:T(8,128)(2,1)}, u32[]{:S(2)}) %copy-start) | copy-done | bytes 2097176
  17.5 0.0 copy-start.2
  17.5 0.8 copy-done.2
  18.3 0.0 copy-start.1
  18.3 0.9 shard_map.75
  19.2 2.2 %collective-permute-start.1 = (bf16[128,256]{1,0:T(8,128)(2,1)S(1)}, bf16[128,256]{1,0:T(8,128)(2,1)S(1)}, u32[]{:S(2)}, u32[]{:S(2)}) collective-permute-start(bf16[128,256]{1,0:T(8,128)(2,1)S(1)} %get-tuple-element.10.mine), channel_id=1, source_target_pairs={{0,16},{16,0},{1,17},{17,1},{2,18},{18,2},{3,19},{19,3},{4,20},{20... | collective-permute-start | bytes 196616 | tf_op jit(solution)/shard_map/ppermute | solution.py:139
  21.4 0.9 collective-permute-done.1.theirs
  22.3 4.1 %all-to-all-done = bf16[16,32,256]{2,1,0:T(8,128)(2,1)S(1)} async-done(((bf16[16,32,256]{2,1,0:T(8,128)(2,1)}), bf16[16,32,256]{2,1,0:T(8,128)(2,1)S(1)}, u32[]{:S(2)}, u32[]{:S(2)}) %all-to-all-start) | async-done | bytes 262176 | tf_op jit(solution)/shard_map/all_to_all | solution.py:144
  26.4 0.0 collective-permute-done.got
  26.4 0.0 copy-done.1
  26.4 2.5 %shard_map.76 = bf16[8,1024,256]{2,1,0:T(8,128)(2,1)S(1)} custom-call(s32[1]{0:T(128)} %bitcast.core, bf16[128,8192]{1,0:T(8,128)(2,1)S(1)} %copy-done.1, bf16[128,8192]{1,0:T(8,128)(2,1)} %collective-permute-done.got, bf16[128,256]{1,0:T(8,128)(2,1)S(1)} %get-tuple-element.10.mine, bf16[128,256]{1,0:T(8,128)(2,1)S(1)} %collective-permute-done.1.theirs, ...), custom_call_target="tpu_custom_call" | custom-call | flops 536870912 | bytes 8388608 | tf_op jit(solution)/shard_map/pallas_call | solution.py:67
  29.0 42.7 %all_to_all.15 = bf16[8,1024,256]{2,1,0:T(8,128)(2,1)S(1)} all-to-all(bf16[8,1024,256]{2,1,0:T(8,128)(2,1)S(1)} %shard_map.76), channel_id=1, replica_groups={{0,2,32,34,1,3,33,35},{4,6,36,38,5,7,37,39},{8,10,40,42,9,11,41,43},{12..., dimensions={0} | all-to-all | bytes 8388608 | tf_op jit(solution)/shard_map/all_to_all | solution.py:147
  71.6 0.0 copy-start.4
  71.7 0.0 copy-start.3
  71.7 2.4 %fusion = (bf16[8,512,256]{2,1,0:T(8,128)(2,1)}, bf16[512,256]{1,0:T(8,128)(2,1)}) fusion(bf16[8,1024,256]{2,1,0:T(8,128)(2,1)S(1)} %all_to_all.15), kind=kLoop, calls=%fused_computation.7 | loop fusion | flops 917504 | bytes 6553600 | tf_op jit(solution)/shard_map/slice | solution.py:149
  74.0 1.9 %collective-permute-start.2 = (bf16[8,512,256]{2,1,0:T(8,128)(2,1)}, bf16[8,512,256]{2,1,0:T(8,128)(2,1)}, u32[]{:S(2)}, u32[]{:S(2)}) collective-permute-start(bf16[8,512,256]{2,1,0:T(8,128)(2,1)} %get-tuple-element.16.w_mine), channel_id=1, source_target_pairs={{0,16},{16,0},{1,17},{17,1},{2,18},{18,2},{3,19},{19,3},{4,20},{20... | collective-permute-start | bytes 6291464 | tf_op jit(solution)/shard_map/ppermute | solution.py:150
  75.9 5.1 %all-to-all-start.2 = ((bf16[32,16,256]{2,1,0:T(8,128)(2,1)}), bf16[32,16,256]{2,1,0:T(8,128)(2,1)S(1)}, u32[]{:S(2)}, u32[]{:S(2)}) async-start(bf16[32,16,256]{2,1,0:T(8,128)(2,1)} %bitcast.5), calls=%async_computation.2 | async-start | bytes 524288 | tf_op jit(solution)/shard_map/all_to_all | solution.py:152
  81.0 0.0 copy-done.4
  81.1 0.1 convert_multiply_fusion
  81.1 0.0 collective-permute-done.2.w_theirs
  81.1 0.0 copy-done.3
  81.1 6.0 %shard_map.77 = (bf16[128,256]{1,0:T(8,128)(2,1)}, bf16[128,8192]{1,0:T(8,128)(2,1)}) custom-call(s32[1]{0:T(128)} %bitcast.core, bf16[128,8192]{1,0:T(8,128)(2,1)S(1)} %copy-done.1, bf16[128,256]{1,0:T(8,128)(2,1)S(1)} %copy-done.3, f32[128,128]{1,0:T(8,128)S(1)} %get-tuple-element.11.inv, bf16[8,512,256]{2,1,0:T(8,128)(2,1)} %get-tuple-element.16.w_mine, ...), custom_call_target="tpu_custom_call" | custom-call | flops 1073741824 | bytes 8388608 | tf_op jit(solution)/shard_map/pallas_call | solution.py:102
  87.2 9.1 %all-to-all-done.2 = bf16[32,16,256]{2,1,0:T(8,128)(2,1)S(1)} async-done(((bf16[32,16,256]{2,1,0:T(8,128)(2,1)}), bf16[32,16,256]{2,1,0:T(8,128)(2,1)S(1)}, u32[]{:S(2)}, u32[]{:S(2)}) %all-to-all-start.2) | async-done | bytes 262176 | tf_op jit(solution)/shard_map/all_to_all | solution.py:152
  96.3 2.0 %multiply_reduce_fusion = (bf16[16]{0:T(256)(128)(2,1)}, bf16[16,256]{1,0:T(8,128)(2,1)}) fusion(f32[16,256]{1,0:T(8,128)S(1)} %convert_reduce_fusion, bf16[256,256]{1,0:T(8,128)(2,1)} %param.6, s32[]{:T(128)S(6)} %select_n.12, f32[16]{0:T(128)S(1)} %convert_multiply_fusion), kind=kLoop, calls=%fused_computation.4 | loop fusion | flops 24560 | bytes 32868 | tf_op jit(solution)/shard_map/reduce_sum | solution.py:159
  (2 shorter events, 0.1 us)
Async XLA Ops:
  0.6 25.8 %collective-permute-start = (bf16[128,8192]{1,0:T(8,128)(2,1)}, bf16[128,8192]{1,0:T(8,128)(2,1)}, u32[]{:S(2)}, u32[]{:S(2)}) collective-permute-start(bf16[128,8192]{1,0:T(8,128)(2,1)} %tokens.5), channel_id=1, source_target_pairs={{0,16},{16,0},{1,17},{17,1},{2,18},{18,2},{3,19},{19,3},{4,20},{20... | collective-permute-start | bytes 6291464 | tf_op jit(solution)/shard_map/ppermute | solution.py:137
  11.9 14.6 %all-to-all-start = ((bf16[16,32,256]{2,1,0:T(8,128)(2,1)}), bf16[16,32,256]{2,1,0:T(8,128)(2,1)S(1)}, u32[]{:S(2)}, u32[]{:S(2)}) async-start(bf16[16,32,256]{2,1,0:T(8,128)(2,1)} %bitcast.3), calls=%async_computation | async-start | bytes 524288 | tf_op jit(solution)/shard_map/all_to_all | solution.py:144
  15.9 1.6 %copy-start = (bf16[128,8192]{1,0:T(8,128)(2,1)S(1)}, bf16[128,8192]{1,0:T(8,128)(2,1)}, u32[]{:S(2)}) copy-start(bf16[128,8192]{1,0:T(8,128)(2,1)} %tokens.5) | copy-start | bytes 6291460
  17.5 0.8 copy-start.2
  18.3 8.1 %copy-start.1 = (bf16[128,8192]{1,0:T(8,128)(2,1)S(1)}, bf16[128,8192]{1,0:T(8,128)(2,1)}, u32[]{:S(2)}) copy-start(bf16[128,8192]{1,0:T(8,128)(2,1)} %tokens.5) | copy-start | bytes 6291460
  19.2 3.2 %collective-permute-start.1 = (bf16[128,256]{1,0:T(8,128)(2,1)S(1)}, bf16[128,256]{1,0:T(8,128)(2,1)S(1)}, u32[]{:S(2)}, u32[]{:S(2)}) collective-permute-start(bf16[128,256]{1,0:T(8,128)(2,1)S(1)} %get-tuple-element.10.mine), channel_id=1, source_target_pairs={{0,16},{16,0},{1,17},{17,1},{2,18},{18,2},{3,19},{19,3},{4,20},{20... | collective-permute-start | bytes 196616 | tf_op jit(solution)/shard_map/ppermute | solution.py:139
  71.6 9.4 %copy-start.4 = (bf16[256]{0:T(256)(128)(2,1)S(1)}, bf16[256]{0:T(256)(128)(2,1)}, u32[]{:S(2)}) copy-start(bf16[256]{0:T(256)(128)(2,1)} %param.7) | copy-start | bytes 1540
  71.7 9.5 %copy-start.3 = (bf16[128,256]{1,0:T(8,128)(2,1)S(1)}, bf16[128,256]{1,0:T(8,128)(2,1)}, u32[]{:S(2)}) copy-start(bf16[128,256]{1,0:T(8,128)(2,1)} %cot.3) | copy-start | bytes 196612
  74.0 7.1 %collective-permute-start.2 = (bf16[8,512,256]{2,1,0:T(8,128)(2,1)}, bf16[8,512,256]{2,1,0:T(8,128)(2,1)}, u32[]{:S(2)}, u32[]{:S(2)}) collective-permute-start(bf16[8,512,256]{2,1,0:T(8,128)(2,1)} %get-tuple-element.16.w_mine), channel_id=1, source_target_pairs={{0,16},{16,0},{1,17},{17,1},{2,18},{18,2},{3,19},{19,3},{4,20},{20... | collective-permute-start | bytes 6291464 | tf_op jit(solution)/shard_map/ppermute | solution.py:150
  75.9 20.3 %all-to-all-start.2 = ((bf16[32,16,256]{2,1,0:T(8,128)(2,1)}), bf16[32,16,256]{2,1,0:T(8,128)(2,1)S(1)}, u32[]{:S(2)}, u32[]{:S(2)}) async-start(bf16[32,16,256]{2,1,0:T(8,128)(2,1)} %bitcast.5), calls=%async_computation.2 | async-start | bytes 524288 | tf_op jit(solution)/shard_map/all_to_all | solution.py:152

commit v5 on v4

v5 whole, which is shorter than its diff:
```python
import itertools
import math

import jax
import jax.numpy as jnp
import numpy as np
from jax import lax
from jax.experimental import pallas as pl
from jax.experimental.pallas import tpu as pltpu
from jax.sharding import Mesh, PartitionSpec as P

AXES = ("xh", "yh", "yl", "c", "zh", "zl", "xl")
SIZES = (2, 4, 2, 2, 4, 2, 2)
F32, BF16 = jnp.float32, jnp.bfloat16


def prep_kernel(tokens, cot, scaled, inv):
    wide = tokens[...].astype(F32)
    root = lax.rsqrt(jnp.mean(wide * wide, -1, keepdims=True) + 1e-05)
    inv[...] = jnp.broadcast_to(root, inv.shape)
    scaled[...] = (cot[...].astype(F32) * root).astype(BF16)


def prep(tokens, cot):
    rows, width = tokens.shape
    steps = 4
    return pl.pallas_call(
        prep_kernel,
        grid=(steps,),
        in_specs=[
            pl.BlockSpec((rows // steps, width), lambda i: (i, 0)),
            pl.BlockSpec((rows // steps, 256), lambda i: (i, 0)),
        ],
        out_specs=[
            pl.BlockSpec((rows // steps, 256), lambda i: (i, 0)),
            pl.BlockSpec((rows // steps, 128), lambda i: (i, 0)),
        ],
        out_shape=[
            jax.ShapeDtypeStruct(cot.shape, BF16),
            jax.ShapeDtypeStruct((rows, 128), F32),
        ],
        compiler_params=pltpu.CompilerParams(vmem_limit_bytes=8 << 20),
        cost_estimate=pl.CostEstimate(flops=2 * rows * width, bytes_accessed=2 * rows * width, transcendentals=0),
    )(tokens, cot)


def share_kernel(place, weight, gain, out, scaled):
    xl, zl = place[1], place[2]
    row = lax.broadcasted_iota(jnp.int32, (256, 256), 0)
    column = lax.broadcasted_iota(jnp.int32, (256, 256), 1)
    diagonal = jnp.where(row == column, gain[...].astype(F32), 0.0).astype(BF16)
    scaled[...] = jnp.dot(diagonal, weight[...], preferred_element_type=F32).astype(BF16)
    for yl in range(2):
        rows = scaled[pl.ds(pl.multiple_of(128 * xl + 64 * yl + 32 * zl, 32), 32), :]
        for k in range(8):
            out[2 * k + yl] = rows


def make_share(place, weight, gain):
    vmem = pl.BlockSpec(memory_space=pltpu.VMEM)
    return pl.pallas_call(
        share_kernel,
        in_specs=[pl.BlockSpec(memory_space=pltpu.SMEM), vmem, vmem],
        out_specs=vmem,
        out_shape=jax.ShapeDtypeStruct((16, 32, 256), BF16),
        scratch_shapes=[pltpu.VMEM((256, 256), BF16)],
        compiler_params=pltpu.CompilerParams(vmem_limit_bytes=4 << 20),
        cost_estimate=pl.CostEstimate(flops=1 << 25, bytes_accessed=1 << 19, transcendentals=0),
    )(place, weight, gain)


def merge_kernel(place, tokens, got, mine, theirs, weights, out):
    right = jnp.concatenate([mine[...], theirs[...]], 0)
    for xh in range(2):
        for yh in range(4):
            for yl in range(2):
                block = 8 * xh + 2 * yh + yl
                start = pl.multiple_of(512 * block + 256 * place[0], 256)
                left = jnp.concatenate([tokens[:, pl.ds(start, 256)], got[:, pl.ds(start, 256)]], 0)
                u = lax.dot_general(left, right, (((0,), (0,)), ((), ())), preferred_element_type=F32)
                u = u.reshape(4, 2, 2, 16, 256).astype(BF16)
                first = 64 * (4 * xh + yh)
                for xl in range(2):
                    for zl in range(2):
                        out[4 * xl + 2 * yl + zl, first : first + 64] = u[:, zl, xl].reshape(64, 256)
    for k in range(8):
        first = 256 * (k // 4)
        out[k, 512:] = weights[first : first + 256]


def merge(place, tokens, got, mine, theirs, weights):
    vmem = pl.BlockSpec(memory_space=pltpu.VMEM)
    return pl.pallas_call(
        merge_kernel,
        in_specs=[pl.BlockSpec(memory_space=pltpu.SMEM)] + [vmem] * 5,
        out_specs=vmem,
        out_shape=jax.ShapeDtypeStruct((8, 768, 256), BF16),
        compiler_params=pltpu.CompilerParams(vmem_limit_bytes=12 << 20),
        cost_estimate=pl.CostEstimate(flops=2 * tokens.size * 256, bytes_accessed=8 * tokens.size, transcendentals=0),
    )(place, tokens, got, mine, theirs, weights)


def split_kernel(both, u, weights):
    total = both[0, :512].astype(F32)
    for k in range(1, 8):
        total += both[k, :512].astype(F32)
    u[...] = total.astype(BF16)
    for k in range(8):
        weights[k] = both[k, 512:]


def split_sum(both):
    vmem = pl.BlockSpec(memory_space=pltpu.VMEM)
    return pl.pallas_call(
        split_kernel,
        in_specs=[vmem],
        out_specs=[vmem, vmem],
        out_shape=[jax.ShapeDtypeStruct((512, 256), BF16), jax.ShapeDtypeStruct((8, 256, 256), BF16)],
        compiler_params=pltpu.CompilerParams(vmem_limit_bytes=8 << 20),
        cost_estimate=pl.CostEstimate(flops=1 << 20, bytes_accessed=5 << 20, transcendentals=0),
    )(both)


def weight_pieces(place, half, refs):
    pieces = []
    for block in range(8):
        for ref, side in zip(refs, (place[0], 1 - place[0])):
            start = pl.multiple_of(512 * (8 * half + block) + 256 * side, 256)
            pieces.append((ref, 32 * block, start))
    return pieces


def project(tokens, pieces, total):
    for ref, row, start in pieces:
        w = ref[:, row : row + 32].reshape(256, 256)
        total += jnp.dot(tokens[:, pl.ds(start, 256)], w, preferred_element_type=F32)
    return total


def first_kernel(place, tokens, w0, w1, out):
    out[...] = project(tokens, weight_pieces(place, place[1], (w0, w1)), jnp.zeros(out.shape, F32))


def first_half(place, tokens, weights):
    vmem = pl.BlockSpec(memory_space=pltpu.VMEM)
    return pl.pallas_call(
        first_kernel,
        in_specs=[pl.BlockSpec(memory_space=pltpu.SMEM)] + [vmem] * 3,
        out_specs=vmem,
        out_shape=jax.ShapeDtypeStruct((tokens.shape[0], 256), F32),
        compiler_params=pltpu.CompilerParams(vmem_limit_bytes=8 << 20),
        cost_estimate=pl.CostEstimate(flops=1 << 20, bytes_accessed=1 << 10, transcendentals=0),
    )(place, tokens, *weights)


def final_kernel(place, tokens, cot, inv, kv_half, w0, w1, w2, w3, kv_out, token_grad):
    width = tokens.shape[1]
    later = weight_pieces(place, 1 - place[1], (w2, w3))
    root = inv[:, :1]
    kv = project(tokens, later, kv_half[...]) * root
    kv_out[...] = kv.astype(BF16)
    g = cot[...]
    slopes = jnp.sum(g.astype(F32) * kv, -1, keepdims=True) * (1.0 / width)
    slopes = root * slopes
    for ref, row, start in weight_pieces(place, place[1], (w0, w1)) + later:
        w = ref[:, row : row + 32].reshape(256, 256)
        back = lax.dot_general(g, w, (((1,), (1,)), ((), ())), preferred_element_type=F32)
        x = tokens[:, pl.ds(start, 256)].astype(F32)
        token_grad[:, pl.ds(start, 256)] = (root * (back - x * slopes)).astype(BF16)


def final(place, tokens, cot, inv, kv_half, weights):
    vmem = pl.BlockSpec(memory_space=pltpu.VMEM)
    return pl.pallas_call(
        final_kernel,
        in_specs=[pl.BlockSpec(memory_space=pltpu.SMEM)] + [vmem] * 8,
        out_specs=[vmem, vmem],
        out_shape=[
            jax.ShapeDtypeStruct(cot.shape, BF16),
            jax.ShapeDtypeStruct(tokens.shape, BF16),
        ],
        compiler_params=pltpu.CompilerParams(vmem_limit_bytes=14 << 20),
        cost_estimate=pl.CostEstimate(flops=1 << 20, bytes_accessed=1 << 10, transcendentals=0),
    )(place, tokens, cot, inv, kv_half, *weights)


def total_kernel(parts, out):
    total = parts[0].astype(F32)
    for k in range(1, parts.shape[0]):
        total += parts[k].astype(F32)
    out[...] = total * (1.0 / 256.0)


def total_of(parts):
    vmem = pl.BlockSpec(memory_space=pltpu.VMEM)
    return pl.pallas_call(
        total_kernel,
        in_specs=[vmem],
        out_specs=vmem,
        out_shape=jax.ShapeDtypeStruct(parts.shape[1:], F32),
        compiler_params=pltpu.CompilerParams(vmem_limit_bytes=2 << 20),
        cost_estimate=pl.CostEstimate(flops=50 * 10**9, bytes_accessed=1 << 18, transcendentals=0),
    )(parts)


SWAP = [(0, 1), (1, 0)]


def cubes():
    index = np.arange(math.prod(SIZES)).reshape(SIZES)
    groups = []
    for core in range(2):
        for x0, y0, z0 in itertools.product(range(core, 4, 2), range(core, 8, 2), range(core, 8, 2)):
            members = {}
            for a, b, c in itertools.product(range(2), repeat=3):
                x, y, z = (x0 + a) % 4, (y0 + b) % 8, (z0 + c) % 8
                members[x % 2, y % 2, z % 2] = int(index[x // 2, y // 2, y % 2, core, z // 2, z % 2, x % 2])
            groups.append([members[k] for k in sorted(members)])
    return groups


ALONG_X = [
    (4 * (x // 2) + 2 * c + x % 2, 4 * ((x ^ (1 + 2 * c)) // 2) + 2 * c + 1 - x % 2)
    for c in range(2)
    for x in range(4)
]


def body(tokens, cotangent, kv_weight, norm_gain):
    xl, zl = lax.axis_index("xl"), lax.axis_index("zl")
    place = jnp.stack([lax.axis_index("c"), xl, zl]).astype(jnp.int32)
    piece = 4 * lax.axis_index("zh") + 2 * zl + xl

    share = make_share(place, kv_weight, norm_gain.reshape(1, 256))
    share = lax.all_to_all(share, ("xh", "yh", "yl"), 0, 0, tiled=True).reshape(512, 256)

    got = lax.ppermute(tokens, "c", SWAP)
    scaled, inv = prep(tokens, cotangent)
    got_scaled = lax.ppermute(scaled, "c", SWAP)

    both = merge(place, tokens, got, scaled, got_scaled, share)
    both = lax.all_to_all(both, AXES, 0, 0, tiled=True, axis_index_groups=cubes())
    u, w0 = split_sum(both)

    w2 = lax.ppermute(w0, ("xh", "c", "xl"), ALONG_X)
    w1 = lax.ppermute(w0, "c", SWAP)
    kv_half = first_half(place, tokens, (w0, w1))
    w2, kv_half = lax.optimization_barrier((w2, kv_half))
    w3 = lax.ppermute(w2, "c", SWAP)

    u = lax.all_to_all(u.reshape(32, 16, 256), ("xh", "yh", "zh"), 0, 0, tiled=True)
    u, w3 = lax.optimization_barrier((total_of(u), w3))
    kv_out, token_grad = final(place, tokens, cotangent, inv, kv_half, (w0, w1, w2, w3))
    gain = lax.dynamic_slice_in_dim(norm_gain, 16 * piece, 16, 0).astype(F32)[:, None]
    rows = lax.dynamic_slice_in_dim(kv_weight, 16 * piece, 16, 0).astype(F32)
    kv_grad = (u * gain).astype(BF16)
    gain_grad = jnp.sum(u * rows, -1).astype(BF16)
    return (kv_out, token_grad, kv_grad, gain_grad)


def solution(mesh):
    split = Mesh(mesh.devices.reshape(SIZES), AXES)
    every, inner = P(AXES, None), ("xh", "yh", "yl", "c")
    return jax.shard_map(
        body,
        mesh=split,
        in_specs=(every, every, P(inner, None), P(inner)),
        out_specs=(every, every, every, P(AXES)),
        check_vma=False,
    )
```

time: 98.9 us -> 101 us (1.021)
  blocking collectives: 42.7 us -> 37.1 us
  starting transfers between devices: 22 us -> 26.7 us
  other arithmetic: 6.15 us -> 2.14 us
  Pallas kernels: 9.41 us -> 12.7 us
  waiting for transfers between devices: 14.1 us -> 15.9 us
  local copies, waits for them, and re-layouts: 3.18 us -> 4.65 us
    ppermute x1 -> x3, waiting for transfers between devices: 0.01 us -> 9.63 us  [the longest x1 8.92 us: body(): w2 = lax.ppermute(w0, ('xh', 'c', 'xl'), ALONG_X)]
    all_to_all x1, waiting for transfers between devices: 9.09 us -> 1.84 us  [body(): lax.all_to_all(u.reshape(32, 16, 256), ('xh', 'yh', 'zh'), 0, 0, tiled=True)]
    all_to_all x1, blocking collectives: 42.7 us -> 37.1 us  [body(): lax.all_to_all(both, AXES, 0, 0, tiled=True, axis_index_groups=cubes())]
    ppermute x1 -> x3, starting transfers between devices: 1.91 us -> 6.6 us  [the longest x1 2.5 us: body(): w3 = lax.ppermute(w2, 'c', SWAP)]
    pallas_call x0 -> x4, Pallas kernels: none -> 4.18 us  [the longest x1 1.69 us: first_half(): pl.pallas_call(first_kernel, in_specs=[pl.BlockSpec(memory_space=pltpu.SM...]
    slice x1 -> x0, other arithmetic: 2.37 us -> none  [body(): w_mine = both[:, 512:]]
    convert_element_type x2 -> x1, other arithmetic: 1.66 us -> 0.08 us  [body(): lax.dynamic_slice_in_dim(norm_gain, 16 * piece, 16, 0).astype(F32)[:, None]]
    unnamed x10 -> x16, local copies, waits for them, and re-layouts: 2.44 us -> 3.99 us
  transfers between devices with their start and end apart: 5 -> 7, of which waited for: 3 -> 5; matrix products, arithmetic and copies ran while one was open for 3% -> 1% of each run, Pallas kernels for 7% -> 4%
where the time goes in v5:
time: 101 us; the launch traced here: 99.9 us
  blocking collectives  37.1 us (37%)
  starting transfers between devices  26.7 us (26%)
  waiting for transfers between devices  15.9 us (16%)
  Pallas kernels  12.7 us (13%)
  local copies, waits for them, and re-layouts  4.65 us (5%)
  other arithmetic  2.14 us (2%)
    all_to_all x1, blocking collectives, body(): lax.all_to_all(both, AXES, 0, 0, tiled=True, axis_index_groups=cubes())  37.1 us
    ppermute x1, waiting for transfers between devices, body(): w2 = lax.ppermute(w0, ('xh', 'c', 'xl'), ALONG_X)  8.92 us
    ppermute x1, starting transfers between devices, body(): got = lax.ppermute(tokens, 'c', SWAP)  8.79 us
    pallas_call x1, Pallas kernels, final(): pl.pallas_call(final_kernel, in_specs=[pl.BlockSpec(memory_space=pltpu.SM...  5.23 us
    all_to_all x1, starting transfers between devices, body(): lax.all_to_all(u.reshape(32, 16, 256), ('xh', 'yh', 'zh'), 0, 0, tiled=True)  5.15 us
    all_to_all x1, starting transfers between devices, body(): lax.all_to_all(share, ('xh', 'yh', 'yl'), 0, 0, tiled=True)  4.01 us
    unnamed x16, local copies, waits for them, and re-layouts  3.99 us
    all_to_all x1, waiting for transfers between devices, body(): lax.all_to_all(share, ('xh', 'yh', 'yl'), 0, 0, tiled=True)  3.45 us
  transfers between devices with their start and end apart: 7, of which 5 were waited for; matrix products, arithmetic and copies ran while one was open for 1% of the time, Pallas kernels for 4%

profile of v5, /device:TPU:1, one launch (start us, length us, event | category | flops | bytes accessed | tf_op | source)
XLA Modules:
  0.0 99.9 jit_solution(12212199727988552173)
XLA Ops:
  0.6 8.8 %collective-permute-start = (bf16[128,8192]{1,0:T(8,128)(2,1)}, bf16[128,8192]{1,0:T(8,128)(2,1)}, u32[]{:S(2)}, u32[]{:S(2)}) collective-permute-start(bf16[128,8192]{1,0:T(8,128)(2,1)} %tokens.7), channel_id=1, source_target_pairs={{0,16},{16,0},{1,17},{17,1},{2,18},{18,2},{3,19},{19,3},{4,20},{20... | collective-permute-start | bytes 6291464 | tf_op jit(solution)/shard_map/ppermute | solution.py:237
  9.4 0.7 reshape.18.gain
  10.1 0.1 pad_add_fusion.place
  10.2 0.9 copy-done.4
  11.1 1.4 %shard_map.76 = bf16[16,32,256]{2,1,0:T(8,128)(2,1)} custom-call(s32[3]{0:T(128)S(1)} %pad_add_fusion.place, bf16[256,256]{1,0:T(8,128)(2,1)S(1)} %copy-done.4, bf16[1,256]{1,0:T(2,128)(2,1)S(1)} %reshape.18.gain), custom_call_target="tpu_custom_call" | custom-call | flops 33554432 | bytes 524288 | tf_op jit(solution)/shard_map/pallas_call | solution.py:61
  12.5 4.0 %all-to-all-start = ((bf16[16,32,256]{2,1,0:T(8,128)(2,1)}), bf16[16,32,256]{2,1,0:T(8,128)(2,1)S(1)}, u32[]{:S(2)}, u32[]{:S(2)}) async-start(bf16[16,32,256]{2,1,0:T(8,128)(2,1)} %shard_map.76), calls=%async_computation | async-start | bytes 524288 | tf_op jit(solution)/shard_map/all_to_all | solution.py:235
  16.5 0.0 copy-start
  16.6 1.6 %copy-done = bf16[128,8192]{1,0:T(8,128)(2,1)S(1)} copy-done((bf16[128,8192]{1,0:T(8,128)(2,1)S(1)}, bf16[128,8192]{1,0:T(8,128)(2,1)}, u32[]{:S(2)}) %copy-start) | copy-done | bytes 2097176
  18.1 0.8 copy-done.2
  19.0 0.9 shard_map.75
  19.8 0.0 copy-start.5
  19.9 0.6 copy-done.5
  20.5 2.2 %collective-permute-start.1 = (bf16[128,256]{1,0:T(8,128)(2,1)S(1)}, bf16[128,256]{1,0:T(8,128)(2,1)S(1)}, u32[]{:S(2)}, u32[]{:S(2)}) collective-permute-start(bf16[128,256]{1,0:T(8,128)(2,1)S(1)} %get-tuple-element.15.mine), channel_id=1, source_target_pairs={{0,16},{16,0},{1,17},{17,1},{2,18},{18,2},{3,19},{19,3},{4,20},{20... | collective-permute-start | bytes 196616 | tf_op jit(solution)/shard_map/ppermute | solution.py:239
  22.7 0.9 collective-permute-done.1.theirs
  23.6 3.4 %all-to-all-done = bf16[16,32,256]{2,1,0:T(8,128)(2,1)S(1)} async-done(((bf16[16,32,256]{2,1,0:T(8,128)(2,1)}), bf16[16,32,256]{2,1,0:T(8,128)(2,1)S(1)}, u32[]{:S(2)}, u32[]{:S(2)}) %all-to-all-start) | async-done | bytes 262176 | tf_op jit(solution)/shard_map/all_to_all | solution.py:235
  27.1 0.0 collective-permute-done.got
  27.1 2.4 %shard_map.77 = bf16[8,768,256]{2,1,0:T(8,128)(2,1)S(1)} custom-call(s32[3]{0:T(128)S(1)} %pad_add_fusion.place, bf16[128,8192]{1,0:T(8,128)(2,1)S(1)} %copy-done.1, bf16[128,8192]{1,0:T(8,128)(2,1)} %collective-permute-done.got, bf16[128,256]{1,0:T(8,128)(2,1)S(1)} %get-tuple-element.15.mine, bf16[128,256]{1,0:T(8,128)(2,1)S(1)} %collective-permute-done.1.theirs, ...), custom_call_target="tpu_custom_call" | custom-call | flops 536870912 | bytes 8388608 | tf_op jit(solution)/shard_map/pallas_call | solution.py:93
  29.5 37.1 %all_to_all.15.both = bf16[8,768,256]{2,1,0:T(8,128)(2,1)S(1)} all-to-all(bf16[8,768,256]{2,1,0:T(8,128)(2,1)S(1)} %shard_map.77), channel_id=1, replica_groups={{0,2,32,34,1,3,33,35},{4,6,36,38,5,7,37,39},{8,10,40,42,9,11,41,43},{12..., dimensions={0} | all-to-all | bytes 6291456 | tf_op jit(solution)/shard_map/all_to_all | solution.py:242
  66.6 1.0 shard_map.78
  67.6 1.9 %collective-permute-start.3 = (bf16[8,256,256]{2,1,0:T(8,128)(2,1)S(1)}, bf16[8,256,256]{2,1,0:T(8,128)(2,1)}, u32[]{:S(2)}, u32[]{:S(2)}) collective-permute-start(bf16[8,256,256]{2,1,0:T(8,128)(2,1)S(1)} %get-tuple-element.16.w0), channel_id=1, source_target_pairs={{0,16},{16,0},{1,17},{17,1},{2,18},{18,2},{3,19},{19,3},{4,20},{20... | collective-permute-start | bytes 3145736 | tf_op jit(solution)/shard_map/ppermute | solution.py:246
  69.5 2.2 %collective-permute-start.2 = (bf16[8,256,256]{2,1,0:T(8,128)(2,1)S(1)}, bf16[8,256,256]{2,1,0:T(8,128)(2,1)}, u32[]{:S(2)}, u32[]{:S(2)}) collective-permute-start(bf16[8,256,256]{2,1,0:T(8,128)(2,1)S(1)} %get-tuple-element.16.w0), channel_id=1, source_target_pairs={{0,1},{1,0},{256,257},{257,256},{16,273},{17,272},{272,17},{273,16... | collective-permute-start | bytes 3145736 | tf_op jit(solution)/shard_map/ppermute | solution.py:245
  71.7 5.2 %all-to-all-start.2 = ((bf16[32,16,256]{2,1,0:T(8,128)(2,1)}), bf16[32,16,256]{2,1,0:T(8,128)(2,1)S(1)}, u32[]{:S(2)}, u32[]{:S(2)}) async-start(bf16[32,16,256]{2,1,0:T(8,128)(2,1)} %bitcast.4), calls=%async_computation.2 | async-start | bytes 524288 | tf_op jit(solution)/shard_map/all_to_all | solution.py:251
  76.9 0.1 dynamic-slice_convert_fusion
  77.0 0.0 collective-permute-done.3.w1
  77.0 1.7 %shard_map.79.kv_half = f32[128,256]{1,0:T(8,128)S(1)} custom-call(s32[3]{0:T(128)S(1)} %pad_add_fusion.place, bf16[128,8192]{1,0:T(8,128)(2,1)S(1)} %copy-done.1, bf16[8,256,256]{2,1,0:T(8,128)(2,1)S(1)} %get-tuple-element.16.w0, bf16[8,256,256]{2,1,0:T(8,128)(2,1)} %collective-permute-done.3.w1), custom_call_target="tpu_custom_call" | custom-call | flops 1048576 | bytes 1024 | tf_op jit(solution)/shard_map/pallas_call | solution.py:146
  78.7 8.9 %collective-permute-done.2.w2 = bf16[8,256,256]{2,1,0:T(8,128)(2,1)} collective-permute-done((bf16[8,256,256]{2,1,0:T(8,128)(2,1)S(1)}, bf16[8,256,256]{2,1,0:T(8,128)(2,1)}, u32[]{:S(2)}, u32[]{:S(2)}) %collective-permute-start.2) | collective-permute-done | bytes 1048608 | tf_op jit(solution)/shard_map/ppermute | solution.py:245
  87.6 2.5 %collective-permute-start.4 = (bf16[8,256,256]{2,1,0:T(8,128)(2,1)}, bf16[8,256,256]{2,1,0:T(8,128)(2,1)}, u32[]{:S(2)}, u32[]{:S(2)}) collective-permute-start(bf16[8,256,256]{2,1,0:T(8,128)(2,1)} %collective-permute-done.2.w2), channel_id=1, source_target_pairs={{0,16},{16,0},{1,17},{17,1},{2,18},{18,2},{3,19},{19,3},{4,20},{20... | collective-permute-start | bytes 3145736 | tf_op jit(solution)/shard_map/ppermute | solution.py:249
  90.1 1.8 %all-to-all-done.2.parts = bf16[32,16,256]{2,1,0:T(8,128)(2,1)S(1)} async-done(((bf16[32,16,256]{2,1,0:T(8,128)(2,1)}), bf16[32,16,256]{2,1,0:T(8,128)(2,1)S(1)}, u32[]{:S(2)}, u32[]{:S(2)}) %all-to-all-start.2) | async-done | bytes 262176 | tf_op jit(solution)/shard_map/all_to_all | solution.py:251
  92.0 0.7 collective-permute-done.4.w3
  92.7 2.0 %multiply_reduce_fusion = (bf16[16]{0:T(256)(128)(2,1)}, bf16[16,256]{1,0:T(8,128)(2,1)}) fusion(f32[16,256]{1,0:T(8,128)S(1)} %shard_map.80, bf16[256,256]{1,0:T(8,128)(2,1)} %weight.1, s32[]{:T(128)S(6)} %select_n.4, f32[16]{0:T(128)S(1)} %dynamic-slice_convert_fusion), kind=kLoop, calls=%fused_computation | loop fusion | flops 20464 | bytes 32868 | tf_op jit(solution)/shard_map/reduce_sum | solution.py:257
  94.7 0.0 copy-done.6
  94.7 5.2 %shard_map.81 = (bf16[128,256]{1,0:T(8,128)(2,1)}, bf16[128,8192]{1,0:T(8,128)(2,1)}) custom-call(s32[3]{0:T(128)S(1)} %pad_add_fusion.place, bf16[128,8192]{1,0:T(8,128)(2,1)S(1)} %copy-done.1, bf16[128,256]{1,0:T(8,128)(2,1)S(1)} %copy-done.3, f32[128,128]{1,0:T(8,128)S(1)} %copy-done.6, f32[128,256]{1,0:T(8,128)S(1)} %shard_map.79.kv_half, ...), custom_call_target="tpu_custom_call" | custom-call | flops 1048576 | bytes 1024 | tf_op jit(solution)/shard_map/pallas_call | solution.py:174
  (10 shorter events, 0.1 us)
Async XLA Ops:
  0.6 26.5 %collective-permute-start = (bf16[128,8192]{1,0:T(8,128)(2,1)}, bf16[128,8192]{1,0:T(8,128)(2,1)}, u32[]{:S(2)}, u32[]{:S(2)}) collective-permute-start(bf16[128,8192]{1,0:T(8,128)(2,1)} %tokens.7), channel_id=1, source_target_pairs={{0,16},{16,0},{1,17},{17,1},{2,18},{18,2},{3,19},{19,3},{4,20},{20... | collective-permute-start | bytes 6291464 | tf_op jit(solution)/shard_map/ppermute | solution.py:237
  10.2 0.9 copy-start.4
  12.5 14.6 %all-to-all-start = ((bf16[16,32,256]{2,1,0:T(8,128)(2,1)}), bf16[16,32,256]{2,1,0:T(8,128)(2,1)S(1)}, u32[]{:S(2)}, u32[]{:S(2)}) async-start(bf16[16,32,256]{2,1,0:T(8,128)(2,1)} %shard_map.76), calls=%async_computation | async-start | bytes 524288 | tf_op jit(solution)/shard_map/all_to_all | solution.py:235
  16.5 1.6 %copy-start = (bf16[128,8192]{1,0:T(8,128)(2,1)S(1)}, bf16[128,8192]{1,0:T(8,128)(2,1)}, u32[]{:S(2)}) copy-start(bf16[128,8192]{1,0:T(8,128)(2,1)} %tokens.7) | copy-start | bytes 6291460
  18.1 0.8 copy-start.2
  19.0 8.1 %copy-start.1 = (bf16[128,8192]{1,0:T(8,128)(2,1)S(1)}, bf16[128,8192]{1,0:T(8,128)(2,1)}, u32[]{:S(2)}) copy-start(bf16[128,8192]{1,0:T(8,128)(2,1)} %tokens.7) | copy-start | bytes 6291460
  19.8 0.7 copy-start.5
  20.5 3.1 %collective-permute-start.1 = (bf16[128,256]{1,0:T(8,128)(2,1)S(1)}, bf16[128,256]{1,0:T(8,128)(2,1)S(1)}, u32[]{:S(2)}, u32[]{:S(2)}) collective-permute-start(bf16[128,256]{1,0:T(8,128)(2,1)S(1)} %get-tuple-element.15.mine), channel_id=1, source_target_pairs={{0,16},{16,0},{1,17},{17,1},{2,18},{18,2},{3,19},{19,3},{4,20},{20... | collective-permute-start | bytes 196616 | tf_op jit(solution)/shard_map/ppermute | solution.py:239
  66.6 10.3 %copy-start.7 = (bf16[256]{0:T(256)(128)(2,1)S(1)}, bf16[256]{0:T(256)(128)(2,1)}, u32[]{:S(2)}) copy-start(bf16[256]{0:T(256)(128)(2,1)} %param.7) | copy-start | bytes 1540
  67.6 9.4 %collective-permute-start.3 = (bf16[8,256,256]{2,1,0:T(8,128)(2,1)S(1)}, bf16[8,256,256]{2,1,0:T(8,128)(2,1)}, u32[]{:S(2)}, u32[]{:S(2)}) collective-permute-start(bf16[8,256,256]{2,1,0:T(8,128)(2,1)S(1)} %get-tuple-element.16.w0), channel_id=1, source_target_pairs={{0,16},{16,0},{1,17},{17,1},{2,18},{18,2},{3,19},{19,3},{4,20},{20... | collective-permute-start | bytes 3145736 | tf_op jit(solution)/shard_map/ppermute | solution.py:246
  69.5 18.1 %collective-permute-start.2 = (bf16[8,256,256]{2,1,0:T(8,128)(2,1)S(1)}, bf16[8,256,256]{2,1,0:T(8,128)(2,1)}, u32[]{:S(2)}, u32[]{:S(2)}) collective-permute-start(bf16[8,256,256]{2,1,0:T(8,128)(2,1)S(1)} %get-tuple-element.16.w0), channel_id=1, source_target_pairs={{0,1},{1,0},{256,257},{257,256},{16,273},{17,272},{272,17},{273,16... | collective-permute-start | bytes 3145736 | tf_op jit(solution)/shard_map/ppermute | solution.py:245
  71.7 20.2 %all-to-all-start.2 = ((bf16[32,16,256]{2,1,0:T(8,128)(2,1)}), bf16[32,16,256]{2,1,0:T(8,128)(2,1)S(1)}, u32[]{:S(2)}, u32[]{:S(2)}) async-start(bf16[32,16,256]{2,1,0:T(8,128)(2,1)} %bitcast.4), calls=%async_computation.2 | async-start | bytes 524288 | tf_op jit(solution)/shard_map/all_to_all | solution.py:251
  87.6 5.1 %collective-permute-start.4 = (bf16[8,256,256]{2,1,0:T(8,128)(2,1)}, bf16[8,256,256]{2,1,0:T(8,128)(2,1)}, u32[]{:S(2)}, u32[]{:S(2)}) collective-permute-start(bf16[8,256,256]{2,1,0:T(8,128)(2,1)} %collective-permute-done.2.w2), channel_id=1, source_target_pairs={{0,16},{16,0},{1,17},{17,1},{2,18},{18,2},{3,19},{19,3},{4,20},{20... | collective-permute-start | bytes 3145736 | tf_op jit(solution)/shard_map/ppermute | solution.py:249
  91.9 2.8 %copy-start.3 = (bf16[128,256]{1,0:T(8,128)(2,1)S(1)}, bf16[128,256]{1,0:T(8,128)(2,1)}, u32[]{:S(2)}) copy-start(bf16[128,256]{1,0:T(8,128)(2,1)} %cot.3) | copy-start | bytes 196612
  92.0 2.8 %copy-start.6 = (f32[128,128]{1,0:T(8,128)S(1)}, f32[128,128]{1,0:T(8,128)}, u32[]{:S(2)}) copy-start(f32[128,128]{1,0:T(8,128)} %copy-done.5) | copy-start | bytes 196612

commit v6 on v5

v6 whole, which is shorter than its diff:
```python
import itertools
import math

import jax
import jax.numpy as jnp
import numpy as np
from jax import lax
from jax.experimental import pallas as pl
from jax.experimental.pallas import tpu as pltpu
from jax.sharding import Mesh, PartitionSpec as P

AXES = ("xh", "yh", "yl", "c", "zh", "zl", "xl")
SIZES = (2, 4, 2, 2, 4, 2, 2)
F32, BF16 = jnp.float32, jnp.bfloat16


def share_kernel(place, weight, gain, out, scaled):
    xl, zl = place[1], place[3]
    row = lax.broadcasted_iota(jnp.int32, (256, 256), 0)
    column = lax.broadcasted_iota(jnp.int32, (256, 256), 1)
    diagonal = jnp.where(row == column, gain[...].astype(F32).reshape(1, 256), 0.0).astype(BF16)
    scaled[...] = jnp.dot(diagonal, weight[...], preferred_element_type=F32).astype(BF16)
    for yl in range(2):
        rows = scaled[pl.ds(pl.multiple_of(128 * xl + 64 * yl + 32 * zl, 32), 32), :]
        for k in range(8):
            out[2 * k + yl] = rows


def make_share(place, weight, gain):
    vmem = pl.BlockSpec(memory_space=pltpu.VMEM)
    return pl.pallas_call(
        share_kernel,
        in_specs=[pl.BlockSpec(memory_space=pltpu.SMEM), vmem, vmem],
        out_specs=vmem,
        out_shape=jax.ShapeDtypeStruct((16, 32, 256), BF16),
        scratch_shapes=[pltpu.VMEM((256, 256), BF16)],
        compiler_params=pltpu.CompilerParams(vmem_limit_bytes=4 << 20),
        cost_estimate=pl.CostEstimate(flops=1 << 25, bytes_accessed=1 << 19, transcendentals=0),
    )(place, weight, gain)


def roots(tokens):
    wide = tokens[...].astype(F32)
    return lax.rsqrt(jnp.mean(wide * wide, -1, keepdims=True) + 1e-05)


def outer_kernel(core, tokens, got, cot, got_cot, out, inv):
    mine, theirs = roots(tokens), roots(got)
    inv[...] = jnp.broadcast_to(mine, inv.shape)
    right = jnp.concatenate([cot[...].astype(F32) * mine, got_cot[...].astype(F32) * theirs], 0).astype(BF16)
    for xh in range(2):
        for yh in range(4):
            for yl in range(2):
                block = 8 * xh + 2 * yh + yl
                start = pl.multiple_of(512 * block + 256 * core[0], 256)
                left = jnp.concatenate([tokens[:, pl.ds(start, 256)], got[:, pl.ds(start, 256)]], 0)
                u = lax.dot_general(left, right, (((0,), (0,)), ((), ())), preferred_element_type=F32)
                u = u.reshape(4, 2, 2, 16, 256).astype(BF16)
                first = 64 * (4 * xh + yh)
                for xl in range(2):
                    for zl in range(2):
                        out[4 * xl + 2 * yl + zl, first : first + 64] = u[:, zl, xl].reshape(64, 256)


def outer_terms(core, tokens, got, cot, got_cot):
    vmem = pl.BlockSpec(memory_space=pltpu.VMEM)
    return pl.pallas_call(
        outer_kernel,
        in_specs=[pl.BlockSpec(memory_space=pltpu.SMEM)] + [vmem] * 4,
        out_specs=[vmem, vmem],
        out_shape=[
            jax.ShapeDtypeStruct((8, 512, 256), BF16),
            jax.ShapeDtypeStruct((tokens.shape[0], 128), F32),
        ],
        compiler_params=pltpu.CompilerParams(vmem_limit_bytes=12 << 20),
        cost_estimate=pl.CostEstimate(flops=2 * tokens.size * 256, bytes_accessed=8 * tokens.size, transcendentals=0),
    )(core, tokens, got, cot, got_cot)


def sum_kernel(parts, out, after):
    after[...] = jnp.zeros_like(after)
    total = parts[0].astype(F32)
    for k in range(1, 8):
        total += parts[k].astype(F32)
    out[...] = total.astype(BF16)


def sum_of(parts):
    vmem = pl.BlockSpec(memory_space=pltpu.VMEM)
    return pl.pallas_call(
        sum_kernel,
        in_specs=[vmem],
        out_specs=[vmem, vmem],
        out_shape=[jax.ShapeDtypeStruct(parts.shape[1:], BF16), jax.ShapeDtypeStruct((8, 128), F32)],
        compiler_params=pltpu.CompilerParams(vmem_limit_bytes=8 << 20),
        cost_estimate=pl.CostEstimate(flops=1 << 20, bytes_accessed=2 << 20, transcendentals=0),
    )(parts)


def weight_pieces(place, half, refs):
    yl, zl = place[2], place[3]

    def reader(ref, row):
        return lambda: jnp.concatenate(
            [ref[2 * (sz + zl - 2 * sz * zl) + (sy + yl - 2 * sy * yl), row : row + 32] for sy in range(2) for sz in range(2)], 0
        )

    pieces = []
    for block in range(16):
        for ref, side in zip(refs, (place[0], 1 - place[0])):
            start = pl.multiple_of(512 * block + 256 * side + 128 * half, 128)
            pieces.append((reader(ref, 32 * block), start))
    return pieces


def project(tokens, pieces, total):
    for read, start in pieces:
        total += jnp.dot(tokens[:, pl.ds(start, 128)], read(), preferred_element_type=F32)
    return total


def first_kernel(place, tokens, w0, w1, out):
    out[...] = project(tokens, weight_pieces(place, place[1], (w0, w1)), jnp.zeros(out.shape, F32))


def first_half(place, tokens, weights):
    vmem = pl.BlockSpec(memory_space=pltpu.VMEM)
    return pl.pallas_call(
        first_kernel,
        in_specs=[pl.BlockSpec(memory_space=pltpu.SMEM)] + [vmem] * 3,
        out_specs=vmem,
        out_shape=jax.ShapeDtypeStruct((tokens.shape[0], 256), F32),
        compiler_params=pltpu.CompilerParams(vmem_limit_bytes=8 << 20),
        cost_estimate=pl.CostEstimate(flops=1 << 20, bytes_accessed=1 << 10, transcendentals=0),
    )(place, tokens, *weights)


def final_kernel(place, tokens, cot, inv, kv_half, w0, w1, w2, w3, kv_out, token_grad):
    width = tokens.shape[1]
    later = weight_pieces(place, 1 - place[1], (w2, w3))
    root = inv[:, :1]
    kv = project(tokens, later, kv_half[...]) * root
    kv_out[...] = kv.astype(BF16)
    g = cot[...]
    slopes = jnp.sum(g.astype(F32) * kv, -1, keepdims=True) * (1.0 / width)
    slopes = root * slopes
    for read, start in weight_pieces(place, place[1], (w0, w1)) + later:
        back = lax.dot_general(g, read(), (((1,), (1,)), ((), ())), preferred_element_type=F32)
        x = tokens[:, pl.ds(start, 128)].astype(F32)
        token_grad[:, pl.ds(start, 128)] = (root * (back - x * slopes)).astype(BF16)


def final(place, tokens, cot, inv, kv_half, weights):
    vmem = pl.BlockSpec(memory_space=pltpu.VMEM)
    return pl.pallas_call(
        final_kernel,
        in_specs=[pl.BlockSpec(memory_space=pltpu.SMEM)] + [vmem] * 8,
        out_specs=[vmem, vmem],
        out_shape=[
            jax.ShapeDtypeStruct(cot.shape, BF16),
            jax.ShapeDtypeStruct(tokens.shape, BF16),
        ],
        compiler_params=pltpu.CompilerParams(vmem_limit_bytes=14 << 20),
        cost_estimate=pl.CostEstimate(flops=1 << 20, bytes_accessed=1 << 10, transcendentals=0),
    )(place, tokens, cot, inv, kv_half, *weights)


def total_kernel(parts, out):
    total = parts[0].astype(F32)
    for k in range(1, parts.shape[0]):
        total += parts[k].astype(F32)
    out[...] = total * (1.0 / 256.0)


def total_of(parts):
    vmem = pl.BlockSpec(memory_space=pltpu.VMEM)
    return pl.pallas_call(
        total_kernel,
        in_specs=[vmem],
        out_specs=vmem,
        out_shape=jax.ShapeDtypeStruct(parts.shape[1:], F32),
        compiler_params=pltpu.CompilerParams(vmem_limit_bytes=2 << 20),
        cost_estimate=pl.CostEstimate(flops=50 * 10**9, bytes_accessed=1 << 18, transcendentals=0),
    )(parts)


SWAP = [(0, 1), (1, 0)]


def cubes():
    index = np.arange(math.prod(SIZES)).reshape(SIZES)
    groups = []
    for core in range(2):
        for x0, y0, z0 in itertools.product(range(core, 4, 2), range(core, 8, 2), range(core, 8, 2)):
            members = {}
            for a, b, c in itertools.product(range(2), repeat=3):
                x, y, z = (x0 + a) % 4, (y0 + b) % 8, (z0 + c) % 8
                members[x % 2, y % 2, z % 2] = int(index[x // 2, y // 2, y % 2, core, z // 2, z % 2, x % 2])
            groups.append([members[k] for k in sorted(members)])
    return groups


def neighbours(axis):
    count = 4 if axis == "x" else 8

    def place(at, core):
        high, low = at // 2, at % 2
        if axis == "x":
            return 4 * high + 2 * core + low
        if axis == "y":
            return 4 * high + 2 * low + core
        return 8 * core + at

    return [
        (place(at, core), place((at + (1 if at % 2 == core else -1)) % count, core))
        for core in range(2)
        for at in range(count)
    ]


def body(tokens, cotangent, kv_weight, norm_gain):
    yl, xl, zl = lax.axis_index("yl"), lax.axis_index("xl"), lax.axis_index("zl")
    place = jnp.stack([lax.axis_index("c"), xl, yl, zl]).astype(jnp.int32)
    piece = 4 * lax.axis_index("zh") + 2 * zl + xl

    share = make_share(place, kv_weight, norm_gain)
    share = lax.all_to_all(share, ("xh", "yh", "yl"), 0, 0, tiled=True).reshape(1, 512, 256)

    got, got_cotangent = lax.ppermute(tokens, "c", SWAP), lax.ppermute(cotangent, "c", SWAP)
    u, inv = outer_terms(place, tokens, got, cotangent, got_cotangent)
    u, after = sum_of(lax.all_to_all(u, AXES, 0, 0, tiled=True, axis_index_groups=cubes()))
    u = lax.all_to_all(u.reshape(32, 16, 256), ("xh", "yh", "zh"), 0, 0, tiled=True)

    share = jnp.concatenate([share, lax.ppermute(share, ("yh", "yl", "c"), neighbours("y"))])
    w0 = jnp.concatenate([share, lax.ppermute(share, ("c", "zh", "zl"), neighbours("z"))])
    w2 = lax.ppermute(w0, ("xh", "c", "xl"), neighbours("x"))
    w1 = lax.ppermute(w0, "c", SWAP)
    kv_half = first_half(place, tokens, (w0, w1))
    w2, kv_half = lax.optimization_barrier((w2, kv_half))
    w3 = lax.ppermute(w2, "c", SWAP)
    u, w3 = lax.optimization_barrier((total_of(u), w3))
    kv_out, token_grad = final(place, tokens, cotangent, inv, kv_half, (w0, w1, w2, w3))

    gain = lax.dynamic_slice_in_dim(norm_gain, 16 * piece, 16, 0).astype(F32)[:, None]
    rows = lax.dynamic_slice_in_dim(kv_weight, 16 * piece, 16, 0).astype(F32)
    kv_grad = (u * gain).astype(BF16)
    gain_grad = jnp.sum(u * rows, -1).astype(BF16)
    return (kv_out, token_grad, kv_grad, gain_grad)


def solution(mesh):
    split = Mesh(mesh.devices.reshape(SIZES), AXES)
    every, inner = P(AXES, None), ("xh", "yh", "yl", "c")
    return jax.shard_map(
        body,
        mesh=split,
        in_specs=(every, every, P(inner, None), P(inner)),
        out_specs=(every, every, every, P(AXES)),
        check_vma=False,
    )
```

time: 101 us -> 112 us (1.11)
  the two profiles are of different devices: /device:TPU:1 before, /device:TPU:8 now
where the time goes in v6:
time: 112 us; the launch traced here: 111 us
  starting transfers between devices  49.2 us (44%)
  waiting for transfers between devices  38.6 us (34%)
  Pallas kernels  15 us (13%)
  local copies, waits for them, and re-layouts  5.32 us (5%)
  other arithmetic  2.3 us (2%)
    ppermute x1, waiting for transfers between devices, body(): lax.ppermute(share, ('yh', 'yl', 'c'), neighbours('y'))  15.3 us
    all_to_all x1, waiting for transfers between devices, body(): lax.all_to_all(u.reshape(32, 16, 256), ('xh', 'yh', 'zh'), 0, 0, tiled=True)  11.9 us
    all_to_all x1, starting transfers between devices, body(): lax.all_to_all(u.reshape(32, 16, 256), ('xh', 'yh', 'zh'), 0, 0, tiled=True)  11 us
    all_to_all x1, starting transfers between devices, body(): lax.all_to_all(share, ('xh', 'yh', 'yl'), 0, 0, tiled=True)  10 us
    ppermute x1, starting transfers between devices, body(): w1 = lax.ppermute(w0, 'c', SWAP)  7.46 us
    ppermute x1, waiting for transfers between devices, body(): lax.ppermute(share, ('c', 'zh', 'zl'), neighbours('z'))  7.14 us
    pallas_call x1, Pallas kernels, final(): pl.pallas_call(final_kernel, in_specs=[pl.BlockSpec(memory_space=pltpu.SM...  5.89 us
    ppermute x1, starting transfers between devices, body(): lax.ppermute(share, ('c', 'zh', 'zl'), neighbours('z'))  5.36 us
  transfers between devices with their start and end apart: 10, of which 5 were waited for; matrix products, arithmetic and copies ran while one was open for 0% of the time, Pallas kernels for 8%

profile of v6, /device:TPU:8, one launch (start us, length us, event | category | flops | bytes accessed | tf_op | source)
XLA Modules:
  0.0 111.2 jit_solution(7078006629322058909)
XLA Ops:
  0.6 1.9 %collective-permute-start = (bf16[128,8192]{1,0:T(8,128)(2,1)}, bf16[128,8192]{1,0:T(8,128)(2,1)S(1)}, u32[]{:S(2)}, u32[]{:S(2)}) collective-permute-start(bf16[128,8192]{1,0:T(8,128)(2,1)} %tokens.5), channel_id=1, source_target_pairs={{0,16},{16,0},{1,17},{17,1},{2,18},{18,2},{3,19},{19,3},{4,20},{20... | collective-permute-start | bytes 6291464 | tf_op jit(solution)/shard_map/ppermute | solution.py:229
  2.6 0.1 pad_add_fusion.core.place
  2.6 0.9 copy-done.5
  3.6 0.7 copy-done.6
  4.2 1.4 %shard_map.76 = bf16[16,32,256]{2,1,0:T(8,128)(2,1)} custom-call(s32[4]{0:T(128)S(1)} %pad_add_fusion.core.place, bf16[256,256]{1,0:T(8,128)(2,1)S(1)} %copy-done.5, bf16[256]{0:T(256)(128)(2,1)S(1)} %copy-done.6), custom_call_target="tpu_custom_call" | custom-call | flops 33554432 | bytes 524288 | tf_op jit(solution)/shard_map/pallas_call | solution.py:31
  5.6 10.0 %all-to-all-start = ((bf16[16,32,256]{2,1,0:T(8,128)(2,1)}), bf16[16,32,256]{2,1,0:T(8,128)(2,1)S(1)}, u32[]{:S(2)}, u32[]{:S(2)}) async-start(bf16[16,32,256]{2,1,0:T(8,128)(2,1)} %shard_map.76), calls=%async_computation | async-start | bytes 524288 | tf_op jit(solution)/shard_map/all_to_all | solution.py:227
  15.7 1.9 %collective-permute-start.1 = (bf16[128,256]{1,0:T(8,128)(2,1)}, bf16[128,256]{1,0:T(8,128)(2,1)S(1)}, u32[]{:S(2)}, u32[]{:S(2)}) collective-permute-start(bf16[128,256]{1,0:T(8,128)(2,1)} %cot.3), channel_id=1, source_target_pairs={{0,16},{16,0},{1,17},{17,1},{2,18},{18,2},{3,19},{19,3},{4,20},{20... | collective-permute-start | bytes 196616 | tf_op jit(solution)/shard_map/ppermute | solution.py:229
  17.6 1.4 %collective-permute-done.1.got_cot = bf16[128,256]{1,0:T(8,128)(2,1)S(1)} collective-permute-done((bf16[128,256]{1,0:T(8,128)(2,1)}, bf16[128,256]{1,0:T(8,128)(2,1)S(1)}, u32[]{:S(2)}, u32[]{:S(2)}) %collective-permute-start.1) | collective-permute-done | bytes 65568 | tf_op jit(solution)/shard_map/ppermute | solution.py:229
  19.0 1.6 %copy-done = bf16[128,8192]{1,0:T(8,128)(2,1)S(1)} copy-done((bf16[128,8192]{1,0:T(8,128)(2,1)S(1)}, bf16[128,8192]{1,0:T(8,128)(2,1)}, u32[]{:S(2)}) %copy-start) | copy-done | bytes 2097176
  20.6 0.8 copy-done.3
  21.5 2.2 %shard_map.75 = (bf16[8,512,256]{2,1,0:T(8,128)(2,1)S(1)}, f32[128,128]{1,0:T(8,128)S(1)}) custom-call(s32[4]{0:T(128)S(1)} %pad_add_fusion.core.place, bf16[128,8192]{1,0:T(8,128)(2,1)S(1)} %copy-done, bf16[128,8192]{1,0:T(8,128)(2,1)S(1)} %collective-permute-done.got, bf16[128,256]{1,0:T(8,128)(2,1)S(1)} %copy-done.3, ...), custom_call_target="tpu_custom_call" | custom-call | flops 536870912 | bytes 8388608 | tf_op jit(solution)/shard_map/pallas_call | solution.py:67
  23.6 0.0 copy-start.2
  23.7 1.3 %copy-done.2 = bf16[8,512,256]{2,1,0:T(8,128)(2,1)} copy-done((bf16[8,512,256]{2,1,0:T(8,128)(2,1)}, bf16[8,512,256]{2,1,0:T(8,128)(2,1)S(1)}, u32[]{:S(2)}) %copy-start.2) | copy-done | bytes 2097176
  25.0 2.8 %all-to-all-done = bf16[16,32,256]{2,1,0:T(8,128)(2,1)S(1)} async-done(((bf16[16,32,256]{2,1,0:T(8,128)(2,1)}), bf16[16,32,256]{2,1,0:T(8,128)(2,1)S(1)}, u32[]{:S(2)}, u32[]{:S(2)}) %all-to-all-start) | async-done | bytes 262176 | tf_op jit(solution)/shard_map/all_to_all | solution.py:227
  27.8 5.1 %all-to-all-start.1 = ((bf16[8,512,256]{2,1,0:T(8,128)(2,1)}), bf16[8,512,256]{2,1,0:T(8,128)(2,1)}, u32[]{:S(2)}, u32[]{:S(2)}) async-start(bf16[8,512,256]{2,1,0:T(8,128)(2,1)} %copy-done.2), calls=%async_computation.1 | async-start | bytes 4194304 | tf_op jit(solution)/shard_map/all_to_all | solution.py:231
  32.9 1.9 %collective-permute-start.2 = (bf16[1,512,256]{2,1,0:T(8,128)(2,1)S(1)}, bf16[1,512,256]{2,1,0:T(8,128)(2,1)S(1)}, u32[]{:S(2)}, u32[]{:S(2)}) collective-permute-start(bf16[1,512,256]{2,1,0:T(8,128)(2,1)S(1)} %bitcast.6), channel_id=1, source_target_pairs={{0,32},{32,0},{64,96},{96,64},{128,160},{160,128},{192,224},{224,1... | collective-permute-start | bytes 786440 | tf_op jit(solution)/shard_map/ppermute | solution.py:234
  34.9 15.3 %collective-permute-done.2 = bf16[1,512,256]{2,1,0:T(8,128)(2,1)S(1)} collective-permute-done((bf16[1,512,256]{2,1,0:T(8,128)(2,1)S(1)}, bf16[1,512,256]{2,1,0:T(8,128)(2,1)S(1)}, u32[]{:S(2)}, u32[]{:S(2)}) %collective-permute-start.2) | collective-permute-done | bytes 262176 | tf_op jit(solution)/shard_map/ppermute | solution.py:234
  50.1 0.1 pad_maximum_fusion.1
  50.2 5.4 %collective-permute-start.3 = (bf16[2,512,256]{2,1,0:T(8,128)(2,1)S(1)}, bf16[2,512,256]{2,1,0:T(8,128)(2,1)S(1)}, u32[]{:S(2)}, u32[]{:S(2)}) collective-permute-start(bf16[2,512,256]{2,1,0:T(8,128)(2,1)S(1)} %pad_maximum_fusion.1), channel_id=1, source_target_pairs={{0,2},{2,0},{4,6},{6,4},{8,10},{10,8},{12,14},{14,12},{16,30},{18,... | collective-permute-start | bytes 1572872 | tf_op jit(solution)/shard_map/ppermute | solution.py:235
  55.6 7.1 %collective-permute-done.3 = bf16[2,512,256]{2,1,0:T(8,128)(2,1)S(1)} collective-permute-done((bf16[2,512,256]{2,1,0:T(8,128)(2,1)S(1)}, bf16[2,512,256]{2,1,0:T(8,128)(2,1)S(1)}, u32[]{:S(2)}, u32[]{:S(2)}) %collective-permute-start.3) | collective-permute-done | bytes 524320 | tf_op jit(solution)/shard_map/ppermute | solution.py:235
  62.7 0.1 pad_maximum_fusion.w0
  62.8 7.5 %collective-permute-start.5 = (bf16[4,512,256]{2,1,0:T(8,128)(2,1)S(1)}, bf16[4,512,256]{2,1,0:T(8,128)(2,1)}, u32[]{:S(2)}, u32[]{:S(2)}) collective-permute-start(bf16[4,512,256]{2,1,0:T(8,128)(2,1)S(1)} %pad_maximum_fusion.w0), channel_id=1, source_target_pairs={{0,16},{16,0},{1,17},{17,1},{2,18},{18,2},{3,19},{19,3},{4,20},{20... | collective-permute-start | bytes 3145736 | tf_op jit(solution)/shard_map/ppermute | solution.py:237
  70.3 2.5 %collective-permute-start.4 = (bf16[4,512,256]{2,1,0:T(8,128)(2,1)S(1)}, bf16[4,512,256]{2,1,0:T(8,128)(2,1)}, u32[]{:S(2)}, u32[]{:S(2)}) collective-permute-start(bf16[4,512,256]{2,1,0:T(8,128)(2,1)S(1)} %pad_maximum_fusion.w0), channel_id=1, source_target_pairs={{0,1},{1,0},{256,257},{257,256},{16,273},{17,272},{272,17},{273,16... | collective-permute-start | bytes 3145736 | tf_op jit(solution)/shard_map/ppermute | solution.py:236
  72.8 2.6 %shard_map.78 = (bf16[512,256]{1,0:T(8,128)(2,1)}, f32[8,128]{1,0:T(8,128)}) custom-call(bf16[8,512,256]{2,1,0:T(8,128)(2,1)} %all-to-all-done.1.parts), custom_call_target="tpu_custom_call" | custom-call | flops 1048576 | bytes 2097152 | tf_op jit(solution)/shard_map/pallas_call | solution.py:90
  75.4 11.0 %all-to-all-start.2 = ((bf16[32,16,256]{2,1,0:T(8,128)(2,1)}), bf16[32,16,256]{2,1,0:T(8,128)(2,1)}, u32[]{:S(2)}, u32[]{:S(2)}) async-start(bf16[32,16,256]{2,1,0:T(8,128)(2,1)} %bitcast.5), calls=%async_computation.2 | async-start | bytes 524288 | tf_op jit(solution)/shard_map/all_to_all | solution.py:232
  86.4 0.1 dynamic-slice_convert_fusion
  86.5 1.9 %shard_map.77.kv_half = f32[128,256]{1,0:T(8,128)S(1)} custom-call(s32[4]{0:T(128)S(1)} %pad_add_fusion.core.place, bf16[128,8192]{1,0:T(8,128)(2,1)S(1)} %copy-done.1, bf16[4,512,256]{2,1,0:T(8,128)(2,1)S(1)} %pad_maximum_fusion.w0, bf16[4,512,256]{2,1,0:T(8,128)(2,1)} %collective-permute-done.5.w1), custom_call_target="tpu_custom_call" | custom-call | flops 1048576 | bytes 1024 | tf_op jit(solution)/shard_map/pallas_call | solution.py:128
  88.5 1.9 %collective-permute-start.6 = (bf16[4,512,256]{2,1,0:T(8,128)(2,1)}, bf16[4,512,256]{2,1,0:T(8,128)(2,1)}, u32[]{:S(2)}, u32[]{:S(2)}) collective-permute-start(bf16[4,512,256]{2,1,0:T(8,128)(2,1)} %collective-permute-done.4.w2), channel_id=1, source_target_pairs={{0,16},{16,0},{1,17},{17,1},{2,18},{18,2},{3,19},{19,3},{4,20},{20... | collective-permute-start | bytes 3145736 | tf_op jit(solution)/shard_map/ppermute | solution.py:240
  90.4 11.9 %all-to-all-done.2.parts = bf16[32,16,256]{2,1,0:T(8,128)(2,1)} async-done(((bf16[32,16,256]{2,1,0:T(8,128)(2,1)}), bf16[32,16,256]{2,1,0:T(8,128)(2,1)}, u32[]{:S(2)}, u32[]{:S(2)}) %all-to-all-start.2) | async-done | bytes 262176 | tf_op jit(solution)/shard_map/all_to_all | solution.py:232
  102.3 1.0 shard_map.79
  103.4 2.0 %multiply_reduce_fusion = (bf16[16]{0:T(256)(128)(2,1)}, bf16[16,256]{1,0:T(8,128)(2,1)}) fusion(f32[16,256]{1,0:T(8,128)S(1)} %shard_map.79, bf16[256,256]{1,0:T(8,128)(2,1)} %weight.1, s32[]{:T(128)S(6)} %select_n.4, f32[16]{0:T(128)S(1)} %dynamic-slice_convert_fusion), kind=kLoop, calls=%fused_computation.2 | loop fusion | flops 20464 | bytes 32868 | tf_op jit(solution)/shard_map/reduce_sum | solution.py:247
  105.4 5.9 %shard_map.80 = (bf16[128,256]{1,0:T(8,128)(2,1)}, bf16[128,8192]{1,0:T(8,128)(2,1)}) custom-call(s32[4]{0:T(128)S(1)} %pad_add_fusion.core.place, bf16[128,8192]{1,0:T(8,128)(2,1)S(1)} %copy-done.1, bf16[128,256]{1,0:T(8,128)(2,1)S(1)} %copy-done.4, f32[128,128]{1,0:T(8,128)S(1)} %get-tuple-element.13.inv, f32[128,256]{1,0:T(8,128)S(1)} %shard_map.77.kv_half, ...), custom_call_target="tpu_custom_call" | custom-call | flops 1048576 | bytes 1024 | tf_op jit(solution)/shard_map/pallas_call | solution.py:155
  (15 shorter events, 0.0 us)
Async XLA Ops:
  0.6 18.4 %collective-permute-start = (bf16[128,8192]{1,0:T(8,128)(2,1)}, bf16[128,8192]{1,0:T(8,128)(2,1)S(1)}, u32[]{:S(2)}, u32[]{:S(2)}) collective-permute-start(bf16[128,8192]{1,0:T(8,128)(2,1)} %tokens.5), channel_id=1, source_target_pairs={{0,16},{16,0},{1,17},{17,1},{2,18},{18,2},{3,19},{19,3},{4,20},{20... | collective-permute-start | bytes 6291464 | tf_op jit(solution)/shard_map/ppermute | solution.py:229
  2.6 0.9 copy-start.5
  3.6 0.7 copy-start.6
  5.6 22.1 %all-to-all-start = ((bf16[16,32,256]{2,1,0:T(8,128)(2,1)}), bf16[16,32,256]{2,1,0:T(8,128)(2,1)S(1)}, u32[]{:S(2)}, u32[]{:S(2)}) async-start(bf16[16,32,256]{2,1,0:T(8,128)(2,1)} %shard_map.76), calls=%async_computation | async-start | bytes 524288 | tf_op jit(solution)/shard_map/all_to_all | solution.py:227
  15.7 3.3 %collective-permute-start.1 = (bf16[128,256]{1,0:T(8,128)(2,1)}, bf16[128,256]{1,0:T(8,128)(2,1)S(1)}, u32[]{:S(2)}, u32[]{:S(2)}) collective-permute-start(bf16[128,256]{1,0:T(8,128)(2,1)} %cot.3), channel_id=1, source_target_pairs={{0,16},{16,0},{1,17},{17,1},{2,18},{18,2},{3,19},{19,3},{4,20},{20... | collective-permute-start | bytes 196616 | tf_op jit(solution)/shard_map/ppermute | solution.py:229
  19.0 1.6 %copy-start = (bf16[128,8192]{1,0:T(8,128)(2,1)S(1)}, bf16[128,8192]{1,0:T(8,128)(2,1)}, u32[]{:S(2)}) copy-start(bf16[128,8192]{1,0:T(8,128)(2,1)} %tokens.5) | copy-start | bytes 6291460
  20.6 0.8 copy-start.3
  23.6 1.3 %copy-start.2 = (bf16[8,512,256]{2,1,0:T(8,128)(2,1)}, bf16[8,512,256]{2,1,0:T(8,128)(2,1)S(1)}, u32[]{:S(2)}) copy-start(bf16[8,512,256]{2,1,0:T(8,128)(2,1)S(1)} %get-tuple-element.16) | copy-start | bytes 6291460
  27.8 45.0 %all-to-all-start.1 = ((bf16[8,512,256]{2,1,0:T(8,128)(2,1)}), bf16[8,512,256]{2,1,0:T(8,128)(2,1)}, u32[]{:S(2)}, u32[]{:S(2)}) async-start(bf16[8,512,256]{2,1,0:T(8,128)(2,1)} %copy-done.2), calls=%async_computation.1 | async-start | bytes 4194304 | tf_op jit(solution)/shard_map/all_to_all | solution.py:231
  32.9 17.2 %collective-permute-start.2 = (bf16[1,512,256]{2,1,0:T(8,128)(2,1)S(1)}, bf16[1,512,256]{2,1,0:T(8,128)(2,1)S(1)}, u32[]{:S(2)}, u32[]{:S(2)}) collective-permute-start(bf16[1,512,256]{2,1,0:T(8,128)(2,1)S(1)} %bitcast.6), channel_id=1, source_target_pairs={{0,32},{32,0},{64,96},{96,64},{128,160},{160,128},{192,224},{224,1... | collective-permute-start | bytes 786440 | tf_op jit(solution)/shard_map/ppermute | solution.py:234
  50.2 36.2 %copy-start.7 = (bf16[256]{0:T(256)(128)(2,1)S(1)}, bf16[256]{0:T(256)(128)(2,1)}, u32[]{:S(2)}) copy-start(bf16[256]{0:T(256)(128)(2,1)} %gain.1) | copy-start | bytes 1540
  50.2 36.3 %copy-start.1 = (bf16[128,8192]{1,0:T(8,128)(2,1)S(1)}, bf16[128,8192]{1,0:T(8,128)(2,1)}, u32[]{:S(2)}) copy-start(bf16[128,8192]{1,0:T(8,128)(2,1)} %tokens.5) | copy-start | bytes 6291460
  50.2 12.5 %collective-permute-start.3 = (bf16[2,512,256]{2,1,0:T(8,128)(2,1)S(1)}, bf16[2,512,256]{2,1,0:T(8,128)(2,1)S(1)}, u32[]{:S(2)}, u32[]{:S(2)}) collective-permute-start(bf16[2,512,256]{2,1,0:T(8,128)(2,1)S(1)} %pad_maximum_fusion.1), channel_id=1, source_target_pairs={{0,2},{2,0},{4,6},{6,4},{8,10},{10,8},{12,14},{14,12},{16,30},{18,... | collective-permute-start | bytes 1572872 | tf_op jit(solution)/shard_map/ppermute | solution.py:235
  62.8 23.7 %collective-permute-start.5 = (bf16[4,512,256]{2,1,0:T(8,128)(2,1)S(1)}, bf16[4,512,256]{2,1,0:T(8,128)(2,1)}, u32[]{:S(2)}, u32[]{:S(2)}) collective-permute-start(bf16[4,512,256]{2,1,0:T(8,128)(2,1)S(1)} %pad_maximum_fusion.w0), channel_id=1, source_target_pairs={{0,16},{16,0},{1,17},{17,1},{2,18},{18,2},{3,19},{19,3},{4,20},{20... | collective-permute-start | bytes 3145736 | tf_op jit(solution)/shard_map/ppermute | solution.py:237
  70.3 18.2 %collective-permute-start.4 = (bf16[4,512,256]{2,1,0:T(8,128)(2,1)S(1)}, bf16[4,512,256]{2,1,0:T(8,128)(2,1)}, u32[]{:S(2)}, u32[]{:S(2)}) collective-permute-start(bf16[4,512,256]{2,1,0:T(8,128)(2,1)S(1)} %pad_maximum_fusion.w0), channel_id=1, source_target_pairs={{0,1},{1,0},{256,257},{257,256},{16,273},{17,272},{272,17},{273,16... | collective-permute-start | bytes 3145736 | tf_op jit(solution)/shard_map/ppermute | solution.py:236
  75.4 26.9 %all-to-all-start.2 = ((bf16[32,16,256]{2,1,0:T(8,128)(2,1)}), bf16[32,16,256]{2,1,0:T(8,128)(2,1)}, u32[]{:S(2)}, u32[]{:S(2)}) async-start(bf16[32,16,256]{2,1,0:T(8,128)(2,1)} %bitcast.5), calls=%async_computation.2 | async-start | bytes 524288 | tf_op jit(solution)/shard_map/all_to_all | solution.py:232
  88.5 16.9 %copy-start.4 = (bf16[128,256]{1,0:T(8,128)(2,1)S(1)}, bf16[128,256]{1,0:T(8,128)(2,1)}, u32[]{:S(2)}) copy-start(bf16[128,256]{1,0:T(8,128)(2,1)} %cot.3) | copy-start | bytes 196612
  88.5 14.8 %collective-permute-start.6 = (bf16[4,512,256]{2,1,0:T(8,128)(2,1)}, bf16[4,512,256]{2,1,0:T(8,128)(2,1)}, u32[]{:S(2)}, u32[]{:S(2)}) collective-permute-start(bf16[4,512,256]{2,1,0:T(8,128)(2,1)} %collective-permute-done.4.w2), channel_id=1, source_target_pairs={{0,16},{16,0},{1,17},{17,1},{2,18},{18,2},{3,19},{19,3},{4,20},{20... | collective-permute-start | bytes 3145736 | tf_op jit(solution)/shard_map/ppermute | solution.py:240

commit v7 on v4

v7 whole, which is shorter than its diff:
```python
import itertools
import math

import jax
import jax.numpy as jnp
import numpy as np
from jax import lax
from jax.experimental import pallas as pl
from jax.experimental.pallas import tpu as pltpu
from jax.sharding import Mesh, PartitionSpec as P

AXES = ("xh", "yh", "yl", "c", "zh", "zl", "xl")
SIZES = (2, 4, 2, 2, 4, 2, 2)
F32, BF16 = jnp.float32, jnp.bfloat16


def share_kernel(place, weight, gain, out, held, held_gain, scaled, sems):
    xl, zl = place[1], place[2]
    fetches = [
        pltpu.make_async_copy(weight, held, sems.at[0]),
        pltpu.make_async_copy(gain, held_gain, sems.at[1]),
    ]
    for fetch in fetches:
        fetch.start()
    row = lax.broadcasted_iota(jnp.int32, (256, 256), 0)
    column = lax.broadcasted_iota(jnp.int32, (256, 256), 1)
    for fetch in fetches:
        fetch.wait()
    diagonal = jnp.where(row == column, held_gain[...].astype(F32).reshape(1, 256), 0.0).astype(BF16)
    scaled[...] = jnp.dot(diagonal, held[...], preferred_element_type=F32).astype(BF16)
    for yl in range(2):
        rows = scaled[pl.ds(pl.multiple_of(128 * xl + 64 * yl + 32 * zl, 32), 32), :]
        for k in range(8):
            out[2 * k + yl] = rows


def make_share(place, weight, gain):
    main = pl.BlockSpec(memory_space=pltpu.HBM)
    return pl.pallas_call(
        share_kernel,
        in_specs=[pl.BlockSpec(memory_space=pltpu.SMEM), main, main],
        out_specs=pl.BlockSpec(memory_space=pltpu.VMEM),
        out_shape=jax.ShapeDtypeStruct((16, 32, 256), BF16),
        scratch_shapes=[
            pltpu.VMEM((256, 256), BF16),
            pltpu.VMEM((256,), BF16),
            pltpu.VMEM((256, 256), BF16),
            pltpu.SemaphoreType.DMA((2,)),
        ],
        compiler_params=pltpu.CompilerParams(vmem_limit_bytes=4 << 20),
        cost_estimate=pl.CostEstimate(flops=1 << 25, bytes_accessed=1 << 19, transcendentals=0),
    )(place, weight, gain)


def roots(tokens):
    wide = tokens[...].astype(F32)
    return lax.rsqrt(jnp.mean(wide * wide, -1, keepdims=True) + 1e-05)


def outer_kernel(core, tokens, got, cot, got_cot, out, inv):
    mine, theirs = roots(tokens), roots(got)
    inv[...] = jnp.broadcast_to(mine, inv.shape)
    right = jnp.concatenate([cot[...].astype(F32) * mine, got_cot[...].astype(F32) * theirs], 0).astype(BF16)
    for xh in range(2):
        for yh in range(4):
            for yl in range(2):
                block = 8 * xh + 2 * yh + yl
                start = pl.multiple_of(512 * block + 256 * core[0], 256)
                left = jnp.concatenate([tokens[:, pl.ds(start, 256)], got[:, pl.ds(start, 256)]], 0)
                u = lax.dot_general(left, right, (((0,), (0,)), ((), ())), preferred_element_type=F32)
                u = u.reshape(4, 2, 2, 16, 256).astype(BF16)
                first = 64 * (4 * xh + yh)
                for xl in range(2):
                    for zl in range(2):
                        out[4 * xl + 2 * yl + zl, first : first + 64] = u[:, zl, xl].reshape(64, 256)


def outer_terms(core, tokens, got, cot, got_cot):
    vmem = pl.BlockSpec(memory_space=pltpu.VMEM)
    return pl.pallas_call(
        outer_kernel,
        in_specs=[pl.BlockSpec(memory_space=pltpu.SMEM)] + [vmem] * 4,
        out_specs=[vmem, vmem],
        out_shape=[
            jax.ShapeDtypeStruct((8, 1024, 256), BF16),
            jax.ShapeDtypeStruct((tokens.shape[0], 128), F32),
        ],
        compiler_params=pltpu.CompilerParams(vmem_limit_bytes=12 << 20),
        cost_estimate=pl.CostEstimate(flops=2 * tokens.size * 256, bytes_accessed=8 * tokens.size, transcendentals=0),
    )(core, tokens, got, cot, got_cot)


def split_kernel(both, u, weights):
    total = both[0, :512].astype(F32)
    for k in range(1, 8):
        total += both[k, :512].astype(F32)
    u[...] = total.astype(BF16)
    for k in range(8):
        weights[k] = both[k, 512:]


def split_sum(both):
    vmem = pl.BlockSpec(memory_space=pltpu.VMEM)
    return pl.pallas_call(
        split_kernel,
        in_specs=[vmem],
        out_specs=[vmem, vmem],
        out_shape=[jax.ShapeDtypeStruct((512, 256), BF16), jax.ShapeDtypeStruct((8, 512, 256), BF16)],
        compiler_params=pltpu.CompilerParams(vmem_limit_bytes=10 << 20),
        cost_estimate=pl.CostEstimate(flops=1 << 20, bytes_accessed=6 << 20, transcendentals=0),
    )(both)


def final_kernel(place, tokens, cot, inv, w_mine, w_theirs, kv_out, token_grad):
    rows, width = tokens.shape
    pieces = []
    for block in range(16):
        for ref, side in ((w_mine, place[0]), (w_theirs, 1 - place[0])):
            pieces.append((ref, 32 * block, pl.multiple_of(512 * block + 256 * side, 256)))
    total = jnp.zeros((rows, 256), F32)
    for ref, row, start in pieces:
        w = ref[:, row : row + 32].reshape(256, 256)
        total += jnp.dot(tokens[:, pl.ds(start, 256)], w, preferred_element_type=F32)
    root = inv[:, :1]
    kv = total * root
    kv_out[...] = kv.astype(BF16)
    g = cot[...]
    slopes = jnp.sum(g.astype(F32) * kv, -1, keepdims=True) * (1.0 / width)
    slopes = root * slopes
    for ref, row, start in pieces:
        w = ref[:, row : row + 32].reshape(256, 256)
        back = lax.dot_general(g, w, (((1,), (1,)), ((), ())), preferred_element_type=F32)
        x = tokens[:, pl.ds(start, 256)].astype(F32)
        token_grad[:, pl.ds(start, 256)] = (root * (back - x * slopes)).astype(BF16)


def final(place, tokens, cot, inv, w_mine, w_theirs):
    vmem = pl.BlockSpec(memory_space=pltpu.VMEM)
    return pl.pallas_call(
        final_kernel,
        in_specs=[pl.BlockSpec(memory_space=pltpu.SMEM)] + [vmem] * 5,
        out_specs=[vmem, vmem],
        out_shape=[
            jax.ShapeDtypeStruct(cot.shape, BF16),
            jax.ShapeDtypeStruct(tokens.shape, BF16),
        ],
        compiler_params=pltpu.CompilerParams(vmem_limit_bytes=14 << 20),
        cost_estimate=pl.CostEstimate(flops=4 * tokens.size * 256, bytes_accessed=8 << 20, transcendentals=0),
    )(place, tokens, cot, inv, w_mine, w_theirs)


def finish_kernel(parts, rows, gain, kv_grad, gain_grad):
    u = parts[0].astype(F32)
    for k in range(1, parts.shape[0]):
        u += parts[k].astype(F32)
    u = u * (1.0 / 256.0)
    size = u.shape[0]
    diagonal = lax.broadcasted_iota(jnp.int32, (size, size), 0) == lax.broadcasted_iota(jnp.int32, (size, size), 1)
    column = jnp.sum(jnp.where(diagonal, gain[...].astype(F32).reshape(1, size), 0.0), 1, keepdims=True)
    kv_grad[...] = (u * column).astype(BF16)
    sums = jnp.sum(u * rows[...].astype(F32), 1, keepdims=True)
    gain_grad[...] = jnp.sum(jnp.where(diagonal, sums, 0.0), 0).astype(BF16)


def finish(parts, rows, gain):
    vmem = pl.BlockSpec(memory_space=pltpu.VMEM)
    return pl.pallas_call(
        finish_kernel,
        in_specs=[vmem] * 3,
        out_specs=[vmem, vmem],
        out_shape=[jax.ShapeDtypeStruct(rows.shape, BF16), jax.ShapeDtypeStruct(gain.shape, BF16)],
        compiler_params=pltpu.CompilerParams(vmem_limit_bytes=2 << 20),
        cost_estimate=pl.CostEstimate(flops=1 << 20, bytes_accessed=1 << 18, transcendentals=0),
    )(parts, rows, gain)


SWAP = [(0, 1), (1, 0)]


def cubes():
    index = np.arange(math.prod(SIZES)).reshape(SIZES)
    groups = []
    for core in range(2):
        for x0, y0, z0 in itertools.product(range(core, 4, 2), range(core, 8, 2), range(core, 8, 2)):
            members = {}
            for a, b, c in itertools.product(range(2), repeat=3):
                x, y, z = (x0 + a) % 4, (y0 + b) % 8, (z0 + c) % 8
                members[x % 2, y % 2, z % 2] = int(index[x // 2, y // 2, y % 2, core, z // 2, z % 2, x % 2])
            groups.append([members[k] for k in sorted(members)])
    return groups


def body(tokens, cotangent, kv_weight, norm_gain):
    xl, zl = lax.axis_index("xl"), lax.axis_index("zl")
    place = jnp.stack([lax.axis_index("c"), xl, zl]).astype(jnp.int32)
    piece = 4 * lax.axis_index("zh") + 2 * zl + xl

    share = make_share(place, kv_weight, norm_gain)
    share = lax.all_to_all(share, ("xh", "yh", "yl"), 0, 0, tiled=True).reshape(512, 256)

    got, got_cotangent = lax.ppermute(tokens, "c", SWAP), lax.ppermute(cotangent, "c", SWAP)
    both, inv = outer_terms(place, tokens, got, cotangent, got_cotangent)

    both = lax.dynamic_update_slice(both, jnp.broadcast_to(share, (8, 512, 256)), (0, 512, 0))
    both = lax.all_to_all(both, AXES, 0, 0, tiled=True, axis_index_groups=cubes())
    u, w_mine = split_sum(both)
    w_theirs = lax.ppermute(w_mine, "c", SWAP)

    u = lax.all_to_all(u.reshape(32, 16, 256), ("xh", "yh", "zh"), 0, 0, tiled=True)
    kv_out, token_grad = final(place, tokens, cotangent, inv, w_mine, w_theirs)
    gain = lax.dynamic_slice_in_dim(norm_gain, 16 * piece, 16, 0)
    rows = lax.dynamic_slice_in_dim(kv_weight, 16 * piece, 16, 0)
    u, kv_out, gain, rows = lax.optimization_barrier((u, kv_out, gain, rows))
    kv_grad, gain_grad = finish(u, rows, gain)
    return (kv_out, token_grad, kv_grad, gain_grad)


def solution(mesh):
    split = Mesh(mesh.devices.reshape(SIZES), AXES)
    every, inner = P(AXES, None), ("xh", "yh", "yl", "c")
    return jax.shard_map(
        body,
        mesh=split,
        in_specs=(every, every, P(inner, None), P(inner)),
        out_specs=(every, every, every, P(AXES)),
        check_vma=False,
    )
```

time: 98.9 us -> 99.1 us (level)
  other arithmetic: 6.15 us -> 0.08 us
  local copies, waits for them, and re-layouts: 3.18 us -> 8.17 us
  waiting for transfers between devices: 14.1 us -> 9.92 us
  Pallas kernels: 9.41 us -> 12.3 us
  blocking collectives: 42.7 us -> 44.6 us
    unnamed x10 -> x16, local copies, waits for them, and re-layouts: 2.44 us -> 5.95 us
    all_to_all x1, waiting for transfers between devices: 4.08 us -> 0.58 us  [body(): lax.all_to_all(share, ('xh', 'yh', 'yl'), 0, 0, tiled=True)]
    pallas_call x2 -> x4, Pallas kernels: 3.4 us -> 6.31 us  [the longest x1 2.19 us: outer_terms(): pl.pallas_call(outer_kernel, in_specs=[pl.BlockSpec(memory_space=pltpu.SM...]
    slice x1 -> x0, other arithmetic: 2.37 us -> none  [body(): w_mine = both[:, 512:]]
    reduce_sum x2 -> x0, other arithmetic: 2.05 us -> none  [the longest x1 2 us: body(): gain_grad = jnp.sum(u * rows, -1).astype(BF16)]
    all_to_all x1, blocking collectives: 42.7 us -> 44.6 us  [body(): lax.all_to_all(both, AXES, 0, 0, tiled=True, axis_index_groups=cubes())]
    convert_element_type x2 -> x0, other arithmetic: 1.66 us -> none  [the longest x1 1 us: body(): (kv_weight.astype(F32) * norm_gain.astype(F32)[:, None]).astype(BF16)]
    dynamic_update_slice x0 -> x1, local copies, waits for them, and re-layouts: none -> 1.44 us  [body(): lax.dynamic_update_slice(both, jnp.broadcast_to(share, (8, 512, 256)), (0...]
  transfers between devices with their start and end apart: 5 -> 5, of which waited for: 3 -> 3; matrix products, arithmetic and copies ran while one was open for 3% -> 1% of each run, Pallas kernels for 7% -> 10%
where the time goes in v7:
time: 99.1 us; the launch traced here: 98.5 us
  blocking collectives  44.6 us (45%)
  starting transfers between devices  22.7 us (23%)
  Pallas kernels  12.3 us (12%)
  waiting for transfers between devices  9.92 us (10%)
  local copies, waits for them, and re-layouts  8.17 us (8%)
    all_to_all x1, blocking collectives, body(): lax.all_to_all(both, AXES, 0, 0, tiled=True, axis_index_groups=cubes())  44.6 us
    ppermute x1, starting transfers between devices, body(): lax.ppermute(tokens, 'c', SWAP)  8.79 us
    all_to_all x1, waiting for transfers between devices, body(): lax.all_to_all(u.reshape(32, 16, 256), ('xh', 'yh', 'zh'), 0, 0, tiled=True)  8.18 us
    pallas_call x1, Pallas kernels, final(): pl.pallas_call(final_kernel, in_specs=[pl.BlockSpec(memory_space=pltpu.SM...  6.03 us
    unnamed x16, local copies, waits for them, and re-layouts  5.95 us
    all_to_all x1, starting transfers between devices, body(): lax.all_to_all(u.reshape(32, 16, 256), ('xh', 'yh', 'zh'), 0, 0, tiled=True)  5.73 us
    all_to_all x1, starting transfers between devices, body(): lax.all_to_all(share, ('xh', 'yh', 'yl'), 0, 0, tiled=True)  4.03 us
    ppermute x1, starting transfers between devices, body(): lax.ppermute(cotangent, 'c', SWAP)  2.2 us
  transfers between devices with their start and end apart: 5, of which 3 were waited for; matrix products, arithmetic and copies ran while one was open for 1% of the time, Pallas kernels for 10%

profile of v7, /device:TPU:1, one launch (start us, length us, event | category | flops | bytes accessed | tf_op | source)
XLA Modules:
  0.0 98.5 jit_solution(10053907172836391842)
XLA Ops:
  0.6 8.8 %collective-permute-start = (bf16[128,8192]{1,0:T(8,128)(2,1)}, bf16[128,8192]{1,0:T(8,128)(2,1)S(1)}, u32[]{:S(2)}, u32[]{:S(2)}) collective-permute-start(bf16[128,8192]{1,0:T(8,128)(2,1)} %tokens.3), channel_id=1, source_target_pairs={{0,16},{16,0},{1,17},{17,1},{2,18},{18,2},{3,19},{19,3},{4,20},{20... | collective-permute-start | bytes 6291464 | tf_op jit(solution)/shard_map/ppermute | solution.py:201
  9.4 0.1 pad_add_fusion.core.place
  9.5 0.9 copy-done.5
  10.4 0.0 copy-start.6
  10.4 0.7 copy-done.6
  11.1 1.6 %shard_map.76 = bf16[16,32,256]{2,1,0:T(8,128)(2,1)} custom-call(s32[3]{0:T(128)S(1)} %pad_add_fusion.core.place, bf16[256,256]{1,0:T(8,128)(2,1)S(1)} %copy-done.5, bf16[256]{0:T(256)(128)(2,1)S(1)} %copy-done.6), custom_call_target="tpu_custom_call" | custom-call | flops 33554432 | bytes 524288 | tf_op jit(solution)/shard_map/pallas_call | solution.py:39
  12.7 4.0 %all-to-all-start = ((bf16[16,32,256]{2,1,0:T(8,128)(2,1)}), bf16[16,32,256]{2,1,0:T(8,128)(2,1)S(1)}, u32[]{:S(2)}, u32[]{:S(2)}) async-start(bf16[16,32,256]{2,1,0:T(8,128)(2,1)} %shard_map.76), calls=%async_computation | async-start | bytes 524288 | tf_op jit(solution)/shard_map/all_to_all | solution.py:199
  16.8 2.2 %collective-permute-start.1 = (bf16[128,256]{1,0:T(8,128)(2,1)}, bf16[128,256]{1,0:T(8,128)(2,1)S(1)}, u32[]{:S(2)}, u32[]{:S(2)}) collective-permute-start(bf16[128,256]{1,0:T(8,128)(2,1)} %cot.3), channel_id=1, source_target_pairs={{0,16},{16,0},{1,17},{17,1},{2,18},{18,2},{3,19},{19,3},{4,20},{20... | collective-permute-start | bytes 196616 | tf_op jit(solution)/shard_map/ppermute | solution.py:201
  19.0 1.2 %collective-permute-done.1.got_cot = bf16[128,256]{1,0:T(8,128)(2,1)S(1)} collective-permute-done((bf16[128,256]{1,0:T(8,128)(2,1)}, bf16[128,256]{1,0:T(8,128)(2,1)S(1)}, u32[]{:S(2)}, u32[]{:S(2)}) %collective-permute-start.1) | collective-permute-done | bytes 65568 | tf_op jit(solution)/shard_map/ppermute | solution.py:201
  20.1 0.0 collective-permute-done.got
  20.1 0.0 copy-start
  20.1 1.6 %copy-done = bf16[128,8192]{1,0:T(8,128)(2,1)S(1)} copy-done((bf16[128,8192]{1,0:T(8,128)(2,1)S(1)}, bf16[128,8192]{1,0:T(8,128)(2,1)}, u32[]{:S(2)}) %copy-start) | copy-done | bytes 2097176
  21.7 0.0 copy-start.3
  21.7 0.8 copy-done.3
  22.6 2.2 %shard_map.75 = (bf16[8,1024,256]{2,1,0:T(8,128)(2,1)S(1)}, f32[128,128]{1,0:T(8,128)S(1)}) custom-call(s32[3]{0:T(128)S(1)} %pad_add_fusion.core.place, bf16[128,8192]{1,0:T(8,128)(2,1)S(1)} %copy-done, bf16[128,8192]{1,0:T(8,128)(2,1)S(1)} %collective-permute-done.got, bf16[128,256]{1,0:T(8,128)(2,1)S(1)} %copy-done.3, ...), custom_call_target="tpu_custom_call" | custom-call | flops 536870912 | bytes 8388608 | tf_op jit(solution)/shard_map/pallas_call | solution.py:80
  24.8 0.0 copy-start.2
  24.8 1.9 %copy-done.2 = bf16[8,1024,256]{2,1,0:T(8,128)(2,1)} copy-done((bf16[8,1024,256]{2,1,0:T(8,128)(2,1)}, bf16[8,1024,256]{2,1,0:T(8,128)(2,1)S(1)}, u32[]{:S(2)}) %copy-start.2) | copy-done | bytes 4194328
  26.7 0.6 all-to-all-done
  27.3 1.4 %broadcast_dynamic-update-slice_fusion = bf16[8,1024,256]{2,1,0:T(8,128)(2,1)} fusion(bf16[8,1024,256]{2,1,0:T(8,128)(2,1)} %copy-done.2, bf16[512,256]{1,0:T(8,128)(2,1)S(1)} %bitcast.5), kind=kLoop, calls=%fused_computation | loop fusion | bytes 2359296 | tf_op jit(solution)/shard_map/dynamic_update_slice | solution.py:204
  28.7 44.6 %all_to_all.15.both = bf16[8,1024,256]{2,1,0:T(8,128)(2,1)S(1)} all-to-all(bf16[8,1024,256]{2,1,0:T(8,128)(2,1)} %broadcast_dynamic-update-slice_fusion), channel_id=1, replica_groups={{0,2,32,34,1,3,33,35},{4,6,36,38,5,7,37,39},{8,10,40,42,9,11,41,43},{12..., dimensions={0} | all-to-all | bytes 8388608 | tf_op jit(solution)/shard_map/all_to_all | solution.py:205
  73.4 1.8 %shard_map.77 = (bf16[512,256]{1,0:T(8,128)(2,1)}, bf16[8,512,256]{2,1,0:T(8,128)(2,1)}) custom-call(bf16[8,1024,256]{2,1,0:T(8,128)(2,1)S(1)} %all_to_all.15.both), custom_call_target="tpu_custom_call" | custom-call | flops 1048576 | bytes 6291456 | tf_op jit(solution)/shard_map/pallas_call | solution.py:104
  75.1 1.9 %collective-permute-start.2 = (bf16[8,512,256]{2,1,0:T(8,128)(2,1)}, bf16[8,512,256]{2,1,0:T(8,128)(2,1)}, u32[]{:S(2)}, u32[]{:S(2)}) collective-permute-start(bf16[8,512,256]{2,1,0:T(8,128)(2,1)} %get-tuple-element.19.w_mine), channel_id=1, source_target_pairs={{0,16},{16,0},{1,17},{17,1},{2,18},{18,2},{3,19},{19,3},{4,20},{20... | collective-permute-start | bytes 6291464 | tf_op jit(solution)/shard_map/ppermute | solution.py:207
  77.0 5.7 %all-to-all-start.2 = ((bf16[32,16,256]{2,1,0:T(8,128)(2,1)}), bf16[32,16,256]{2,1,0:T(8,128)(2,1)S(1)}, u32[]{:S(2)}, u32[]{:S(2)}) async-start(bf16[32,16,256]{2,1,0:T(8,128)(2,1)} %bitcast.4), calls=%async_computation.2 | async-start | bytes 524288 | tf_op jit(solution)/shard_map/all_to_all | solution.py:209
  82.8 0.0 copy-done.7
  82.8 0.1 dynamic_slice.6.gain
  82.9 0.7 constant_dynamic-slice_fusion.rows
  83.6 0.0 collective-permute-done.2.w_theirs
  83.6 0.0 copy-done.1
  83.6 0.0 copy-done.4
  83.6 6.0 %shard_map.78 = (bf16[128,256]{1,0:T(8,128)(2,1)}, bf16[128,8192]{1,0:T(8,128)(2,1)}) custom-call(s32[3]{0:T(128)S(1)} %pad_add_fusion.core.place, bf16[128,8192]{1,0:T(8,128)(2,1)S(1)} %copy-done.1, bf16[128,256]{1,0:T(8,128)(2,1)S(1)} %copy-done.4, f32[128,128]{1,0:T(8,128)S(1)} %get-tuple-element.18.inv, bf16[8,512,256]{2,1,0:T(8,128)(2,1)} %get-tuple-element.19.w_mine, ...), custom_call_target="tpu_custom_call" | custom-call | flops 1073741824 | bytes 8388608 | tf_op jit(solution)/shard_map/pallas_call | solution.py:139
  89.6 8.2 %all-to-all-done.2.parts = bf16[32,16,256]{2,1,0:T(8,128)(2,1)S(1)} async-done(((bf16[32,16,256]{2,1,0:T(8,128)(2,1)}), bf16[32,16,256]{2,1,0:T(8,128)(2,1)S(1)}, u32[]{:S(2)}, u32[]{:S(2)}) %all-to-all-start.2) | async-done | bytes 262176 | tf_op jit(solution)/shard_map/all_to_all | solution.py:209
  97.8 0.7 shard_map.79
  (4 shorter events, 0.0 us)
Async XLA Ops:
  0.6 19.5 %collective-permute-start = (bf16[128,8192]{1,0:T(8,128)(2,1)}, bf16[128,8192]{1,0:T(8,128)(2,1)S(1)}, u32[]{:S(2)}, u32[]{:S(2)}) collective-permute-start(bf16[128,8192]{1,0:T(8,128)(2,1)} %tokens.3), channel_id=1, source_target_pairs={{0,16},{16,0},{1,17},{17,1},{2,18},{18,2},{3,19},{19,3},{4,20},{20... | collective-permute-start | bytes 6291464 | tf_op jit(solution)/shard_map/ppermute | solution.py:201
  9.5 0.9 copy-start.5
  10.4 0.7 copy-start.6
  12.7 14.6 %all-to-all-start = ((bf16[16,32,256]{2,1,0:T(8,128)(2,1)}), bf16[16,32,256]{2,1,0:T(8,128)(2,1)S(1)}, u32[]{:S(2)}, u32[]{:S(2)}) async-start(bf16[16,32,256]{2,1,0:T(8,128)(2,1)} %shard_map.76), calls=%async_computation | async-start | bytes 524288 | tf_op jit(solution)/shard_map/all_to_all | solution.py:199
  16.8 3.4 %collective-permute-start.1 = (bf16[128,256]{1,0:T(8,128)(2,1)}, bf16[128,256]{1,0:T(8,128)(2,1)S(1)}, u32[]{:S(2)}, u32[]{:S(2)}) collective-permute-start(bf16[128,256]{1,0:T(8,128)(2,1)} %cot.3), channel_id=1, source_target_pairs={{0,16},{16,0},{1,17},{17,1},{2,18},{18,2},{3,19},{19,3},{4,20},{20... | collective-permute-start | bytes 196616 | tf_op jit(solution)/shard_map/ppermute | solution.py:201
  20.1 1.6 %copy-start = (bf16[128,8192]{1,0:T(8,128)(2,1)S(1)}, bf16[128,8192]{1,0:T(8,128)(2,1)}, u32[]{:S(2)}) copy-start(bf16[128,8192]{1,0:T(8,128)(2,1)} %tokens.3) | copy-start | bytes 6291460
  21.7 0.8 copy-start.3
  24.8 2.0 %copy-start.2 = (bf16[8,1024,256]{2,1,0:T(8,128)(2,1)}, bf16[8,1024,256]{2,1,0:T(8,128)(2,1)S(1)}, u32[]{:S(2)}) copy-start(bf16[8,1024,256]{2,1,0:T(8,128)(2,1)S(1)} %get-tuple-element.16) | copy-start | bytes 12582916
  73.4 9.4 %copy-start.7 = (bf16[256]{0:T(256)(128)(2,1)S(1)}, bf16[256]{0:T(256)(128)(2,1)}, u32[]{:S(2)}) copy-start(bf16[256]{0:T(256)(128)(2,1)} %gain.1) | copy-start | bytes 1540
  73.4 10.2 %copy-start.1 = (bf16[128,8192]{1,0:T(8,128)(2,1)S(1)}, bf16[128,8192]{1,0:T(8,128)(2,1)}, u32[]{:S(2)}) copy-start(bf16[128,8192]{1,0:T(8,128)(2,1)} %tokens.3) | copy-start | bytes 6291460
  73.4 10.2 %copy-start.4 = (bf16[128,256]{1,0:T(8,128)(2,1)S(1)}, bf16[128,256]{1,0:T(8,128)(2,1)}, u32[]{:S(2)}) copy-start(bf16[128,256]{1,0:T(8,128)(2,1)} %cot.3) | copy-start | bytes 196612
  75.1 8.5 %collective-permute-start.2 = (bf16[8,512,256]{2,1,0:T(8,128)(2,1)}, bf16[8,512,256]{2,1,0:T(8,128)(2,1)}, u32[]{:S(2)}, u32[]{:S(2)}) collective-permute-start(bf16[8,512,256]{2,1,0:T(8,128)(2,1)} %get-tuple-element.19.w_mine), channel_id=1, source_target_pairs={{0,16},{16,0},{1,17},{17,1},{2,18},{18,2},{3,19},{19,3},{4,20},{20... | collective-permute-start | bytes 6291464 | tf_op jit(solution)/shard_map/ppermute | solution.py:207
  77.0 20.8 %all-to-all-start.2 = ((bf16[32,16,256]{2,1,0:T(8,128)(2,1)}), bf16[32,16,256]{2,1,0:T(8,128)(2,1)S(1)}, u32[]{:S(2)}, u32[]{:S(2)}) async-start(bf16[32,16,256]{2,1,0:T(8,128)(2,1)} %bitcast.4), calls=%async_computation.2 | async-start | bytes 524288 | tf_op jit(solution)/shard_map/all_to_all | solution.py:209

commit v8 on v7

--- a/solution.py
+++ b/solution.py
@@ -52,62 +52,87 @@
     )(place, weight, gain)
 
 
-def roots(tokens):
-    wide = tokens[...].astype(F32)
-    return lax.rsqrt(jnp.mean(wide * wide, -1, keepdims=True) + 1e-05)
-
-
-def outer_kernel(core, tokens, got, cot, got_cot, out, inv):
-    mine, theirs = roots(tokens), roots(got)
+def outer_kernel(place, tokens, got, cot, got_cot, out, inv, held, stage, in_sems, out_sems):
+    width = held.shape[2]
+    chunk = width // 4
+    fetches = [
+        [
+            pltpu.make_async_copy(source.at[:, pl.ds(chunk * q, chunk)], held.at[k, :, pl.ds(chunk * q, chunk)], in_sems.at[k, q])
+            for k, source in enumerate((tokens, got))
+        ]
+        for q in range(4)
+    ]
+    for pair in fetches:
+        for fetch in pair:
+            fetch.start()
+    squares = [jnp.zeros((held.shape[1], 1), F32) for _ in range(2)]
+    for q, pair in enumerate(fetches):
+        for k, fetch in enumerate(pair):
+            fetch.wait()
+            wide = held[k, :, chunk * q : chunk * (q + 1)].astype(F32)
+            squares[k] += jnp.sum(wide * wide, -1, keepdims=True)
+    mine, theirs = (lax.rsqrt(total * (1.0 / width) + 1e-05) for total in squares)
     inv[...] = jnp.broadcast_to(mine, inv.shape)
     right = jnp.concatenate([cot[...].astype(F32) * mine, got_cot[...].astype(F32) * theirs], 0).astype(BF16)
-    for xh in range(2):
-        for yh in range(4):
-            for yl in range(2):
+    stores = []
+    for yl in range(2):
+        for xh in range(2):
+            for yh in range(4):
                 block = 8 * xh + 2 * yh + yl
-                start = pl.multiple_of(512 * block + 256 * core[0], 256)
-                left = jnp.concatenate([tokens[:, pl.ds(start, 256)], got[:, pl.ds(start, 256)]], 0)
+                start = pl.multiple_of(512 * block + 256 * place[0], 256)
+                left = jnp.concatenate([held[k, :, pl.ds(start, 256)] for k in range(2)], 0)
                 u = lax.dot_general(left, right, (((0,), (0,)), ((), ())), preferred_element_type=F32)
                 u = u.reshape(4, 2, 2, 16, 256).astype(BF16)
                 first = 64 * (4 * xh + yh)
                 for xl in range(2):
                     for zl in range(2):
-                        out[4 * xl + 2 * yl + zl, first : first + 64] = u[:, zl, xl].reshape(64, 256)
-
-
-def outer_terms(core, tokens, got, cot, got_cot):
-    vmem = pl.BlockSpec(memory_space=pltpu.VMEM)
+                        stage[4 * xl + 2 * yl + zl, first : first + 64] = u[:, zl, xl].reshape(64, 256)
+        for k in (2 * yl, 2 * yl + 1, 4 + 2 * yl, 5 + 2 * yl):
+            store = pltpu.make_async_copy(stage.at[k], out.at[k, pl.ds(0, 512)], out_sems.at[k])
+            store.start()
+            stores.append(store)
+    for store in stores:
+        store.wait()
+
+
+def outer_terms(place, tokens, got, cot, got_cot):
+    vmem, anywhere = pl.BlockSpec(memory_space=pltpu.VMEM), pl.BlockSpec(memory_space=pl.ANY)
+    rows, width = tokens.shape
     return pl.pallas_call(
         outer_kernel,
-        in_specs=[pl.BlockSpec(memory_space=pltpu.SMEM)] + [vmem] * 4,
-        out_specs=[vmem, vmem],
+        in_specs=[pl.BlockSpec(memory_space=pltpu.SMEM), anywhere, anywhere, vmem, vmem],
+        out_specs=[anywhere, vmem],
         out_shape=[
             jax.ShapeDtypeStruct((8, 1024, 256), BF16),
-            jax.ShapeDtypeStruct((tokens.shape[0], 128), F32),
-        ],
-        compiler_params=pltpu.CompilerParams(vmem_limit_bytes=12 << 20),
+            jax.ShapeDtypeStruct((rows, 128), F32),
+        ],
+        scratch_shapes=[
+            pltpu.VMEM((2, rows, width), BF16),
+            pltpu.VMEM((8, 512, 256), BF16),
+            pltpu.SemaphoreType.DMA((2, 4)),
+            pltpu.SemaphoreType.DMA((8,)),
+        ],
+        compiler_params=pltpu.CompilerParams(vmem_limit_bytes=62 << 20),
         cost_estimate=pl.CostEstimate(flops=2 * tokens.size * 256, bytes_accessed=8 * tokens.size, transcendentals=0),
-    )(core, tokens, got, cot, got_cot)
-
-
-def split_kernel(both, u, weights):
-    total = both[0, :512].astype(F32)
+    )(place, tokens, got, cot, got_cot)
+
+
+def sum_kernel(both, out):
+    total = both[0].astype(F32)
     for k in range(1, 8):
-        total += both[k, :512].astype(F32)
-    u[...] = total.astype(BF16)
-    for k in range(8):
-        weights[k] = both[k, 512:]
-
-
-def split_sum(both):
-    vmem = pl.BlockSpec(memory_space=pltpu.VMEM)
-    return pl.pallas_call(
-        split_kernel,
-        in_specs=[vmem],
-        out_specs=[vmem, vmem],
-        out_shape=[jax.ShapeDtypeStruct((512, 256), BF16), jax.ShapeDtypeStruct((8, 512, 256), BF16)],
-        compiler_params=pltpu.CompilerParams(vmem_limit_bytes=10 << 20),
-        cost_estimate=pl.CostEstimate(flops=1 << 20, bytes_accessed=6 << 20, transcendentals=0),
+        total += both[k].astype(F32)
+    out[...] = total.astype(BF16)
+
+
+def sum_of(both):
+    return pl.pallas_call(
+        sum_kernel,
+        grid=(1,),
+        in_specs=[pl.BlockSpec((8, 512, 256), lambda i: (0, 0, 0))],
+        out_specs=pl.BlockSpec((512, 256), lambda i: (0, 0)),
+        out_shape=jax.ShapeDtypeStruct((512, 256), BF16),
+        compiler_params=pltpu.CompilerParams(vmem_limit_bytes=8 << 20),
+        cost_estimate=pl.CostEstimate(flops=1 << 20, bytes_accessed=2 << 20, transcendentals=0),
     )(both)
 
 
@@ -119,7 +144,7 @@
             pieces.append((ref, 32 * block, pl.multiple_of(512 * block + 256 * side, 256)))
     total = jnp.zeros((rows, 256), F32)
     for ref, row, start in pieces:
-        w = ref[:, row : row + 32].reshape(256, 256)
+        w = ref[:, 512 + row : 544 + row].reshape(256, 256)
         total += jnp.dot(tokens[:, pl.ds(start, 256)], w, preferred_element_type=F32)
     root = inv[:, :1]
     kv = total * root
@@ -128,7 +153,7 @@
     slopes = jnp.sum(g.astype(F32) * kv, -1, keepdims=True) * (1.0 / width)
     slopes = root * slopes
     for ref, row, start in pieces:
-        w = ref[:, row : row + 32].reshape(256, 256)
+        w = ref[:, 512 + row : 544 + row].reshape(256, 256)
         back = lax.dot_general(g, w, (((1,), (1,)), ((), ())), preferred_element_type=F32)
         x = tokens[:, pl.ds(start, 256)].astype(F32)
         token_grad[:, pl.ds(start, 256)] = (root * (back - x * slopes)).astype(BF16)
@@ -203,11 +228,10 @@
 
     both = lax.dynamic_update_slice(both, jnp.broadcast_to(share, (8, 512, 256)), (0, 512, 0))
     both = lax.all_to_all(both, AXES, 0, 0, tiled=True, axis_index_groups=cubes())
-    u, w_mine = split_sum(both)
-    w_theirs = lax.ppermute(w_mine, "c", SWAP)
-
+    w_theirs = lax.ppermute(both, "c", SWAP)
+    u = sum_of(both)
     u = lax.all_to_all(u.reshape(32, 16, 256), ("xh", "yh", "zh"), 0, 0, tiled=True)
-    kv_out, token_grad = final(place, tokens, cotangent, inv, w_mine, w_theirs)
+    kv_out, token_grad = final(place, tokens, cotangent, inv, both, w_theirs)
     gain = lax.dynamic_slice_in_dim(norm_gain, 16 * piece, 16, 0)
     rows = lax.dynamic_slice_in_dim(kv_weight, 16 * piece, 16, 0)
     u, kv_out, gain, rows = lax.optimization_barrier((u, kv_out, gain, rows))

time: 99.1 us -> 101 us (1.019)
  Pallas kernels: 12.3 us -> 18.2 us
  local copies, waits for them, and re-layouts: 8.17 us -> 4.47 us
  waiting for transfers between devices: 9.92 us -> 8.58 us
    pallas_call x1, Pallas kernels: 2.19 us -> 6.03 us  [outer_terms(): pl.pallas_call(outer_kernel, in_specs=[pl.BlockSpec(memory_space=pltpu.SM...]
    unnamed x16 -> x18, local copies, waits for them, and re-layouts: 5.95 us -> 2.2 us
    all_to_all x1, waiting for transfers between devices: 8.18 us -> 6.92 us  [body(): lax.all_to_all(u.reshape(32, 16, 256), ('xh', 'yh', 'zh'), 0, 0, tiled=True)]
    pallas_call x1, Pallas kernels: 6.03 us -> 7.28 us  [final(): pl.pallas_call(final_kernel, in_specs=[pl.BlockSpec(memory_space=pltpu.SM...]
  transfers between devices with their start and end apart: 5 -> 5, of which waited for: 3 -> 3; matrix products, arithmetic and copies ran while one was open for 1% -> 1% of each run, Pallas kernels for 10% -> 17%
where the time goes in v8:
time: 101 us; the launch traced here: 100 us
  blocking collectives  44.8 us (44%)
  starting transfers between devices  23.6 us (23%)
  Pallas kernels  18.2 us (18%)
  waiting for transfers between devices  8.58 us (8%)
  local copies, waits for them, and re-layouts  4.47 us (4%)
    all_to_all x1, blocking collectives, body(): lax.all_to_all(both, AXES, 0, 0, tiled=True, axis_index_groups=cubes())  44.8 us
    ppermute x1, starting transfers between devices, body(): lax.ppermute(tokens, 'c', SWAP)  8.79 us
    pallas_call x1, Pallas kernels, final(): pl.pallas_call(final_kernel, in_specs=[pl.BlockSpec(memory_space=pltpu.SM...  7.28 us
    all_to_all x1, waiting for transfers between devices, body(): lax.all_to_all(u.reshape(32, 16, 256), ('xh', 'yh', 'zh'), 0, 0, tiled=True)  6.92 us
    all_to_all x1, starting transfers between devices, body(): lax.all_to_all(u.reshape(32, 16, 256), ('xh', 'yh', 'zh'), 0, 0, tiled=True)  6.49 us
    pallas_call x1, Pallas kernels, outer_terms(): pl.pallas_call(outer_kernel, in_specs=[pl.BlockSpec(memory_space=pltpu.SM...  6.03 us
    all_to_all x1, starting transfers between devices, body(): lax.all_to_all(share, ('xh', 'yh', 'yl'), 0, 0, tiled=True)  4.02 us
    pallas_call x1, Pallas kernels, sum_of(): pl.pallas_call(sum_kernel, grid=(1,), in_specs=[pl.BlockSpec((8, 512, 256...  2.58 us
  transfers between devices with their start and end apart: 5, of which 3 were waited for; matrix products, arithmetic and copies ran while one was open for 1% of the time, Pallas kernels for 17%

profile of v8, /device:TPU:1, one launch (start us, length us, event | category | flops | bytes accessed | tf_op | source)
XLA Modules:
  0.0 100.5 jit_solution(13455084001333635247)
XLA Ops:
  0.6 8.8 %collective-permute-start = (bf16[128,8192]{1,0:T(8,128)(2,1)}, bf16[128,8192]{1,0:T(8,128)(2,1)}, u32[]{:S(2)}, u32[]{:S(2)}) collective-permute-start(bf16[128,8192]{1,0:T(8,128)(2,1)} %tokens.3), channel_id=1, source_target_pairs={{0,16},{16,0},{1,17},{17,1},{2,18},{18,2},{3,19},{19,3},{4,20},{20... | collective-permute-start | bytes 6291464 | tf_op jit(solution)/shard_map/ppermute | solution.py:226
  9.4 0.1 pad_add_fusion.place
  9.5 0.0 copy-start.2
  9.5 0.9 copy-done.2
  10.4 0.0 copy-start.6
  10.4 0.7 copy-done.6
  11.1 1.6 %shard_map.76 = bf16[16,32,256]{2,1,0:T(8,128)(2,1)} custom-call(s32[3]{0:T(128)S(1)} %pad_add_fusion.place, bf16[256,256]{1,0:T(8,128)(2,1)S(1)} %copy-done.2, bf16[256]{0:T(256)(128)(2,1)S(1)} %copy-done.6), custom_call_target="tpu_custom_call" | custom-call | flops 33554432 | bytes 524288 | tf_op jit(solution)/shard_map/pallas_call | solution.py:39
  12.7 4.0 %all-to-all-start = ((bf16[16,32,256]{2,1,0:T(8,128)(2,1)}), bf16[16,32,256]{2,1,0:T(8,128)(2,1)S(1)}, u32[]{:S(2)}, u32[]{:S(2)}) async-start(bf16[16,32,256]{2,1,0:T(8,128)(2,1)} %shard_map.76), calls=%async_computation | async-start | bytes 524288 | tf_op jit(solution)/shard_map/all_to_all | solution.py:224
  16.8 2.2 %collective-permute-start.1 = (bf16[128,256]{1,0:T(8,128)(2,1)}, bf16[128,256]{1,0:T(8,128)(2,1)S(1)}, u32[]{:S(2)}, u32[]{:S(2)}) collective-permute-start(bf16[128,256]{1,0:T(8,128)(2,1)} %cot.3), channel_id=1, source_target_pairs={{0,16},{16,0},{1,17},{17,1},{2,18},{18,2},{3,19},{19,3},{4,20},{20... | collective-permute-start | bytes 196616 | tf_op jit(solution)/shard_map/ppermute | solution.py:226
  19.0 1.1 %collective-permute-done.1.got_cot = bf16[128,256]{1,0:T(8,128)(2,1)S(1)} collective-permute-done((bf16[128,256]{1,0:T(8,128)(2,1)}, bf16[128,256]{1,0:T(8,128)(2,1)S(1)}, u32[]{:S(2)}, u32[]{:S(2)}) %collective-permute-start.1) | collective-permute-done | bytes 65568 | tf_op jit(solution)/shard_map/ppermute | solution.py:226
  20.1 0.0 collective-permute-done.got
  20.1 0.0 copy-done.4
  20.1 0.6 copy-done.8
  20.7 6.0 %shard_map.75 = (bf16[8,1024,256]{2,1,0:T(8,128)(2,1)}, f32[128,128]{1,0:T(8,128)}) custom-call(s32[3]{0:T(128)} %copy-done.4, bf16[128,8192]{1,0:T(8,128)(2,1)} %tokens.3, bf16[128,8192]{1,0:T(8,128)(2,1)} %collective-permute-done.got, bf16[128,256]{1,0:T(8,128)(2,1)} %cot.3, bf16[128,256]{1,0:T(8,128)(2,1)} %copy-done.8), custom_call_target="tpu_custom_call" | custom-call | flops 536870912 | bytes 8388608 | tf_op jit(solution)/shard_map/pallas_call | solution.py:101
  26.8 0.5 all-to-all-done
  27.3 1.5 %broadcast_dynamic-update-slice_fusion = bf16[8,1024,256]{2,1,0:T(8,128)(2,1)} fusion(bf16[8,1024,256]{2,1,0:T(8,128)(2,1)} %get-tuple-element.14, bf16[512,256]{1,0:T(8,128)(2,1)S(1)} %bitcast.5), kind=kLoop, calls=%fused_computation | loop fusion | bytes 2359296 | tf_op jit(solution)/shard_map/dynamic_update_slice | solution.py:229
  28.8 44.8 %all_to_all.15.both.w_mine = bf16[8,1024,256]{2,1,0:T(8,128)(2,1)} all-to-all(bf16[8,1024,256]{2,1,0:T(8,128)(2,1)} %broadcast_dynamic-update-slice_fusion), channel_id=1, replica_groups={{0,2,32,34,1,3,33,35},{4,6,36,38,5,7,37,39},{8,10,40,42,9,11,41,43},{12..., dimensions={0} | all-to-all | bytes 8388608 | tf_op jit(solution)/shard_map/all_to_all | solution.py:230
  73.6 0.0 copy-start.5
  73.6 2.1 %collective-permute-start.2 = (bf16[8,1024,256]{2,1,0:T(8,128)(2,1)}, bf16[8,1024,256]{2,1,0:T(8,128)(2,1)}, u32[]{:S(2)}, u32[]{:S(2)}) collective-permute-start(bf16[8,1024,256]{2,1,0:T(8,128)(2,1)} %all_to_all.15.both.w_mine), channel_id=1, source_target_pairs={{0,16},{16,0},{1,17},{17,1},{2,18},{18,2},{3,19},{19,3},{4,20},{20... | collective-permute-start | bytes 12582920 | tf_op jit(solution)/shard_map/ppermute | solution.py:231
  75.7 2.6 %shard_map.77 = bf16[512,256]{1,0:T(8,128)(2,1)} custom-call(bf16[8,1024,256]{2,1,0:T(8,128)(2,1)} %all_to_all.15.both.w_mine), custom_call_target="tpu_custom_call" | custom-call | flops 1048576 | bytes 2097152 | tf_op jit(solution)/shard_map/pallas_call | solution.py:128
  78.3 6.5 %all-to-all-start.2 = ((bf16[32,16,256]{2,1,0:T(8,128)(2,1)}), bf16[32,16,256]{2,1,0:T(8,128)(2,1)S(1)}, u32[]{:S(2)}, u32[]{:S(2)}) async-start(bf16[32,16,256]{2,1,0:T(8,128)(2,1)} %bitcast.4), calls=%async_computation.2 | async-start | bytes 524288 | tf_op jit(solution)/shard_map/all_to_all | solution.py:233
  84.8 0.0 copy-done.7
  84.8 0.1 dynamic_slice.6.gain
  84.9 0.7 constant_dynamic-slice_fusion.rows
  85.6 0.0 collective-permute-done.2.w_theirs
  85.6 0.0 copy-done
  85.6 0.0 copy-done.1
  85.6 0.0 copy-done.3
  85.6 0.0 copy-done.5
  85.6 7.3 %shard_map.78 = (bf16[128,256]{1,0:T(8,128)(2,1)}, bf16[128,8192]{1,0:T(8,128)(2,1)}) custom-call(s32[3]{0:T(128)S(1)} %copy-done.5, bf16[128,8192]{1,0:T(8,128)(2,1)S(1)} %copy-done, bf16[128,256]{1,0:T(8,128)(2,1)S(1)} %copy-done.1, f32[128,128]{1,0:T(8,128)S(1)} %copy-done.3, bf16[8,1024,256]{2,1,0:T(8,128)(2,1)} %all_to_all.15.both.w_mine, ...), custom_call_target="tpu_custom_call" | custom-call | flops 1073741824 | bytes 8388608 | tf_op jit(solution)/shard_map/pallas_call | solution.py:164
  92.9 6.9 %all-to-all-done.2.parts = bf16[32,16,256]{2,1,0:T(8,128)(2,1)S(1)} async-done(((bf16[32,16,256]{2,1,0:T(8,128)(2,1)}), bf16[32,16,256]{2,1,0:T(8,128)(2,1)S(1)}, u32[]{:S(2)}, u32[]{:S(2)}) %all-to-all-start.2) | async-done | bytes 262176 | tf_op jit(solution)/shard_map/all_to_all | solution.py:233
  99.8 0.7 shard_map.79
  (6 shorter events, 0.0 us)
Async XLA Ops:
  0.6 19.5 %collective-permute-start = (bf16[128,8192]{1,0:T(8,128)(2,1)}, bf16[128,8192]{1,0:T(8,128)(2,1)}, u32[]{:S(2)}, u32[]{:S(2)}) collective-permute-start(bf16[128,8192]{1,0:T(8,128)(2,1)} %tokens.3), channel_id=1, source_target_pairs={{0,16},{16,0},{1,17},{17,1},{2,18},{18,2},{3,19},{19,3},{4,20},{20... | collective-permute-start | bytes 6291464 | tf_op jit(solution)/shard_map/ppermute | solution.py:226
  9.5 0.9 copy-start.2
  10.4 0.7 copy-start.6
  11.1 9.1 %copy-start.4 = (s32[3]{0:T(128)}, s32[3]{0:T(128)S(1)}, u32[]{:S(2)}) copy-start(s32[3]{0:T(128)S(1)} %pad_add_fusion.place) | copy-start | bytes 40
  12.7 14.6 %all-to-all-start = ((bf16[16,32,256]{2,1,0:T(8,128)(2,1)}), bf16[16,32,256]{2,1,0:T(8,128)(2,1)S(1)}, u32[]{:S(2)}, u32[]{:S(2)}) async-start(bf16[16,32,256]{2,1,0:T(8,128)(2,1)} %shard_map.76), calls=%async_computation | async-start | bytes 524288 | tf_op jit(solution)/shard_map/all_to_all | solution.py:224
  16.8 3.4 %collective-permute-start.1 = (bf16[128,256]{1,0:T(8,128)(2,1)}, bf16[128,256]{1,0:T(8,128)(2,1)S(1)}, u32[]{:S(2)}, u32[]{:S(2)}) collective-permute-start(bf16[128,256]{1,0:T(8,128)(2,1)} %cot.3), channel_id=1, source_target_pairs={{0,16},{16,0},{1,17},{17,1},{2,18},{18,2},{3,19},{19,3},{4,20},{20... | collective-permute-start | bytes 196616 | tf_op jit(solution)/shard_map/ppermute | solution.py:226
  20.1 0.6 copy-start.8
  73.6 11.2 %copy-start.7 = (bf16[256]{0:T(256)(128)(2,1)S(1)}, bf16[256]{0:T(256)(128)(2,1)}, u32[]{:S(2)}) copy-start(bf16[256]{0:T(256)(128)(2,1)} %gain.1) | copy-start | bytes 1540
  73.6 12.0 %copy-start = (bf16[128,8192]{1,0:T(8,128)(2,1)S(1)}, bf16[128,8192]{1,0:T(8,128)(2,1)}, u32[]{:S(2)}) copy-start(bf16[128,8192]{1,0:T(8,128)(2,1)} %tokens.3) | copy-start | bytes 6291460
  73.6 12.0 %copy-start.1 = (bf16[128,256]{1,0:T(8,128)(2,1)S(1)}, bf16[128,256]{1,0:T(8,128)(2,1)}, u32[]{:S(2)}) copy-start(bf16[128,256]{1,0:T(8,128)(2,1)} %cot.3) | copy-start | bytes 196612
  73.6 12.0 %copy-start.3 = (f32[128,128]{1,0:T(8,128)S(1)}, f32[128,128]{1,0:T(8,128)}, u32[]{:S(2)}) copy-start(f32[128,128]{1,0:T(8,128)} %get-tuple-element.15.inv) | copy-start | bytes 196612
  73.6 12.0 %copy-start.5 = (s32[3]{0:T(128)S(1)}, s32[3]{0:T(128)}, u32[]{:S(2)}) copy-start(s32[3]{0:T(128)} %copy-done.4) | copy-start | bytes 40
  73.6 11.9 %collective-permute-start.2 = (bf16[8,1024,256]{2,1,0:T(8,128)(2,1)}, bf16[8,1024,256]{2,1,0:T(8,128)(2,1)}, u32[]{:S(2)}, u32[]{:S(2)}) collective-permute-start(bf16[8,1024,256]{2,1,0:T(8,128)(2,1)} %all_to_all.15.both.w_mine), channel_id=1, source_target_pairs={{0,16},{16,0},{1,17},{17,1},{2,18},{18,2},{3,19},{19,3},{4,20},{20... | collective-permute-start | bytes 12582920 | tf_op jit(solution)/shard_map/ppermute | solution.py:231
  78.3 21.5 %all-to-all-start.2 = ((bf16[32,16,256]{2,1,0:T(8,128)(2,1)}), bf16[32,16,256]{2,1,0:T(8,128)(2,1)S(1)}, u32[]{:S(2)}, u32[]{:S(2)}) async-start(bf16[32,16,256]{2,1,0:T(8,128)(2,1)} %bitcast.4), calls=%async_computation.2 | async-start | bytes 524288 | tf_op jit(solution)/shard_map/all_to_all | solution.py:233

commit v9 on v4

--- a/solution.py
+++ b/solution.py
@@ -112,6 +112,52 @@
     )(core, tokens, cot, inv, w_mine, w_theirs)
 
 
+def split_kernel(both, u, weights):
+    total = both[0, :512].astype(F32)
+    for k in range(1, 8):
+        total += both[k, :512].astype(F32)
+    u[...] = total.astype(BF16)
+    for k in range(8):
+        weights[k] = both[k, 512:]
+
+
+def split_sum(both):
+    vmem = pl.BlockSpec(memory_space=pltpu.VMEM)
+    return pl.pallas_call(
+        split_kernel,
+        in_specs=[vmem],
+        out_specs=[vmem, vmem],
+        out_shape=[jax.ShapeDtypeStruct((512, 256), BF16), jax.ShapeDtypeStruct((8, 512, 256), BF16)],
+        compiler_params=pltpu.CompilerParams(vmem_limit_bytes=10 << 20),
+        cost_estimate=pl.CostEstimate(flops=1 << 20, bytes_accessed=6 << 20, transcendentals=0),
+    )(both)
+
+
+def finish_kernel(parts, rows, gain, kv_grad, gain_grad):
+    u = parts[0].astype(F32)
+    for k in range(1, parts.shape[0]):
+        u += parts[k].astype(F32)
+    u = u * (1.0 / 256.0)
+    size = u.shape[0]
+    diagonal = lax.broadcasted_iota(jnp.int32, (size, size), 0) == lax.broadcasted_iota(jnp.int32, (size, size), 1)
+    column = jnp.sum(jnp.where(diagonal, gain[...].astype(F32).reshape(1, size), 0.0), 1, keepdims=True)
+    kv_grad[...] = (u * column).astype(BF16)
+    sums = jnp.sum(u * rows[...].astype(F32), 1, keepdims=True)
+    gain_grad[...] = jnp.sum(jnp.where(diagonal, sums, 0.0), 0).astype(BF16)
+
+
+def finish(parts, rows, gain):
+    vmem = pl.BlockSpec(memory_space=pltpu.VMEM)
+    return pl.pallas_call(
+        finish_kernel,
+        in_specs=[vmem] * 3,
+        out_specs=[vmem, vmem],
+        out_shape=[jax.ShapeDtypeStruct(rows.shape, BF16), jax.ShapeDtypeStruct(gain.shape, BF16)],
+        compiler_params=pltpu.CompilerParams(vmem_limit_bytes=2 << 20),
+        cost_estimate=pl.CostEstimate(flops=1 << 20, bytes_accessed=1 << 18, transcendentals=0),
+    )(parts, rows, gain)
+
+
 SWAP = [(0, 1), (1, 0)]
 
 
@@ -129,7 +175,6 @@
 
 
 def body(tokens, cotangent, kv_weight, norm_gain):
-    factor = 1.0 / 256.0
     core = lax.axis_index("c").astype(jnp.int32).reshape(1)
     xl, zl = lax.axis_index("xl"), lax.axis_index("zl")
     piece = 4 * lax.axis_index("zh") + 2 * zl + xl
@@ -145,19 +190,15 @@
 
     both = merge(core, tokens, got, scaled, got_scaled, share)
     both = lax.all_to_all(both, AXES, 0, 0, tiled=True, axis_index_groups=cubes())
-    u = jnp.sum(both[:, :512], 0, dtype=F32).astype(BF16).reshape(32, 16, 256)
-    w_mine = both[:, 512:]
+    u, w_mine = split_sum(both)
     w_theirs = lax.ppermute(w_mine, "c", SWAP)
 
-    u = lax.all_to_all(u, ("xh", "yh", "zh"), 0, 0, tiled=True)
+    u = lax.all_to_all(u.reshape(32, 16, 256), ("xh", "yh", "zh"), 0, 0, tiled=True)
     kv_out, token_grad = final(core, tokens, cotangent, inv, w_mine, w_theirs)
-    u, kv_out = lax.optimization_barrier((u, kv_out))
-    u = jnp.sum(u, 0, dtype=F32) * factor
-    gain = lax.dynamic_slice_in_dim(norm_gain, 16 * piece, 16, 0).astype(F32)
-    kv_grad = (u * gain[:, None]).astype(BF16)
-    rows = lax.dynamic_slice_in_dim(kv_weight, 16 * piece, 16, 0).astype(F32)
-    gain_grad = jnp.sum(u * rows, -1).astype(BF16)
-
+    gain = lax.dynamic_slice_in_dim(norm_gain, 16 * piece, 16, 0)
+    rows = lax.dynamic_slice_in_dim(kv_weight, 16 * piece, 16, 0)
+    u, kv_out, gain, rows = lax.optimization_barrier((u, kv_out, gain, rows))
+    kv_grad, gain_grad = finish(u, rows, gain)
     return (kv_out, token_grad, kv_grad, gain_grad)
 
 

time: 98.9 us -> 96.9 us (0.980)
  other arithmetic: 6.15 us -> 1.66 us
  Pallas kernels: 9.41 us -> 11.9 us
    pallas_call x0 -> x2, Pallas kernels: none -> 2.48 us  [the longest x1 1.76 us: split_sum(): pl.pallas_call(split_kernel, in_specs=[vmem], out_specs=[vmem, vmem], out...]
    slice x1 -> x0, other arithmetic: 2.37 us -> none  [body(): w_mine = both[:, 512:]]
    reduce_sum x2 -> x0, other arithmetic: 2.05 us -> none  [the longest x1 2 us: body(): gain_grad = jnp.sum(u * rows, -1).astype(BF16)]
where the time goes in v9:
time: 96.9 us; the launch traced here: 96.4 us
  blocking collectives  42.7 us (44%)
  starting transfers between devices  22 us (23%)
  waiting for transfers between devices  13.4 us (14%)
  Pallas kernels  11.9 us (12%)
  local copies, waits for them, and re-layouts  3.96 us (4%)
  other arithmetic  1.66 us (2%)
    all_to_all x1, blocking collectives, body(): lax.all_to_all(both, AXES, 0, 0, tiled=True, axis_index_groups=cubes())  42.7 us
    ppermute x1, starting transfers between devices, body(): got = lax.ppermute(tokens, 'c', SWAP)  8.79 us
    all_to_all x1, waiting for transfers between devices, body(): lax.all_to_all(u.reshape(32, 16, 256), ('xh', 'yh', 'zh'), 0, 0, tiled=True)  8.4 us
    pallas_call x1, Pallas kernels, final(): pl.pallas_call(final_kernel, in_specs=[pl.BlockSpec(memory_space=pltpu.SM...  6.01 us
    all_to_all x1, starting transfers between devices, body(): lax.all_to_all(u.reshape(32, 16, 256), ('xh', 'yh', 'zh'), 0, 0, tiled=True)  5.09 us
    all_to_all x1, waiting for transfers between devices, body(): lax.all_to_all(share, ('xh', 'yh', 'yl'), 0, 0, tiled=True)  4.08 us
    all_to_all x1, starting transfers between devices, body(): lax.all_to_all(share, ('xh', 'yh', 'yl'), 0, 0, tiled=True)  4.01 us
    pallas_call x1, Pallas kernels, merge(): pl.pallas_call(merge_kernel, in_specs=[pl.BlockSpec(memory_space=pltpu.SM...  2.54 us
  transfers between devices with their start and end apart: 5, of which 3 were waited for; matrix products, arithmetic and copies ran while one was open for 3% of the time, Pallas kernels for 7%

profile of v9, /device:TPU:1, one launch (start us, length us, event | category | flops | bytes accessed | tf_op | source)
XLA Modules:
  0.0 96.4 jit_solution(14125214796501929270)
XLA Ops:
  0.6 8.8 %collective-permute-start = (bf16[128,8192]{1,0:T(8,128)(2,1)}, bf16[128,8192]{1,0:T(8,128)(2,1)}, u32[]{:S(2)}, u32[]{:S(2)}) collective-permute-start(bf16[128,8192]{1,0:T(8,128)(2,1)} %tokens.5), channel_id=1, source_target_pairs={{0,16},{16,0},{1,17},{17,1},{2,18},{18,2},{3,19},{19,3},{4,20},{20... | collective-permute-start | bytes 6291464 | tf_op jit(solution)/shard_map/ppermute | solution.py:182
  9.4 0.7 convert_element_type.10
  10.1 1.0 %multiply_convert_fusion = bf16[256,256]{1,0:T(8,128)(2,1)S(1)} fusion(bf16[256,256]{1,0:T(8,128)(2,1)} %param.6, f32[256]{0:T(256)S(1)} %convert_element_type.10), kind=kLoop, calls=%fused_computation | loop fusion | flops 196608 | bytes 263168 | tf_op jit(solution)/shard_map/convert_element_type | solution.py:186
  11.1 0.7 broadcast_in_dim.4
  11.9 4.0 %all-to-all-start = ((bf16[16,32,256]{2,1,0:T(8,128)(2,1)}), bf16[16,32,256]{2,1,0:T(8,128)(2,1)S(1)}, u32[]{:S(2)}, u32[]{:S(2)}) async-start(bf16[16,32,256]{2,1,0:T(8,128)(2,1)} %bitcast.3), calls=%async_computation | async-start | bytes 524288 | tf_op jit(solution)/shard_map/all_to_all | solution.py:189
  15.9 0.0 copy-start
  15.9 1.6 %copy-done = bf16[128,8192]{1,0:T(8,128)(2,1)S(1)} copy-done((bf16[128,8192]{1,0:T(8,128)(2,1)S(1)}, bf16[128,8192]{1,0:T(8,128)(2,1)}, u32[]{:S(2)}) %copy-start) | copy-done | bytes 2097176
  17.5 0.0 copy-start.2
  17.5 0.8 copy-done.2
  18.3 0.0 copy-start.1
  18.3 0.9 shard_map.75
  19.2 2.2 %collective-permute-start.1 = (bf16[128,256]{1,0:T(8,128)(2,1)S(1)}, bf16[128,256]{1,0:T(8,128)(2,1)S(1)}, u32[]{:S(2)}, u32[]{:S(2)}) collective-permute-start(bf16[128,256]{1,0:T(8,128)(2,1)S(1)} %get-tuple-element.16.mine), channel_id=1, source_target_pairs={{0,16},{16,0},{1,17},{17,1},{2,18},{18,2},{3,19},{19,3},{4,20},{20... | collective-permute-start | bytes 196616 | tf_op jit(solution)/shard_map/ppermute | solution.py:184
  21.4 0.9 collective-permute-done.1.theirs
  22.3 4.1 %all-to-all-done = bf16[16,32,256]{2,1,0:T(8,128)(2,1)S(1)} async-done(((bf16[16,32,256]{2,1,0:T(8,128)(2,1)}), bf16[16,32,256]{2,1,0:T(8,128)(2,1)S(1)}, u32[]{:S(2)}, u32[]{:S(2)}) %all-to-all-start) | async-done | bytes 262176 | tf_op jit(solution)/shard_map/all_to_all | solution.py:189
  26.4 0.0 collective-permute-done.got
  26.4 0.0 copy-done.1
  26.4 2.5 %shard_map.76 = bf16[8,1024,256]{2,1,0:T(8,128)(2,1)S(1)} custom-call(s32[1]{0:T(128)} %bitcast.core, bf16[128,8192]{1,0:T(8,128)(2,1)S(1)} %copy-done.1, bf16[128,8192]{1,0:T(8,128)(2,1)} %collective-permute-done.got, bf16[128,256]{1,0:T(8,128)(2,1)S(1)} %get-tuple-element.16.mine, bf16[128,256]{1,0:T(8,128)(2,1)S(1)} %collective-permute-done.1.theirs, ...), custom_call_target="tpu_custom_call" | custom-call | flops 536870912 | bytes 8388608 | tf_op jit(solution)/shard_map/pallas_call | solution.py:67
  29.0 42.7 %all_to_all.15.both = bf16[8,1024,256]{2,1,0:T(8,128)(2,1)S(1)} all-to-all(bf16[8,1024,256]{2,1,0:T(8,128)(2,1)S(1)} %shard_map.76), channel_id=1, replica_groups={{0,2,32,34,1,3,33,35},{4,6,36,38,5,7,37,39},{8,10,40,42,9,11,41,43},{12..., dimensions={0} | all-to-all | bytes 8388608 | tf_op jit(solution)/shard_map/all_to_all | solution.py:192
  71.6 0.0 copy-start.4
  71.7 0.0 copy-start.3
  71.7 1.8 %shard_map.77 = (bf16[512,256]{1,0:T(8,128)(2,1)}, bf16[8,512,256]{2,1,0:T(8,128)(2,1)}) custom-call(bf16[8,1024,256]{2,1,0:T(8,128)(2,1)S(1)} %all_to_all.15.both), custom_call_target="tpu_custom_call" | custom-call | flops 1048576 | bytes 6291456 | tf_op jit(solution)/shard_map/pallas_call | solution.py:126
  73.4 1.9 %collective-permute-start.2 = (bf16[8,512,256]{2,1,0:T(8,128)(2,1)}, bf16[8,512,256]{2,1,0:T(8,128)(2,1)}, u32[]{:S(2)}, u32[]{:S(2)}) collective-permute-start(bf16[8,512,256]{2,1,0:T(8,128)(2,1)} %get-tuple-element.19.w_mine), channel_id=1, source_target_pairs={{0,16},{16,0},{1,17},{17,1},{2,18},{18,2},{3,19},{19,3},{4,20},{20... | collective-permute-start | bytes 6291464 | tf_op jit(solution)/shard_map/ppermute | solution.py:194
  75.3 5.1 %all-to-all-start.2 = ((bf16[32,16,256]{2,1,0:T(8,128)(2,1)}), bf16[32,16,256]{2,1,0:T(8,128)(2,1)S(1)}, u32[]{:S(2)}, u32[]{:S(2)}) async-start(bf16[32,16,256]{2,1,0:T(8,128)(2,1)} %bitcast.5), calls=%async_computation.2 | async-start | bytes 524288 | tf_op jit(solution)/shard_map/all_to_all | solution.py:196
  80.4 0.0 copy-done.4
  80.4 0.1 dynamic_slice.10.gain
  80.5 0.7 constant_dynamic-slice_fusion.rows
  81.2 0.0 collective-permute-done.2.w_theirs
  81.2 0.0 copy-done.3
  81.2 6.0 %shard_map.78 = (bf16[128,256]{1,0:T(8,128)(2,1)}, bf16[128,8192]{1,0:T(8,128)(2,1)}) custom-call(s32[1]{0:T(128)} %bitcast.core, bf16[128,8192]{1,0:T(8,128)(2,1)S(1)} %copy-done.1, bf16[128,256]{1,0:T(8,128)(2,1)S(1)} %copy-done.3, f32[128,128]{1,0:T(8,128)S(1)} %get-tuple-element.18.inv, bf16[8,512,256]{2,1,0:T(8,128)(2,1)} %get-tuple-element.19.w_mine, ...), custom_call_target="tpu_custom_call" | custom-call | flops 1073741824 | bytes 8388608 | tf_op jit(solution)/shard_map/pallas_call | solution.py:102
  87.2 8.4 %all-to-all-done.2.parts = bf16[32,16,256]{2,1,0:T(8,128)(2,1)S(1)} async-done(((bf16[32,16,256]{2,1,0:T(8,128)(2,1)}), bf16[32,16,256]{2,1,0:T(8,128)(2,1)S(1)}, u32[]{:S(2)}, u32[]{:S(2)}) %all-to-all-start.2) | async-done | bytes 262176 | tf_op jit(solution)/shard_map/all_to_all | solution.py:196
  95.6 0.7 shard_map.79
  (1 shorter events, 0.0 us)
Async XLA Ops:
  0.6 25.8 %collective-permute-start = (bf16[128,8192]{1,0:T(8,128)(2,1)}, bf16[128,8192]{1,0:T(8,128)(2,1)}, u32[]{:S(2)}, u32[]{:S(2)}) collective-permute-start(bf16[128,8192]{1,0:T(8,128)(2,1)} %tokens.5), channel_id=1, source_target_pairs={{0,16},{16,0},{1,17},{17,1},{2,18},{18,2},{3,19},{19,3},{4,20},{20... | collective-permute-start | bytes 6291464 | tf_op jit(solution)/shard_map/ppermute | solution.py:182
  11.9 14.6 %all-to-all-start = ((bf16[16,32,256]{2,1,0:T(8,128)(2,1)}), bf16[16,32,256]{2,1,0:T(8,128)(2,1)S(1)}, u32[]{:S(2)}, u32[]{:S(2)}) async-start(bf16[16,32,256]{2,1,0:T(8,128)(2,1)} %bitcast.3), calls=%async_computation | async-start | bytes 524288 | tf_op jit(solution)/shard_map/all_to_all | solution.py:189
  15.9 1.6 %copy-start = (bf16[128,8192]{1,0:T(8,128)(2,1)S(1)}, bf16[128,8192]{1,0:T(8,128)(2,1)}, u32[]{:S(2)}) copy-start(bf16[128,8192]{1,0:T(8,128)(2,1)} %tokens.5) | copy-start | bytes 6291460
  17.5 0.8 copy-start.2
  18.3 8.1 %copy-start.1 = (bf16[128,8192]{1,0:T(8,128)(2,1)S(1)}, bf16[128,8192]{1,0:T(8,128)(2,1)}, u32[]{:S(2)}) copy-start(bf16[128,8192]{1,0:T(8,128)(2,1)} %tokens.5) | copy-start | bytes 6291460
  19.2 3.2 %collective-permute-start.1 = (bf16[128,256]{1,0:T(8,128)(2,1)S(1)}, bf16[128,256]{1,0:T(8,128)(2,1)S(1)}, u32[]{:S(2)}, u32[]{:S(2)}) collective-permute-start(bf16[128,256]{1,0:T(8,128)(2,1)S(1)} %get-tuple-element.16.mine), channel_id=1, source_target_pairs={{0,16},{16,0},{1,17},{17,1},{2,18},{18,2},{3,19},{19,3},{4,20},{20... | collective-permute-start | bytes 196616 | tf_op jit(solution)/shard_map/ppermute | solution.py:184
  71.6 8.8 %copy-start.4 = (bf16[256]{0:T(256)(128)(2,1)S(1)}, bf16[256]{0:T(256)(128)(2,1)}, u32[]{:S(2)}) copy-start(bf16[256]{0:T(256)(128)(2,1)} %param.7) | copy-start | bytes 1540
  71.7 9.6 %copy-start.3 = (bf16[128,256]{1,0:T(8,128)(2,1)S(1)}, bf16[128,256]{1,0:T(8,128)(2,1)}, u32[]{:S(2)}) copy-start(bf16[128,256]{1,0:T(8,128)(2,1)} %cot.3) | copy-start | bytes 196612
  73.4 7.8 %collective-permute-start.2 = (bf16[8,512,256]{2,1,0:T(8,128)(2,1)}, bf16[8,512,256]{2,1,0:T(8,128)(2,1)}, u32[]{:S(2)}, u32[]{:S(2)}) collective-permute-start(bf16[8,512,256]{2,1,0:T(8,128)(2,1)} %get-tuple-element.19.w_mine), channel_id=1, source_target_pairs={{0,16},{16,0},{1,17},{17,1},{2,18},{18,2},{3,19},{19,3},{4,20},{20... | collective-permute-start | bytes 6291464 | tf_op jit(solution)/shard_map/ppermute | solution.py:194
  75.3 20.3 %all-to-all-start.2 = ((bf16[32,16,256]{2,1,0:T(8,128)(2,1)}), bf16[32,16,256]{2,1,0:T(8,128)(2,1)S(1)}, u32[]{:S(2)}, u32[]{:S(2)}) async-start(bf16[32,16,256]{2,1,0:T(8,128)(2,1)} %bitcast.5), calls=%async_computation.2 | async-start | bytes 524288 | tf_op jit(solution)/shard_map/all_to_all | solution.py:196

commit v10 on v9

--- a/solution.py
+++ b/solution.py
@@ -112,13 +112,16 @@
     )(core, tokens, cot, inv, w_mine, w_theirs)
 
 
-def split_kernel(both, u, weights):
+def split_kernel(both, u, weights, sems):
+    copies = [pltpu.make_async_copy(both.at[k, pl.ds(512, 512)], weights.at[k], sems.at[k]) for k in range(8)]
+    for copy in copies:
+        copy.start()
     total = both[0, :512].astype(F32)
     for k in range(1, 8):
         total += both[k, :512].astype(F32)
     u[...] = total.astype(BF16)
-    for k in range(8):
-        weights[k] = both[k, 512:]
+    for copy in copies:
+        copy.wait()
 
 
 def split_sum(both):
@@ -126,8 +129,9 @@
     return pl.pallas_call(
         split_kernel,
         in_specs=[vmem],
-        out_specs=[vmem, vmem],
+        out_specs=[vmem, pl.BlockSpec(memory_space=pl.ANY)],
         out_shape=[jax.ShapeDtypeStruct((512, 256), BF16), jax.ShapeDtypeStruct((8, 512, 256), BF16)],
+        scratch_shapes=[pltpu.SemaphoreType.DMA((8,))],
         compiler_params=pltpu.CompilerParams(vmem_limit_bytes=10 << 20),
         cost_estimate=pl.CostEstimate(flops=1 << 20, bytes_accessed=6 << 20, transcendentals=0),
     )(both)
@@ -183,8 +187,8 @@
     scaled, inv = prep(tokens, cotangent)
     got_scaled = lax.ppermute(scaled, "c", SWAP)
 
-    scaled_weight = (kv_weight.astype(F32) * norm_gain.astype(F32)[:, None]).astype(BF16).reshape(2, 2, 2, 32, 256)
-    share = lax.dynamic_slice(scaled_weight, (xl, 0, zl, 0, 0), (1, 2, 1, 32, 256)).reshape(2, 32, 256)
+    scaled_weight = (kv_weight * norm_gain[:, None]).reshape(2, 2, 2, 32, 256)
+    share = lax.dynamic_slice(scaled_weight, (xl, 0, zl, 0, 0), (1, 2, 1, 32, 256)).reshape(1, 2, 32, 256)
     share = jnp.broadcast_to(share, (8, 2, 32, 256)).reshape(16, 32, 256)
     share = lax.all_to_all(share, ("xh", "yh", "yl"), 0, 0, tiled=True).reshape(512, 256)
 

time: 96.9 us -> 96.6 us (level)
    convert_element_type x2 -> x0, other arithmetic: 1.66 us -> none  [the longest x1 1 us: body(): (kv_weight.astype(F32) * norm_gain.astype(F32)[:, None]).astype(BF16)]
    mul x0 -> x1, other arithmetic: none -> 1 us  [body(): scaled_weight = (kv_weight * norm_gain[:, None]).reshape(2, 2, 2, 32, 256)]
where the time goes in v10:
time: 96.6 us; the launch traced here: 96.1 us
  blocking collectives  42.7 us (44%)
  starting transfers between devices  22 us (23%)
  waiting for transfers between devices  13.4 us (14%)
  Pallas kernels  12.2 us (13%)
  local copies, waits for them, and re-layouts  3.96 us (4%)
  other arithmetic  1 us (1%)
    all_to_all x1, blocking collectives, body(): lax.all_to_all(both, AXES, 0, 0, tiled=True, axis_index_groups=cubes())  42.7 us
    ppermute x1, starting transfers between devices, body(): got = lax.ppermute(tokens, 'c', SWAP)  8.79 us
    all_to_all x1, waiting for transfers between devices, body(): lax.all_to_all(u.reshape(32, 16, 256), ('xh', 'yh', 'zh'), 0, 0, tiled=True)  8.4 us
    pallas_call x1, Pallas kernels, final(): pl.pallas_call(final_kernel, in_specs=[pl.BlockSpec(memory_space=pltpu.SM...  6.02 us
    all_to_all x1, starting transfers between devices, body(): lax.all_to_all(u.reshape(32, 16, 256), ('xh', 'yh', 'zh'), 0, 0, tiled=True)  5.09 us
    all_to_all x1, waiting for transfers between devices, body(): lax.all_to_all(share, ('xh', 'yh', 'yl'), 0, 0, tiled=True)  4.08 us
    all_to_all x1, starting transfers between devices, body(): lax.all_to_all(share, ('xh', 'yh', 'yl'), 0, 0, tiled=True)  4.01 us
    pallas_call x1, Pallas kernels, merge(): pl.pallas_call(merge_kernel, in_specs=[pl.BlockSpec(memory_space=pltpu.SM...  2.54 us
  transfers between devices with their start and end apart: 5, of which 3 were waited for; matrix products, arithmetic and copies ran while one was open for 3% of the time, Pallas kernels for 7%

profile of v10, /device:TPU:1, one launch (start us, length us, event | category | flops | bytes accessed | tf_op | source)
XLA Modules:
  0.0 96.1 jit_solution(6701648600264063839)
XLA Ops:
  0.6 8.8 %collective-permute-start = (bf16[128,8192]{1,0:T(8,128)(2,1)}, bf16[128,8192]{1,0:T(8,128)(2,1)}, u32[]{:S(2)}, u32[]{:S(2)}) collective-permute-start(bf16[128,8192]{1,0:T(8,128)(2,1)} %tokens.5), channel_id=1, source_target_pairs={{0,16},{16,0},{1,17},{17,1},{2,18},{18,2},{3,19},{19,3},{4,20},{20... | collective-permute-start | bytes 6291464 | tf_op jit(solution)/shard_map/ppermute | solution.py:186
  9.4 1.0 %broadcast_multiply_fusion = bf16[256,256]{1,0:T(8,128)(2,1)S(1)} fusion(bf16[256,256]{1,0:T(8,128)(2,1)} %param.6, bf16[256]{0:T(256)(128)(2,1)} %param.7), kind=kLoop, calls=%fused_computation | loop fusion | flops 65536 | bytes 262656 | tf_op jit(solution)/shard_map/mul | solution.py:190
  10.5 0.7 broadcast_in_dim.9
  11.2 4.0 %all-to-all-start = ((bf16[16,32,256]{2,1,0:T(8,128)(2,1)}), bf16[16,32,256]{2,1,0:T(8,128)(2,1)S(1)}, u32[]{:S(2)}, u32[]{:S(2)}) async-start(bf16[16,32,256]{2,1,0:T(8,128)(2,1)} %bitcast.3), calls=%async_computation | async-start | bytes 524288 | tf_op jit(solution)/shard_map/all_to_all | solution.py:193
  15.2 0.0 copy-start
  15.2 1.6 %copy-done = bf16[128,8192]{1,0:T(8,128)(2,1)S(1)} copy-done((bf16[128,8192]{1,0:T(8,128)(2,1)S(1)}, bf16[128,8192]{1,0:T(8,128)(2,1)}, u32[]{:S(2)}) %copy-start) | copy-done | bytes 2097176
  16.8 0.0 copy-start.2
  16.8 0.8 copy-done.2
  17.7 0.0 copy-start.1
  17.7 0.9 shard_map.75
  18.5 2.2 %collective-permute-start.1 = (bf16[128,256]{1,0:T(8,128)(2,1)S(1)}, bf16[128,256]{1,0:T(8,128)(2,1)S(1)}, u32[]{:S(2)}, u32[]{:S(2)}) collective-permute-start(bf16[128,256]{1,0:T(8,128)(2,1)S(1)} %get-tuple-element.16.mine), channel_id=1, source_target_pairs={{0,16},{16,0},{1,17},{17,1},{2,18},{18,2},{3,19},{19,3},{4,20},{20... | collective-permute-start | bytes 196616 | tf_op jit(solution)/shard_map/ppermute | solution.py:188
  20.7 0.9 collective-permute-done.1.theirs
  21.7 4.1 %all-to-all-done = bf16[16,32,256]{2,1,0:T(8,128)(2,1)S(1)} async-done(((bf16[16,32,256]{2,1,0:T(8,128)(2,1)}), bf16[16,32,256]{2,1,0:T(8,128)(2,1)S(1)}, u32[]{:S(2)}, u32[]{:S(2)}) %all-to-all-start) | async-done | bytes 262176 | tf_op jit(solution)/shard_map/all_to_all | solution.py:193
  25.8 0.0 collective-permute-done.got
  25.8 0.0 copy-done.1
  25.8 2.5 %shard_map.76 = bf16[8,1024,256]{2,1,0:T(8,128)(2,1)S(1)} custom-call(s32[1]{0:T(128)} %bitcast.core, bf16[128,8192]{1,0:T(8,128)(2,1)S(1)} %copy-done.1, bf16[128,8192]{1,0:T(8,128)(2,1)} %collective-permute-done.got, bf16[128,256]{1,0:T(8,128)(2,1)S(1)} %get-tuple-element.16.mine, bf16[128,256]{1,0:T(8,128)(2,1)S(1)} %collective-permute-done.1.theirs, ...), custom_call_target="tpu_custom_call" | custom-call | flops 536870912 | bytes 8388608 | tf_op jit(solution)/shard_map/pallas_call | solution.py:67
  28.3 42.7 %all_to_all.15.both = bf16[8,1024,256]{2,1,0:T(8,128)(2,1)S(1)} all-to-all(bf16[8,1024,256]{2,1,0:T(8,128)(2,1)S(1)} %shard_map.76), channel_id=1, replica_groups={{0,2,32,34,1,3,33,35},{4,6,36,38,5,7,37,39},{8,10,40,42,9,11,41,43},{12..., dimensions={0} | all-to-all | bytes 8388608 | tf_op jit(solution)/shard_map/all_to_all | solution.py:196
  71.0 0.0 copy-start.4
  71.0 0.0 copy-start.3
  71.0 2.1 %shard_map.77 = (bf16[512,256]{1,0:T(8,128)(2,1)}, bf16[8,512,256]{2,1,0:T(8,128)(2,1)}) custom-call(bf16[8,1024,256]{2,1,0:T(8,128)(2,1)S(1)} %all_to_all.15.both), custom_call_target="tpu_custom_call" | custom-call | flops 1048576 | bytes 6291456 | tf_op jit(solution)/shard_map/pallas_call | solution.py:129
  73.1 1.9 %collective-permute-start.2 = (bf16[8,512,256]{2,1,0:T(8,128)(2,1)}, bf16[8,512,256]{2,1,0:T(8,128)(2,1)}, u32[]{:S(2)}, u32[]{:S(2)}) collective-permute-start(bf16[8,512,256]{2,1,0:T(8,128)(2,1)} %get-tuple-element.19.w_mine), channel_id=1, source_target_pairs={{0,16},{16,0},{1,17},{17,1},{2,18},{18,2},{3,19},{19,3},{4,20},{20... | collective-permute-start | bytes 6291464 | tf_op jit(solution)/shard_map/ppermute | solution.py:198
  75.0 5.1 %all-to-all-start.2 = ((bf16[32,16,256]{2,1,0:T(8,128)(2,1)}), bf16[32,16,256]{2,1,0:T(8,128)(2,1)S(1)}, u32[]{:S(2)}, u32[]{:S(2)}) async-start(bf16[32,16,256]{2,1,0:T(8,128)(2,1)} %bitcast.5), calls=%async_computation.2 | async-start | bytes 524288 | tf_op jit(solution)/shard_map/all_to_all | solution.py:200
  80.1 0.0 copy-done.4
  80.2 0.1 dynamic_slice.10.gain
  80.2 0.7 constant_dynamic-slice_fusion.rows
  80.9 0.0 collective-permute-done.2.w_theirs
  80.9 0.0 copy-done.3
  80.9 6.0 %shard_map.78 = (bf16[128,256]{1,0:T(8,128)(2,1)}, bf16[128,8192]{1,0:T(8,128)(2,1)}) custom-call(s32[1]{0:T(128)} %bitcast.core, bf16[128,8192]{1,0:T(8,128)(2,1)S(1)} %copy-done.1, bf16[128,256]{1,0:T(8,128)(2,1)S(1)} %copy-done.3, f32[128,128]{1,0:T(8,128)S(1)} %get-tuple-element.18.inv, bf16[8,512,256]{2,1,0:T(8,128)(2,1)} %get-tuple-element.19.w_mine, ...), custom_call_target="tpu_custom_call" | custom-call | flops 1073741824 | bytes 8388608 | tf_op jit(solution)/shard_map/pallas_call | solution.py:102
  87.0 8.4 %all-to-all-done.2.parts = bf16[32,16,256]{2,1,0:T(8,128)(2,1)S(1)} async-done(((bf16[32,16,256]{2,1,0:T(8,128)(2,1)}), bf16[32,16,256]{2,1,0:T(8,128)(2,1)S(1)}, u32[]{:S(2)}, u32[]{:S(2)}) %all-to-all-start.2) | async-done | bytes 262176 | tf_op jit(solution)/shard_map/all_to_all | solution.py:200
  95.4 0.7 shard_map.79
  (1 shorter events, 0.0 us)
Async XLA Ops:
  0.6 25.1 %collective-permute-start = (bf16[128,8192]{1,0:T(8,128)(2,1)}, bf16[128,8192]{1,0:T(8,128)(2,1)}, u32[]{:S(2)}, u32[]{:S(2)}) collective-permute-start(bf16[128,8192]{1,0:T(8,128)(2,1)} %tokens.5), channel_id=1, source_target_pairs={{0,16},{16,0},{1,17},{17,1},{2,18},{18,2},{3,19},{19,3},{4,20},{20... | collective-permute-start | bytes 6291464 | tf_op jit(solution)/shard_map/ppermute | solution.py:186
  11.2 14.6 %all-to-all-start = ((bf16[16,32,256]{2,1,0:T(8,128)(2,1)}), bf16[16,32,256]{2,1,0:T(8,128)(2,1)S(1)}, u32[]{:S(2)}, u32[]{:S(2)}) async-start(bf16[16,32,256]{2,1,0:T(8,128)(2,1)} %bitcast.3), calls=%async_computation | async-start | bytes 524288 | tf_op jit(solution)/shard_map/all_to_all | solution.py:193
  15.2 1.6 %copy-start = (bf16[128,8192]{1,0:T(8,128)(2,1)S(1)}, bf16[128,8192]{1,0:T(8,128)(2,1)}, u32[]{:S(2)}) copy-start(bf16[128,8192]{1,0:T(8,128)(2,1)} %tokens.5) | copy-start | bytes 6291460
  16.8 0.8 copy-start.2
  17.7 8.1 %copy-start.1 = (bf16[128,8192]{1,0:T(8,128)(2,1)S(1)}, bf16[128,8192]{1,0:T(8,128)(2,1)}, u32[]{:S(2)}) copy-start(bf16[128,8192]{1,0:T(8,128)(2,1)} %tokens.5) | copy-start | bytes 6291460
  18.5 3.2 %collective-permute-start.1 = (bf16[128,256]{1,0:T(8,128)(2,1)S(1)}, bf16[128,256]{1,0:T(8,128)(2,1)S(1)}, u32[]{:S(2)}, u32[]{:S(2)}) collective-permute-start(bf16[128,256]{1,0:T(8,128)(2,1)S(1)} %get-tuple-element.16.mine), channel_id=1, source_target_pairs={{0,16},{16,0},{1,17},{17,1},{2,18},{18,2},{3,19},{19,3},{4,20},{20... | collective-permute-start | bytes 196616 | tf_op jit(solution)/shard_map/ppermute | solution.py:188
  71.0 9.2 %copy-start.4 = (bf16[256]{0:T(256)(128)(2,1)S(1)}, bf16[256]{0:T(256)(128)(2,1)}, u32[]{:S(2)}) copy-start(bf16[256]{0:T(256)(128)(2,1)} %param.7) | copy-start | bytes 1540
  71.0 9.9 %copy-start.3 = (bf16[128,256]{1,0:T(8,128)(2,1)S(1)}, bf16[128,256]{1,0:T(8,128)(2,1)}, u32[]{:S(2)}) copy-start(bf16[128,256]{1,0:T(8,128)(2,1)} %cot.3) | copy-start | bytes 196612
  73.1 7.8 %collective-permute-start.2 = (bf16[8,512,256]{2,1,0:T(8,128)(2,1)}, bf16[8,512,256]{2,1,0:T(8,128)(2,1)}, u32[]{:S(2)}, u32[]{:S(2)}) collective-permute-start(bf16[8,512,256]{2,1,0:T(8,128)(2,1)} %get-tuple-element.19.w_mine), channel_id=1, source_target_pairs={{0,16},{16,0},{1,17},{17,1},{2,18},{18,2},{3,19},{19,3},{4,20},{20... | collective-permute-start | bytes 6291464 | tf_op jit(solution)/shard_map/ppermute | solution.py:198
  75.0 20.3 %all-to-all-start.2 = ((bf16[32,16,256]{2,1,0:T(8,128)(2,1)}), bf16[32,16,256]{2,1,0:T(8,128)(2,1)S(1)}, u32[]{:S(2)}, u32[]{:S(2)}) async-start(bf16[32,16,256]{2,1,0:T(8,128)(2,1)} %bitcast.5), calls=%async_computation.2 | async-start | bytes 524288 | tf_op jit(solution)/shard_map/all_to_all | solution.py:200

commit v11 on v9

--- a/solution.py
+++ b/solution.py
@@ -44,7 +44,22 @@
     )(tokens, cot)
 
 
-def merge_kernel(core, tokens, got, mine, theirs, weights, out):
+def arrived_kernel(weights, out):
+    out[...] = jnp.zeros_like(out)
+
+
+def arrived(weights):
+    return pl.pallas_call(
+        arrived_kernel,
+        in_specs=[pl.BlockSpec(memory_space=pl.ANY)],
+        out_specs=pl.BlockSpec(memory_space=pltpu.VMEM),
+        out_shape=jax.ShapeDtypeStruct((8, 128), F32),
+        compiler_params=pltpu.CompilerParams(vmem_limit_bytes=2 << 20),
+        cost_estimate=pl.CostEstimate(flops=50 * 10**9, bytes_accessed=1 << 10, transcendentals=0),
+    )(weights)
+
+
+def merge_kernel(core, tokens, got, mine, theirs, weights, mark, out):
     right = jnp.concatenate([mine[...], theirs[...]], 0)
     for xh in range(2):
         for yh in range(4):
@@ -62,16 +77,16 @@
         out[k, 512:] = weights[...]
 
 
-def merge(core, tokens, got, mine, theirs, weights):
+def merge(core, tokens, got, mine, theirs, weights, mark):
     vmem = pl.BlockSpec(memory_space=pltpu.VMEM)
     return pl.pallas_call(
         merge_kernel,
-        in_specs=[pl.BlockSpec(memory_space=pltpu.SMEM)] + [vmem] * 5,
+        in_specs=[pl.BlockSpec(memory_space=pltpu.SMEM)] + [vmem] * 6,
         out_specs=vmem,
         out_shape=jax.ShapeDtypeStruct((8, 1024, 256), BF16),
         compiler_params=pltpu.CompilerParams(vmem_limit_bytes=12 << 20),
         cost_estimate=pl.CostEstimate(flops=2 * tokens.size * 256, bytes_accessed=8 * tokens.size, transcendentals=0),
-    )(core, tokens, got, mine, theirs, weights)
+    )(core, tokens, got, mine, theirs, weights, mark)
 
 
 def final_kernel(core, tokens, cot, inv, w_mine, w_theirs, kv_out, token_grad):
@@ -183,12 +198,12 @@
     scaled, inv = prep(tokens, cotangent)
     got_scaled = lax.ppermute(scaled, "c", SWAP)
 
-    scaled_weight = (kv_weight.astype(F32) * norm_gain.astype(F32)[:, None]).astype(BF16).reshape(2, 2, 2, 32, 256)
-    share = lax.dynamic_slice(scaled_weight, (xl, 0, zl, 0, 0), (1, 2, 1, 32, 256)).reshape(2, 32, 256)
+    scaled_weight = (kv_weight * norm_gain[:, None]).reshape(2, 2, 2, 32, 256)
+    share = lax.dynamic_slice(scaled_weight, (xl, 0, zl, 0, 0), (1, 2, 1, 32, 256)).reshape(1, 2, 32, 256)
     share = jnp.broadcast_to(share, (8, 2, 32, 256)).reshape(16, 32, 256)
     share = lax.all_to_all(share, ("xh", "yh", "yl"), 0, 0, tiled=True).reshape(512, 256)
 
-    both = merge(core, tokens, got, scaled, got_scaled, share)
+    both = merge(core, tokens, got, scaled, got_scaled, share, arrived(share))
     both = lax.all_to_all(both, AXES, 0, 0, tiled=True, axis_index_groups=cubes())
     u, w_mine = split_sum(both)
     w_theirs = lax.ppermute(w_mine, "c", SWAP)

time: 96.9 us -> 95.5 us (0.986)
  waiting for transfers between devices: 13.4 us -> 10.7 us
  local copies, waits for them, and re-layouts: 3.96 us -> 5.53 us
    all_to_all x1, starting transfers between devices: 4.01 us -> 10.2 us  [body(): lax.all_to_all(share, ('xh', 'yh', 'yl'), 0, 0, tiled=True)]
    ppermute x1, starting transfers between devices: 8.79 us -> 2.87 us  [body(): got = lax.ppermute(tokens, 'c', SWAP)]
    all_to_all x1, waiting for transfers between devices: 4.08 us -> 2.12 us  [body(): lax.all_to_all(share, ('xh', 'yh', 'yl'), 0, 0, tiled=True)]
    convert_element_type x2 -> x0, other arithmetic: 1.66 us -> none  [the longest x1 1 us: body(): (kv_weight.astype(F32) * norm_gain.astype(F32)[:, None]).astype(BF16)]
    unnamed x10, local copies, waits for them, and re-layouts: 2.44 us -> 4.01 us
    mul x0 -> x1, other arithmetic: none -> 1 us  [body(): scaled_weight = (kv_weight * norm_gain[:, None]).reshape(2, 2, 2, 32, 256)]
  transfers between devices with their start and end apart: 5 -> 5, of which waited for: 3 -> 2; matrix products, arithmetic and copies ran while one was open for 3% -> 1% of each run, Pallas kernels for 7% -> 7%
where the time goes in v11:
time: 95.5 us; the launch traced here: 94.6 us
  blocking collectives  43 us (45%)
  starting transfers between devices  21.8 us (23%)
  Pallas kernels  11.9 us (12%)
  waiting for transfers between devices  10.7 us (11%)
  local copies, waits for them, and re-layouts  5.53 us (6%)
  other arithmetic  1 us (1%)
    all_to_all x1, blocking collectives, body(): lax.all_to_all(both, AXES, 0, 0, tiled=True, axis_index_groups=cubes())  43 us
    all_to_all x1, starting transfers between devices, body(): lax.all_to_all(share, ('xh', 'yh', 'yl'), 0, 0, tiled=True)  10.2 us
    all_to_all x1, waiting for transfers between devices, body(): lax.all_to_all(u.reshape(32, 16, 256), ('xh', 'yh', 'zh'), 0, 0, tiled=True)  8.54 us
    pallas_call x1, Pallas kernels, final(): pl.pallas_call(final_kernel, in_specs=[pl.BlockSpec(memory_space=pltpu.SM...  6.02 us
    all_to_all x1, starting transfers between devices, body(): lax.all_to_all(u.reshape(32, 16, 256), ('xh', 'yh', 'zh'), 0, 0, tiled=True)  4.92 us
    unnamed x10, local copies, waits for them, and re-layouts  4.01 us
    ppermute x1, starting transfers between devices, body(): got = lax.ppermute(tokens, 'c', SWAP)  2.87 us
    pallas_call x1, Pallas kernels, merge(): pl.pallas_call(merge_kernel, in_specs=[pl.BlockSpec(memory_space=pltpu.SM...  2.54 us
  transfers between devices with their start and end apart: 5, of which 2 were waited for; matrix products, arithmetic and copies ran while one was open for 1% of the time, Pallas kernels for 7%

profile of v11, /device:TPU:1, one launch (start us, length us, event | category | flops | bytes accessed | tf_op | source)
XLA Modules:
  0.0 94.6 jit_solution(12968417807308059613)
XLA Ops:
  0.6 1.0 %broadcast_multiply_fusion = bf16[256,256]{1,0:T(8,128)(2,1)S(1)} fusion(bf16[256,256]{1,0:T(8,128)(2,1)} %param.6, bf16[256]{0:T(256)(128)(2,1)} %param.7), kind=kLoop, calls=%fused_computation | loop fusion | flops 65536 | bytes 262656 | tf_op jit(solution)/shard_map/mul | solution.py:201
  1.7 0.7 broadcast_in_dim.9
  2.4 10.2 %all-to-all-start = ((bf16[16,32,256]{2,1,0:T(8,128)(2,1)}), bf16[16,32,256]{2,1,0:T(8,128)(2,1)S(1)}, u32[]{:S(2)}, u32[]{:S(2)}) async-start(bf16[16,32,256]{2,1,0:T(8,128)(2,1)} %bitcast.3), calls=%async_computation | async-start | bytes 524288 | tf_op jit(solution)/shard_map/all_to_all | solution.py:204
  12.6 2.9 %collective-permute-start = (bf16[128,8192]{1,0:T(8,128)(2,1)}, bf16[128,8192]{1,0:T(8,128)(2,1)}, u32[]{:S(2)}, u32[]{:S(2)}) collective-permute-start(bf16[128,8192]{1,0:T(8,128)(2,1)} %tokens.5), channel_id=1, source_target_pairs={{0,16},{16,0},{1,17},{17,1},{2,18},{18,2},{3,19},{19,3},{4,20},{20... | collective-permute-start | bytes 6291464 | tf_op jit(solution)/shard_map/ppermute | solution.py:197
  15.5 0.0 copy-start
  15.5 1.6 %copy-done = bf16[128,8192]{1,0:T(8,128)(2,1)S(1)} copy-done((bf16[128,8192]{1,0:T(8,128)(2,1)S(1)}, bf16[128,8192]{1,0:T(8,128)(2,1)}, u32[]{:S(2)}) %copy-start) | copy-done | bytes 2097176
  17.1 0.0 copy-start.2
  17.1 0.8 copy-done.2
  17.9 0.9 shard_map.75
  18.8 1.9 %collective-permute-start.1 = (bf16[128,256]{1,0:T(8,128)(2,1)S(1)}, bf16[128,256]{1,0:T(8,128)(2,1)S(1)}, u32[]{:S(2)}, u32[]{:S(2)}) collective-permute-start(bf16[128,256]{1,0:T(8,128)(2,1)S(1)} %get-tuple-element.16.mine), channel_id=1, source_target_pairs={{0,16},{16,0},{1,17},{17,1},{2,18},{18,2},{3,19},{19,3},{4,20},{20... | collective-permute-start | bytes 196616 | tf_op jit(solution)/shard_map/ppermute | solution.py:199
  20.7 2.1 %all-to-all-done = bf16[16,32,256]{2,1,0:T(8,128)(2,1)S(1)} async-done(((bf16[16,32,256]{2,1,0:T(8,128)(2,1)}), bf16[16,32,256]{2,1,0:T(8,128)(2,1)S(1)}, u32[]{:S(2)}, u32[]{:S(2)}) %all-to-all-start) | async-done | bytes 262176 | tf_op jit(solution)/shard_map/all_to_all | solution.py:204
  22.9 0.0 copy-start.1
  22.9 0.0 collective-permute-done.1.theirs
  22.9 0.0 collective-permute-done.got
  22.9 1.6 %copy-done.1 = bf16[128,8192]{1,0:T(8,128)(2,1)S(1)} copy-done((bf16[128,8192]{1,0:T(8,128)(2,1)S(1)}, bf16[128,8192]{1,0:T(8,128)(2,1)}, u32[]{:S(2)}) %copy-start.1) | copy-done | bytes 2097176
  24.4 2.5 %shard_map.77 = bf16[8,1024,256]{2,1,0:T(8,128)(2,1)S(1)} custom-call(s32[1]{0:T(128)} %bitcast.core, bf16[128,8192]{1,0:T(8,128)(2,1)S(1)} %copy-done.1, bf16[128,8192]{1,0:T(8,128)(2,1)} %collective-permute-done.got, bf16[128,256]{1,0:T(8,128)(2,1)S(1)} %get-tuple-element.16.mine, bf16[128,256]{1,0:T(8,128)(2,1)S(1)} %collective-permute-done.1.theirs, ...), custom_call_target="tpu_custom_call" | custom-call | flops 536870912 | bytes 8388608 | tf_op jit(solution)/shard_map/pallas_call | solution.py:82
  27.0 43.0 %all_to_all.15.both = bf16[8,1024,256]{2,1,0:T(8,128)(2,1)S(1)} all-to-all(bf16[8,1024,256]{2,1,0:T(8,128)(2,1)S(1)} %shard_map.77), channel_id=1, replica_groups={{0,2,32,34,1,3,33,35},{4,6,36,38,5,7,37,39},{8,10,40,42,9,11,41,43},{12..., dimensions={0} | all-to-all | bytes 8388608 | tf_op jit(solution)/shard_map/all_to_all | solution.py:207
  69.9 0.0 copy-start.4
  69.9 0.0 copy-start.3
  69.9 1.8 %shard_map.78 = (bf16[512,256]{1,0:T(8,128)(2,1)}, bf16[8,512,256]{2,1,0:T(8,128)(2,1)}) custom-call(bf16[8,1024,256]{2,1,0:T(8,128)(2,1)S(1)} %all_to_all.15.both), custom_call_target="tpu_custom_call" | custom-call | flops 1048576 | bytes 6291456 | tf_op jit(solution)/shard_map/pallas_call | solution.py:141
  71.7 1.9 %collective-permute-start.2 = (bf16[8,512,256]{2,1,0:T(8,128)(2,1)}, bf16[8,512,256]{2,1,0:T(8,128)(2,1)}, u32[]{:S(2)}, u32[]{:S(2)}) collective-permute-start(bf16[8,512,256]{2,1,0:T(8,128)(2,1)} %get-tuple-element.19.w_mine), channel_id=1, source_target_pairs={{0,16},{16,0},{1,17},{17,1},{2,18},{18,2},{3,19},{19,3},{4,20},{20... | collective-permute-start | bytes 6291464 | tf_op jit(solution)/shard_map/ppermute | solution.py:209
  73.6 4.9 %all-to-all-start.2 = ((bf16[32,16,256]{2,1,0:T(8,128)(2,1)}), bf16[32,16,256]{2,1,0:T(8,128)(2,1)S(1)}, u32[]{:S(2)}, u32[]{:S(2)}) async-start(bf16[32,16,256]{2,1,0:T(8,128)(2,1)} %bitcast.5), calls=%async_computation.2 | async-start | bytes 524288 | tf_op jit(solution)/shard_map/all_to_all | solution.py:211
  78.6 0.0 copy-done.4
  78.6 0.1 dynamic_slice.10.gain
  78.7 0.7 constant_dynamic-slice_fusion.rows
  79.4 0.0 collective-permute-done.2.w_theirs
  79.4 0.0 copy-done.3
  79.4 6.0 %shard_map.79 = (bf16[128,256]{1,0:T(8,128)(2,1)}, bf16[128,8192]{1,0:T(8,128)(2,1)}) custom-call(s32[1]{0:T(128)} %bitcast.core, bf16[128,8192]{1,0:T(8,128)(2,1)S(1)} %copy-done.1, bf16[128,256]{1,0:T(8,128)(2,1)S(1)} %copy-done.3, f32[128,128]{1,0:T(8,128)S(1)} %get-tuple-element.18.inv, bf16[8,512,256]{2,1,0:T(8,128)(2,1)} %get-tuple-element.19.w_mine, ...), custom_call_target="tpu_custom_call" | custom-call | flops 1073741824 | bytes 8388608 | tf_op jit(solution)/shard_map/pallas_call | solution.py:117
  85.4 8.5 %all-to-all-done.2.parts = bf16[32,16,256]{2,1,0:T(8,128)(2,1)S(1)} async-done(((bf16[32,16,256]{2,1,0:T(8,128)(2,1)}), bf16[32,16,256]{2,1,0:T(8,128)(2,1)S(1)}, u32[]{:S(2)}, u32[]{:S(2)}) %all-to-all-start.2) | async-done | bytes 262176 | tf_op jit(solution)/shard_map/all_to_all | solution.py:211
  93.9 0.7 shard_map.80
  (2 shorter events, 0.0 us)
Async XLA Ops:
  2.4 20.5 %all-to-all-start = ((bf16[16,32,256]{2,1,0:T(8,128)(2,1)}), bf16[16,32,256]{2,1,0:T(8,128)(2,1)S(1)}, u32[]{:S(2)}, u32[]{:S(2)}) async-start(bf16[16,32,256]{2,1,0:T(8,128)(2,1)} %bitcast.3), calls=%async_computation | async-start | bytes 524288 | tf_op jit(solution)/shard_map/all_to_all | solution.py:204
  12.6 10.2 %collective-permute-start = (bf16[128,8192]{1,0:T(8,128)(2,1)}, bf16[128,8192]{1,0:T(8,128)(2,1)}, u32[]{:S(2)}, u32[]{:S(2)}) collective-permute-start(bf16[128,8192]{1,0:T(8,128)(2,1)} %tokens.5), channel_id=1, source_target_pairs={{0,16},{16,0},{1,17},{17,1},{2,18},{18,2},{3,19},{19,3},{4,20},{20... | collective-permute-start | bytes 6291464 | tf_op jit(solution)/shard_map/ppermute | solution.py:197
  15.5 1.6 %copy-start = (bf16[128,8192]{1,0:T(8,128)(2,1)S(1)}, bf16[128,8192]{1,0:T(8,128)(2,1)}, u32[]{:S(2)}) copy-start(bf16[128,8192]{1,0:T(8,128)(2,1)} %tokens.5) | copy-start | bytes 6291460
  17.1 0.8 copy-start.2
  18.8 4.1 %collective-permute-start.1 = (bf16[128,256]{1,0:T(8,128)(2,1)S(1)}, bf16[128,256]{1,0:T(8,128)(2,1)S(1)}, u32[]{:S(2)}, u32[]{:S(2)}) collective-permute-start(bf16[128,256]{1,0:T(8,128)(2,1)S(1)} %get-tuple-element.16.mine), channel_id=1, source_target_pairs={{0,16},{16,0},{1,17},{17,1},{2,18},{18,2},{3,19},{19,3},{4,20},{20... | collective-permute-start | bytes 196616 | tf_op jit(solution)/shard_map/ppermute | solution.py:199
  22.9 1.6 %copy-start.1 = (bf16[128,8192]{1,0:T(8,128)(2,1)S(1)}, bf16[128,8192]{1,0:T(8,128)(2,1)}, u32[]{:S(2)}) copy-start(bf16[128,8192]{1,0:T(8,128)(2,1)} %tokens.5) | copy-start | bytes 6291460
  69.9 8.6 %copy-start.4 = (bf16[256]{0:T(256)(128)(2,1)S(1)}, bf16[256]{0:T(256)(128)(2,1)}, u32[]{:S(2)}) copy-start(bf16[256]{0:T(256)(128)(2,1)} %param.7) | copy-start | bytes 1540
  69.9 9.4 %copy-start.3 = (bf16[128,256]{1,0:T(8,128)(2,1)S(1)}, bf16[128,256]{1,0:T(8,128)(2,1)}, u32[]{:S(2)}) copy-start(bf16[128,256]{1,0:T(8,128)(2,1)} %cot.3) | copy-start | bytes 196612
  71.7 7.7 %collective-permute-start.2 = (bf16[8,512,256]{2,1,0:T(8,128)(2,1)}, bf16[8,512,256]{2,1,0:T(8,128)(2,1)}, u32[]{:S(2)}, u32[]{:S(2)}) collective-permute-start(bf16[8,512,256]{2,1,0:T(8,128)(2,1)} %get-tuple-element.19.w_mine), channel_id=1, source_target_pairs={{0,16},{16,0},{1,17},{17,1},{2,18},{18,2},{3,19},{19,3},{4,20},{20... | collective-permute-start | bytes 6291464 | tf_op jit(solution)/shard_map/ppermute | solution.py:209
  73.6 20.3 %all-to-all-start.2 = ((bf16[32,16,256]{2,1,0:T(8,128)(2,1)}), bf16[32,16,256]{2,1,0:T(8,128)(2,1)S(1)}, u32[]{:S(2)}, u32[]{:S(2)}) async-start(bf16[32,16,256]{2,1,0:T(8,128)(2,1)} %bitcast.5), calls=%async_computation.2 | async-start | bytes 524288 | tf_op jit(solution)/shard_map/all_to_all | solution.py:211

commit v12 on v11

--- a/solution.py
+++ b/solution.py
@@ -44,19 +44,19 @@
     )(tokens, cot)
 
 
-def arrived_kernel(weights, out):
+def arrived_kernel(weights, tokens, out):
     out[...] = jnp.zeros_like(out)
 
 
-def arrived(weights):
+def arrived(weights, tokens):
     return pl.pallas_call(
         arrived_kernel,
-        in_specs=[pl.BlockSpec(memory_space=pl.ANY)],
+        in_specs=[pl.BlockSpec(memory_space=pl.ANY)] * 2,
         out_specs=pl.BlockSpec(memory_space=pltpu.VMEM),
         out_shape=jax.ShapeDtypeStruct((8, 128), F32),
         compiler_params=pltpu.CompilerParams(vmem_limit_bytes=2 << 20),
         cost_estimate=pl.CostEstimate(flops=50 * 10**9, bytes_accessed=1 << 10, transcendentals=0),
-    )(weights)
+    )(weights, tokens)
 
 
 def merge_kernel(core, tokens, got, mine, theirs, weights, mark, out):
@@ -203,7 +203,7 @@
     share = jnp.broadcast_to(share, (8, 2, 32, 256)).reshape(16, 32, 256)
     share = lax.all_to_all(share, ("xh", "yh", "yl"), 0, 0, tiled=True).reshape(512, 256)
 
-    both = merge(core, tokens, got, scaled, got_scaled, share, arrived(share))
+    both = merge(core, tokens, got, scaled, got_scaled, share, arrived(share, tokens))
     both = lax.all_to_all(both, AXES, 0, 0, tiled=True, axis_index_groups=cubes())
     u, w_mine = split_sum(both)
     w_theirs = lax.ppermute(w_mine, "c", SWAP)

time: 95.5 us -> 95.1 us (level)
  local copies, waits for them, and re-layouts: 5.53 us -> 3.96 us
  blocking collectives: 43 us -> 44.1 us
    unnamed x10, local copies, waits for them, and re-layouts: 4.01 us -> 2.44 us
    all_to_all x1, blocking collectives: 43 us -> 44.1 us  [body(): lax.all_to_all(both, AXES, 0, 0, tiled=True, axis_index_groups=cubes())]
where the time goes in v12:
time: 95.1 us; the launch traced here: 94.5 us
  blocking collectives  44.1 us (46%)
  starting transfers between devices  21.7 us (23%)
  Pallas kernels  11.9 us (13%)
  waiting for transfers between devices  11 us (12%)
  local copies, waits for them, and re-layouts  3.96 us (4%)
  other arithmetic  1 us (1%)
    all_to_all x1, blocking collectives, body(): lax.all_to_all(both, AXES, 0, 0, tiled=True, axis_index_groups=cubes())  44.1 us
    all_to_all x1, starting transfers between devices, body(): lax.all_to_all(share, ('xh', 'yh', 'yl'), 0, 0, tiled=True)  10.2 us
    all_to_all x1, waiting for transfers between devices, body(): lax.all_to_all(u.reshape(32, 16, 256), ('xh', 'yh', 'zh'), 0, 0, tiled=True)  8.9 us
    pallas_call x1, Pallas kernels, final(): pl.pallas_call(final_kernel, in_specs=[pl.BlockSpec(memory_space=pltpu.SM...  6.02 us
    all_to_all x1, starting transfers between devices, body(): lax.all_to_all(u.reshape(32, 16, 256), ('xh', 'yh', 'zh'), 0, 0, tiled=True)  4.81 us
    ppermute x1, starting transfers between devices, body(): got = lax.ppermute(tokens, 'c', SWAP)  2.87 us
    pallas_call x1, Pallas kernels, merge(): pl.pallas_call(merge_kernel, in_specs=[pl.BlockSpec(memory_space=pltpu.SM...  2.54 us
    unnamed x10, local copies, waits for them, and re-layouts  2.44 us
  transfers between devices with their start and end apart: 5, of which 2 were waited for; matrix products, arithmetic and copies ran while one was open for 1% of the time, Pallas kernels for 7%

profile of v12, /device:TPU:1, one launch (start us, length us, event | category | flops | bytes accessed | tf_op | source)
XLA Modules:
  0.0 94.5 jit_solution(9317138519377243805)
XLA Ops:
  0.6 1.0 %broadcast_multiply_fusion = bf16[256,256]{1,0:T(8,128)(2,1)S(1)} fusion(bf16[256,256]{1,0:T(8,128)(2,1)} %param.6, bf16[256]{0:T(256)(128)(2,1)} %param.7), kind=kLoop, calls=%fused_computation | loop fusion | flops 65536 | bytes 262656 | tf_op jit(solution)/shard_map/mul | solution.py:201
  1.7 0.7 broadcast_in_dim.9
  2.4 10.2 %all-to-all-start = ((bf16[16,32,256]{2,1,0:T(8,128)(2,1)}), bf16[16,32,256]{2,1,0:T(8,128)(2,1)S(1)}, u32[]{:S(2)}, u32[]{:S(2)}) async-start(bf16[16,32,256]{2,1,0:T(8,128)(2,1)} %bitcast.3), calls=%async_computation | async-start | bytes 524288 | tf_op jit(solution)/shard_map/all_to_all | solution.py:204
  12.6 2.9 %collective-permute-start = (bf16[128,8192]{1,0:T(8,128)(2,1)}, bf16[128,8192]{1,0:T(8,128)(2,1)}, u32[]{:S(2)}, u32[]{:S(2)}) collective-permute-start(bf16[128,8192]{1,0:T(8,128)(2,1)} %tokens.7), channel_id=1, source_target_pairs={{0,16},{16,0},{1,17},{17,1},{2,18},{18,2},{3,19},{19,3},{4,20},{20... | collective-permute-start | bytes 6291464 | tf_op jit(solution)/shard_map/ppermute | solution.py:197
  15.5 0.0 copy-start
  15.5 1.6 %copy-done = bf16[128,8192]{1,0:T(8,128)(2,1)S(1)} copy-done((bf16[128,8192]{1,0:T(8,128)(2,1)S(1)}, bf16[128,8192]{1,0:T(8,128)(2,1)}, u32[]{:S(2)}) %copy-start) | copy-done | bytes 2097176
  17.1 0.0 copy-start.2
  17.1 0.8 copy-done.2
  17.9 0.0 copy-start.1
  17.9 0.9 shard_map.75
  18.8 1.9 %collective-permute-start.1 = (bf16[128,256]{1,0:T(8,128)(2,1)S(1)}, bf16[128,256]{1,0:T(8,128)(2,1)S(1)}, u32[]{:S(2)}, u32[]{:S(2)}) collective-permute-start(bf16[128,256]{1,0:T(8,128)(2,1)S(1)} %get-tuple-element.16.mine), channel_id=1, source_target_pairs={{0,16},{16,0},{1,17},{17,1},{2,18},{18,2},{3,19},{19,3},{4,20},{20... | collective-permute-start | bytes 196616 | tf_op jit(solution)/shard_map/ppermute | solution.py:199
  20.7 2.1 %all-to-all-done = bf16[16,32,256]{2,1,0:T(8,128)(2,1)S(1)} async-done(((bf16[16,32,256]{2,1,0:T(8,128)(2,1)}), bf16[16,32,256]{2,1,0:T(8,128)(2,1)S(1)}, u32[]{:S(2)}, u32[]{:S(2)}) %all-to-all-start) | async-done | bytes 262176 | tf_op jit(solution)/shard_map/all_to_all | solution.py:204
  22.9 0.0 copy-done.1
  22.9 0.0 collective-permute-done.1.theirs
  22.9 0.0 collective-permute-done.got
  22.9 2.5 %shard_map.77 = bf16[8,1024,256]{2,1,0:T(8,128)(2,1)S(1)} custom-call(s32[1]{0:T(128)} %bitcast.core, bf16[128,8192]{1,0:T(8,128)(2,1)S(1)} %copy-done.1, bf16[128,8192]{1,0:T(8,128)(2,1)} %collective-permute-done.got, bf16[128,256]{1,0:T(8,128)(2,1)S(1)} %get-tuple-element.16.mine, bf16[128,256]{1,0:T(8,128)(2,1)S(1)} %collective-permute-done.1.theirs, ...), custom_call_target="tpu_custom_call" | custom-call | flops 536870912 | bytes 8388608 | tf_op jit(solution)/shard_map/pallas_call | solution.py:82
  25.4 44.1 %all_to_all.15.both = bf16[8,1024,256]{2,1,0:T(8,128)(2,1)S(1)} all-to-all(bf16[8,1024,256]{2,1,0:T(8,128)(2,1)S(1)} %shard_map.77), channel_id=1, replica_groups={{0,2,32,34,1,3,33,35},{4,6,36,38,5,7,37,39},{8,10,40,42,9,11,41,43},{12..., dimensions={0} | all-to-all | bytes 8388608 | tf_op jit(solution)/shard_map/all_to_all | solution.py:207
  69.6 0.0 copy-start.4
  69.6 0.0 copy-start.3
  69.6 1.8 %shard_map.78 = (bf16[512,256]{1,0:T(8,128)(2,1)}, bf16[8,512,256]{2,1,0:T(8,128)(2,1)}) custom-call(bf16[8,1024,256]{2,1,0:T(8,128)(2,1)S(1)} %all_to_all.15.both), custom_call_target="tpu_custom_call" | custom-call | flops 1048576 | bytes 6291456 | tf_op jit(solution)/shard_map/pallas_call | solution.py:141
  71.3 1.9 %collective-permute-start.2 = (bf16[8,512,256]{2,1,0:T(8,128)(2,1)}, bf16[8,512,256]{2,1,0:T(8,128)(2,1)}, u32[]{:S(2)}, u32[]{:S(2)}) collective-permute-start(bf16[8,512,256]{2,1,0:T(8,128)(2,1)} %get-tuple-element.19.w_mine), channel_id=1, source_target_pairs={{0,16},{16,0},{1,17},{17,1},{2,18},{18,2},{3,19},{19,3},{4,20},{20... | collective-permute-start | bytes 6291464 | tf_op jit(solution)/shard_map/ppermute | solution.py:209
  73.2 4.8 %all-to-all-start.2 = ((bf16[32,16,256]{2,1,0:T(8,128)(2,1)}), bf16[32,16,256]{2,1,0:T(8,128)(2,1)S(1)}, u32[]{:S(2)}, u32[]{:S(2)}) async-start(bf16[32,16,256]{2,1,0:T(8,128)(2,1)} %bitcast.5), calls=%async_computation.2 | async-start | bytes 524288 | tf_op jit(solution)/shard_map/all_to_all | solution.py:211
  78.1 0.0 copy-done.4
  78.1 0.1 dynamic_slice.10.gain
  78.2 0.7 constant_dynamic-slice_fusion.rows
  78.9 0.0 collective-permute-done.2.w_theirs
  78.9 0.0 copy-done.3
  78.9 6.0 %shard_map.79 = (bf16[128,256]{1,0:T(8,128)(2,1)}, bf16[128,8192]{1,0:T(8,128)(2,1)}) custom-call(s32[1]{0:T(128)} %bitcast.core, bf16[128,8192]{1,0:T(8,128)(2,1)S(1)} %copy-done.1, bf16[128,256]{1,0:T(8,128)(2,1)S(1)} %copy-done.3, f32[128,128]{1,0:T(8,128)S(1)} %get-tuple-element.18.inv, bf16[8,512,256]{2,1,0:T(8,128)(2,1)} %get-tuple-element.19.w_mine, ...), custom_call_target="tpu_custom_call" | custom-call | flops 1073741824 | bytes 8388608 | tf_op jit(solution)/shard_map/pallas_call | solution.py:117
  84.9 8.9 %all-to-all-done.2.parts = bf16[32,16,256]{2,1,0:T(8,128)(2,1)S(1)} async-done(((bf16[32,16,256]{2,1,0:T(8,128)(2,1)}), bf16[32,16,256]{2,1,0:T(8,128)(2,1)S(1)}, u32[]{:S(2)}, u32[]{:S(2)}) %all-to-all-start.2) | async-done | bytes 262176 | tf_op jit(solution)/shard_map/all_to_all | solution.py:211
  93.8 0.7 shard_map.80
  (2 shorter events, 0.0 us)
Async XLA Ops:
  2.4 20.5 %all-to-all-start = ((bf16[16,32,256]{2,1,0:T(8,128)(2,1)}), bf16[16,32,256]{2,1,0:T(8,128)(2,1)S(1)}, u32[]{:S(2)}, u32[]{:S(2)}) async-start(bf16[16,32,256]{2,1,0:T(8,128)(2,1)} %bitcast.3), calls=%async_computation | async-start | bytes 524288 | tf_op jit(solution)/shard_map/all_to_all | solution.py:204
  12.6 10.2 %collective-permute-start = (bf16[128,8192]{1,0:T(8,128)(2,1)}, bf16[128,8192]{1,0:T(8,128)(2,1)}, u32[]{:S(2)}, u32[]{:S(2)}) collective-permute-start(bf16[128,8192]{1,0:T(8,128)(2,1)} %tokens.7), channel_id=1, source_target_pairs={{0,16},{16,0},{1,17},{17,1},{2,18},{18,2},{3,19},{19,3},{4,20},{20... | collective-permute-start | bytes 6291464 | tf_op jit(solution)/shard_map/ppermute | solution.py:197
  15.5 1.6 %copy-start = (bf16[128,8192]{1,0:T(8,128)(2,1)S(1)}, bf16[128,8192]{1,0:T(8,128)(2,1)}, u32[]{:S(2)}) copy-start(bf16[128,8192]{1,0:T(8,128)(2,1)} %tokens.7) | copy-start | bytes 6291460
  17.1 0.8 copy-start.2
  17.9 4.9 %copy-start.1 = (bf16[128,8192]{1,0:T(8,128)(2,1)S(1)}, bf16[128,8192]{1,0:T(8,128)(2,1)}, u32[]{:S(2)}) copy-start(bf16[128,8192]{1,0:T(8,128)(2,1)} %tokens.7) | copy-start | bytes 6291460
  18.8 4.1 %collective-permute-start.1 = (bf16[128,256]{1,0:T(8,128)(2,1)S(1)}, bf16[128,256]{1,0:T(8,128)(2,1)S(1)}, u32[]{:S(2)}, u32[]{:S(2)}) collective-permute-start(bf16[128,256]{1,0:T(8,128)(2,1)S(1)} %get-tuple-element.16.mine), channel_id=1, source_target_pairs={{0,16},{16,0},{1,17},{17,1},{2,18},{18,2},{3,19},{19,3},{4,20},{20... | collective-permute-start | bytes 196616 | tf_op jit(solution)/shard_map/ppermute | solution.py:199
  69.6 8.5 %copy-start.4 = (bf16[256]{0:T(256)(128)(2,1)S(1)}, bf16[256]{0:T(256)(128)(2,1)}, u32[]{:S(2)}) copy-start(bf16[256]{0:T(256)(128)(2,1)} %param.7) | copy-start | bytes 1540
  69.6 9.3 %copy-start.3 = (bf16[128,256]{1,0:T(8,128)(2,1)S(1)}, bf16[128,256]{1,0:T(8,128)(2,1)}, u32[]{:S(2)}) copy-start(bf16[128,256]{1,0:T(8,128)(2,1)} %cot.3) | copy-start | bytes 196612
  71.3 7.5 %collective-permute-start.2 = (bf16[8,512,256]{2,1,0:T(8,128)(2,1)}, bf16[8,512,256]{2,1,0:T(8,128)(2,1)}, u32[]{:S(2)}, u32[]{:S(2)}) collective-permute-start(bf16[8,512,256]{2,1,0:T(8,128)(2,1)} %get-tuple-element.19.w_mine), channel_id=1, source_target_pairs={{0,16},{16,0},{1,17},{17,1},{2,18},{18,2},{3,19},{19,3},{4,20},{20... | collective-permute-start | bytes 6291464 | tf_op jit(solution)/shard_map/ppermute | solution.py:209
  73.2 20.5 %all-to-all-start.2 = ((bf16[32,16,256]{2,1,0:T(8,128)(2,1)}), bf16[32,16,256]{2,1,0:T(8,128)(2,1)S(1)}, u32[]{:S(2)}, u32[]{:S(2)}) async-start(bf16[32,16,256]{2,1,0:T(8,128)(2,1)} %bitcast.5), calls=%async_computation.2 | async-start | bytes 524288 | tf_op jit(solution)/shard_map/all_to_all | solution.py:211
